TPU v7x, 32 devices: a whole 2x2x4 slice. The times are simulated.
32 devices in a mesh: seq: 16 (over z, y, core), mp: 2 (over x).
Axes of the slice: x: 2, y: 2, z: 4, core: 2. Of those that a mesh axis runs over, the one named last changes fastest.
Arguments:
- x_in: bfloat16 [10240, 2048], P('seq'), may hold values from -6 to 6
- lengths: int32 [5], replicated, may hold values from 100 to 9640, as said below
- g_attn: float32 [2048], P('seq'), may hold values from 0.5 to 1.5
- w_query: float32 [2048, 2048], P('seq', 'mp'), may hold values from -0.125 to 0.125
- w_key: float32 [2048, 2048], P('seq', 'mp'), may hold values from -0.125 to 0.125
- w_value: float32 [2048, 2048], P('seq', 'mp'), may hold values from -0.125 to 0.125
- w_out: float32 [2048, 2048], P('mp', 'seq'), may hold values from -0.5 to 0.5
- g_ffn: float32 [2048], P('seq'), may hold values from 0.5 to 1.5
- w_gate: float32 [2048, 5504], P('seq', 'mp'), may hold values from -0.125 to 0.125
- w_up: float32 [2048, 5504], P('seq', 'mp'), may hold values from -0.125 to 0.125
- w_down: float32 [5504, 2048], P('mp', 'seq'), may hold values from -0.078125 to 0.078125
- cotangent: bfloat16 [10240, 2048], P('seq'), may hold values from -6 to 6
Outputs:
- out_act: bfloat16 [10240, 2048], P('seq')
- grad_input: bfloat16 [10240, 2048], P('seq')
- grad_g_attn: float32 [2048], P('seq')
- grad_w_query: float32 [2048, 2048], P('seq', 'mp')
- grad_w_key: float32 [2048, 2048], P('seq', 'mp')
- grad_w_value: float32 [2048, 2048], P('seq', 'mp')
- grad_w_out: float32 [2048, 2048], P('mp', 'seq')
- grad_g_ffn: float32 [2048], P('seq')
- grad_w_gate: float32 [2048, 5504], P('seq', 'mp')
- grad_w_up: float32 [2048, 5504], P('seq', 'mp')
- grad_w_down: float32 [5504, 2048], P('mp', 'seq')
Inputs may be any that keep to these rules, and one draw needn't show every extreme that they name: 5 lengths in pack order summing to 10240; the entry at one place of 1 to 3, drawn from the seed, is the long sequence, of exactly 10240 - 4 // 2 * (300) tokens, which begins on the first index of seq and ends on the last; every other entry lies between 100 and 200, both taken in every draw, and these entries sum to 600.
All inputs are finite; a program needn't handle non-finite values.
Results may differ from a plain program's by a relative error of at most 0.015.
Values may be sent and summed in bfloat16 or wider, within the bound.
No kernel may reach another device: no remote copies, remote signals or barrier semaphores. Data moves between devices by JAX's collectives and lax.ppermute only.
A program may use at most 320 MiB of HBM per device.

v0:
```python
import math

import jax
import jax.numpy as jnp
from jax import lax
from jax.sharding import PartitionSpec as P

HEAD_DIM = 128
WINDOW = 64


EPSILON = 1e-06


def shifted(value, axis, steps):
    count = lax.axis_size(axis)
    initial, last = (max(0, -steps), min(count, count - steps))
    return lax.ppermute(value, axis, [(source, source + steps) for source in range(initial, last)])


def mat_nn(left, right):
    return jnp.dot(left, right, preferred_element_type=jnp.float32)


def mat_nt(left, right):
    return lax.dot_general(
        left, right, (((1,), (1,)), ((), ())), preferred_element_type=jnp.float32
    )


def mat_tn(left, right):
    return lax.dot_general(
        left, right, (((0,), (0,)), ((), ())), preferred_element_type=jnp.float32
    )


def attention_weights(g_attn, w_query, w_key, w_value, w_out):
    return (
        lax.all_gather(g_attn.astype(jnp.bfloat16), "seq", axis=0, tiled=True),
        lax.all_gather(w_query.astype(jnp.bfloat16), "seq", axis=0, tiled=True),
        lax.all_gather(w_key.astype(jnp.bfloat16), "seq", axis=0, tiled=True),
        lax.all_gather(w_value.astype(jnp.bfloat16), "seq", axis=0, tiled=True),
        lax.all_gather(w_out.astype(jnp.bfloat16), "seq", axis=1, tiled=True),
    )


def ffn_weights(g_ffn, w_gate, w_up, w_down):
    return (
        lax.all_gather(g_ffn.astype(jnp.bfloat16), "seq", axis=0, tiled=True),
        lax.all_gather(w_gate.astype(jnp.bfloat16), "seq", axis=0, tiled=True),
        lax.all_gather(w_up.astype(jnp.bfloat16), "seq", axis=0, tiled=True),
        lax.all_gather(w_down.astype(jnp.bfloat16), "seq", axis=1, tiled=True),
    )


def band_scores(query_heads, key_ext, allowed, score_scale):
    scores = (
        jnp.einsum("qhd,khd->hqk", query_heads, key_ext, preferred_element_type=jnp.float32)
        * score_scale
    )
    return jnp.where(allowed[None], scores, -1e30)


def norm_back(grad_normed, unit_rows, inverse_rows, gain):
    scaled = grad_normed * gain
    return inverse_rows * (scaled - unit_rows * jnp.mean(scaled * unit_rows, axis=1, keepdims=True))


def per_device(
    x_in, lengths, g_attn, w_query, w_key, w_value, w_out, g_ffn, w_gate, w_up, w_down, cotangent
):
    tokens = x_in.shape[0]
    heads_here = w_query.shape[1] // HEAD_DIM
    window = WINDOW
    score_scale = 1.0 / math.sqrt(HEAD_DIM)
    x_full = x_in.astype(jnp.float32)
    first_place = lax.axis_index("seq") * tokens
    places = first_place + jnp.arange(-window, tokens, dtype=jnp.int32)
    bounds = jnp.cumsum(lengths)[:-1]
    seg_all = jnp.sum((places[:, None] >= bounds[None, :]).astype(jnp.int32), axis=1)
    seg_all = jnp.where(places < 0, -1, seg_all)
    row_ids = jnp.arange(tokens, dtype=jnp.int32)[:, None]
    col_ids = jnp.arange(tokens + window, dtype=jnp.int32)[None, :]
    allowed = (
        (col_ids > row_ids)
        & (col_ids <= row_ids + window)
        & (seg_all[window:][:, None] == seg_all[None, :])
    )
    gain_attn, wq_full, wk_full, wv_full, wo_full = attention_weights(
        g_attn, w_query, w_key, w_value, w_out
    )
    inverse_one = lax.rsqrt(jnp.mean(x_full * x_full, axis=1, keepdims=True) + EPSILON)
    unit_one = x_full * inverse_one
    normed = (unit_one * gain_attn.astype(jnp.float32)).astype(jnp.bfloat16)
    queries = mat_nn(normed, wq_full).astype(jnp.bfloat16)
    key_rows = mat_nn(normed, wk_full).astype(jnp.bfloat16)
    value_rows = mat_nn(normed, wv_full).astype(jnp.bfloat16)
    key_tail, value_tail = shifted(
        (key_rows[tokens - window :], value_rows[tokens - window :]), "seq", 1
    )
    key_ext = jnp.concatenate([key_tail, key_rows], 0).reshape(
        tokens + window, heads_here, HEAD_DIM
    )
    value_ext = jnp.concatenate([value_tail, value_rows], 0).reshape(
        tokens + window, heads_here, HEAD_DIM
    )
    query_heads = queries.reshape(tokens, heads_here, HEAD_DIM)
    scores = band_scores(query_heads, key_ext, allowed, score_scale)
    top = jnp.max(scores, axis=-1, keepdims=True)
    log_total = top + jnp.log(jnp.sum(jnp.exp(scores - top), axis=-1, keepdims=True))
    probs = jnp.exp(scores - log_total)
    mixed = jnp.einsum(
        "hqk,khd->qhd", probs.astype(jnp.bfloat16), value_ext, preferred_element_type=jnp.float32
    )
    mixed = mixed.reshape(tokens, heads_here * HEAD_DIM).astype(jnp.bfloat16)
    branch = lax.psum(mat_nn(mixed, wo_full), "mp")
    middle = x_full + branch
    gain_ffn, wg_full, wu_full, wd_full = ffn_weights(g_ffn, w_gate, w_up, w_down)
    inverse_two = lax.rsqrt(jnp.mean(middle * middle, axis=1, keepdims=True) + EPSILON)
    unit_two = middle * inverse_two
    normed_two = (unit_two * gain_ffn.astype(jnp.float32)).astype(jnp.bfloat16)
    gate_pre = mat_nn(normed_two, wg_full)
    up_pre = mat_nn(normed_two, wu_full)
    sigma = jax.nn.sigmoid(gate_pre)
    silu_val = gate_pre * sigma
    hidden = (silu_val * up_pre).astype(jnp.bfloat16)
    ffn_out = lax.psum(mat_nn(hidden, wd_full).astype(jnp.bfloat16), "mp").astype(jnp.float32)
    result = middle + ffn_out
    gain_ffn, wg_full, wu_full, wd_full = ffn_weights(g_ffn, w_gate, w_up, w_down)
    grad_out = cotangent.astype(jnp.float32)
    grad_down = mat_tn(hidden, cotangent)
    grad_hidden = mat_nt(cotangent, wd_full)
    grad_gate = (grad_hidden * up_pre * sigma * (1.0 + gate_pre * (1.0 - sigma))).astype(
        jnp.bfloat16
    )
    grad_upper = (grad_hidden * silu_val).astype(jnp.bfloat16)
    grad_wgate = mat_tn(normed_two, grad_gate)
    grad_wupper = mat_tn(normed_two, grad_upper)
    grad_normed_two = lax.psum(mat_nt(grad_gate, wg_full) + mat_nt(grad_upper, wu_full), "mp")
    grad_gain_two = jnp.sum(grad_normed_two * unit_two, axis=0)
    grad_middle = grad_out + norm_back(
        grad_normed_two, unit_two, inverse_two, gain_ffn.astype(jnp.float32)
    )
    gain_attn, wq_full, wk_full, wv_full, wo_full = attention_weights(
        g_attn, w_query, w_key, w_value, w_out
    )
    grad_branch = grad_middle.astype(jnp.bfloat16)
    grad_wout = mat_tn(mixed, grad_branch)
    grad_mixed = (
        mat_nt(grad_branch, wo_full).astype(jnp.bfloat16).reshape(tokens, heads_here, HEAD_DIM)
    )
    scores = band_scores(query_heads, key_ext, allowed, score_scale)
    probs = jnp.exp(scores - log_total)
    grad_value_ext = jnp.einsum(
        "hqk,qhd->khd", probs.astype(jnp.bfloat16), grad_mixed, preferred_element_type=jnp.float32
    )
    grad_probs = jnp.einsum(
        "qhd,khd->hqk", grad_mixed, value_ext, preferred_element_type=jnp.float32
    )
    inner = jnp.sum(probs * grad_probs, axis=-1, keepdims=True)
    grad_scores = (probs * (grad_probs - inner)).astype(jnp.bfloat16)
    grad_query = (
        jnp.einsum("hqk,khd->qhd", grad_scores, key_ext, preferred_element_type=jnp.float32)
        * score_scale
    )
    grad_key_ext = (
        jnp.einsum("hqk,qhd->khd", grad_scores, query_heads, preferred_element_type=jnp.float32)
        * score_scale
    )
    back_key, back_value = (
        shifted(grad_key_ext[:window].astype(jnp.bfloat16), "seq", -1).astype(jnp.float32),
        shifted(grad_value_ext[:window].astype(jnp.bfloat16), "seq", -1).astype(jnp.float32),
    )
    grad_key = grad_key_ext[window:].at[tokens - window :].add(back_key)
    grad_value = grad_value_ext[window:].at[tokens - window :].add(back_value)
    grad_query = grad_query.reshape(tokens, heads_here * HEAD_DIM).astype(jnp.bfloat16)
    grad_key = grad_key.reshape(tokens, heads_here * HEAD_DIM).astype(jnp.bfloat16)
    grad_value = grad_value.reshape(tokens, heads_here * HEAD_DIM).astype(jnp.bfloat16)
    grad_wquery = mat_tn(normed, grad_query)
    grad_wkey = mat_tn(normed, grad_key)
    grad_wvalue = mat_tn(normed, grad_value)
    grad_normed = lax.psum(
        (
            mat_nt(grad_query, wq_full) + mat_nt(grad_key, wk_full) + mat_nt(grad_value, wv_full)
        ).astype(jnp.bfloat16),
        "mp",
    ).astype(jnp.float32)
    grad_gain_one = jnp.sum(grad_normed * unit_one, axis=0)
    grad_input = grad_middle + norm_back(
        grad_normed, unit_one, inverse_one, gain_attn.astype(jnp.float32)
    )
    every_sum = (
        lax.psum_scatter(grad_gain_one, "seq", scatter_dimension=0, tiled=True),
        lax.psum_scatter(grad_wquery, "seq", scatter_dimension=0, tiled=True),
        lax.psum_scatter(grad_wkey, "seq", scatter_dimension=0, tiled=True),
        lax.psum_scatter(grad_wvalue, "seq", scatter_dimension=0, tiled=True),
        lax.psum_scatter(grad_wout, "seq", scatter_dimension=1, tiled=True),
        lax.psum_scatter(grad_gain_two, "seq", scatter_dimension=0, tiled=True),
        lax.psum_scatter(grad_wgate, "seq", scatter_dimension=0, tiled=True),
        lax.psum_scatter(grad_wupper, "seq", scatter_dimension=0, tiled=True),
        lax.psum_scatter(grad_down, "seq", scatter_dimension=1, tiled=True),
    )
    attn_sums = every_sum[:5]
    ffn_sums = every_sum[5:]
    return (
        result.astype(jnp.bfloat16),
        grad_input.astype(jnp.bfloat16),
        attn_sums[0],
        attn_sums[1],
        attn_sums[2],
        attn_sums[3],
        attn_sums[4],
        ffn_sums[0],
        ffn_sums[1],
        ffn_sums[2],
        ffn_sums[3],
    )


def solution(mesh):
    placed = (
        P("seq", None),
        P(),
        P("seq"),
        P("seq", "mp"),
        P("seq", "mp"),
        P("seq", "mp"),
        P("mp", "seq"),
        P("seq"),
        P("seq", "mp"),
        P("seq", "mp"),
        P("mp", "seq"),
        P("seq", None),
    )
    return jax.shard_map(
        per_device,
        mesh=mesh,
        in_specs=placed,
        out_specs=(
            P("seq", None),
            P("seq", None),
            P("seq"),
            P("seq", "mp"),
            P("seq", "mp"),
            P("seq", "mp"),
            P("mp", "seq"),
            P("seq"),
            P("seq", "mp"),
            P("seq", "mp"),
            P("mp", "seq"),
        ),
        check_vma=False,
    )
```

profile of v0, /device:TPU:0, one launch (start us, length us, event | category | flops | bytes accessed | tf_op | source)
XLA Modules:
  0.0 2157.3 jit_solution(15707674450002430969)
XLA Ops:
  14.8 23.0 %all-gather = bf16[16,1,128]{2,1,0:T(2,128)(2,1)S(1)} all-gather(bf16[1,1,128]{2,1,0:T(2,128)(2,1)S(1)} %convert_bitcast_fusion.1), channel_id=1, replica_groups=mesh['seq'=16,'mp'=2] {'seq'}, dimensions={0}, use_global_device_ids=true | all-gather | bytes 4352 | tf_op jit(solution)/shard_map/all_gather | solution.py:39
  39.3 24.8 %all-gather.14.cloned.1.call-done = bf16[2048,1024]{1,0:T(8,128)(2,1)} async-done(((bf16[128,1024]{1,0:T(8,128)(2,1)}), bf16[2048,1024]{1,0:T(8,128)(2,1)}) %all-gather.14.cloned.1.call-update) | async-done | bytes 4194320 | tf_op jit(solution)/shard_map/all_gather | solution.py:41
  64.1 5.1 convolution_convert_fusion.3
  73.1 43.0 %all-gather.10.cloned.1.call-done = bf16[2048,1024]{1,0:T(8,128)(2,1)} async-done(((bf16[128,1024]{1,0:T(8,128)(2,1)}), bf16[2048,1024]{1,0:T(8,128)(2,1)}) %all-gather.10.cloned.1.call-update) | async-done | bytes 4194320 | tf_op jit(solution)/shard_map/all_gather | solution.py:42
  116.1 5.1 convolution_convert_fusion.5
  124.4 43.6 %all-gather.12.cloned.1.call-done = bf16[2048,1024]{1,0:T(8,128)(2,1)} async-done(((bf16[128,1024]{1,0:T(8,128)(2,1)}), bf16[2048,1024]{1,0:T(8,128)(2,1)}) %all-gather.12.cloned.1.call-update) | async-done | bytes 4194320 | tf_op jit(solution)/shard_map/all_gather | solution.py:40
  168.1 5.2 fusion.23
  173.3 7.9 fusion
  181.2 8.2 exponential_reduce_fusion
  189.5 10.3 convolution_convert_fusion.2
  199.8 22.6 %all-gather.16.cloned.1.call-done = bf16[1024,2048]{1,0:T(8,128)(2,1)} async-done(((bf16[1024,128]{1,0:T(8,128)(2,1)}), bf16[1024,2048]{1,0:T(8,128)(2,1)}) %all-gather.16.cloned.1.call-update) | async-done | bytes 4194320 | tf_op jit(solution)/shard_map/all_gather | solution.py:43
  222.4 7.8 fusion.53
  237.5 18.8 all-gather.1
  256.4 102.7 %all-reduce.8.cloned.1.call-done = f32[640,2048]{1,0:T(8,128)} async-done(((f32[640,2048]{1,0:T(8,128)}), f32[640,2048]{1,0:T(8,128)}) %all-reduce.8.cloned.1.call-update) | async-done | bytes 5242896 | tf_op jit(solution)/shard_map/psum | solution.py:116
  365.1 92.5 %all-gather.18.cloned.1.call-done = bf16[2048,2752]{0,1:T(8,128)(2,1)} async-done(((bf16[128,2752]{0,1:T(8,128)(2,1)}), bf16[2048,2752]{0,1:T(8,128)(2,1)}) %all-gather.18.cloned.1.call-update) | async-done | bytes 11272208 | tf_op jit(solution)/shard_map/all_gather | solution.py:50
  457.7 13.6 fusion.54
  471.3 83.3 %all-gather.20.cloned.1.call-done = bf16[2048,2752]{0,1:T(8,128)(2,1)} async-done(((bf16[128,2752]{0,1:T(8,128)(2,1)}), bf16[2048,2752]{0,1:T(8,128)(2,1)}) %all-gather.20.cloned.1.call-update) | async-done | bytes 11272208 | tf_op jit(solution)/shard_map/all_gather | solution.py:51
  554.6 13.5 fusion.55
  568.1 82.8 %all-gather.22.cloned.1.call-done = bf16[2752,2048]{1,0:T(8,128)(2,1)} async-done(((bf16[2752,128]{1,0:T(8,128)(2,1)}), bf16[2752,2048]{1,0:T(8,128)(2,1)}) %all-gather.22.cloned.1.call-update) | async-done | bytes 11272208 | tf_op jit(solution)/shard_map/all_gather | solution.py:52
  650.9 19.4 multiply_convert_fusion.1
  670.3 13.4 fusion.56
  683.7 9.7 convolution_add_fusion
  693.5 13.1 convolution_convert_fusion
  706.6 115.7 %all-reduce.10.cloned.1.call-done = f32[640,2048]{1,0:T(8,128)} async-done(((f32[640,2048]{1,0:T(8,128)}), f32[640,2048]{1,0:T(8,128)}) %all-reduce.10.cloned.1.call-update) | async-done | bytes 5242896 | tf_op jit(solution)/shard_map/psum | solution.py:139
  822.3 6.1 multiply_reduce_fusion.1
  837.9 10.7 convolution_bitcast_fusion
  851.2 12.1 multiply_reduce_fusion
  863.4 7.6 multiply_convert_fusion
  877.9 4.8 fusion.57
  886.4 5.3 fusion.58
  891.7 6.2 add_convert_fusion
  899.6 7.4 fusion.48
  907.1 9.7 fusion.29
  916.8 7.4 fusion.44
  924.3 7.5 fusion.46
  931.9 15.5 fusion.60
  947.5 15.5 fusion.61
  963.1 15.9 fusion.59
  980.8 49.2 %all-reduce.12.cloned.1.call-done = (bf16[640,2048]{1,0:T(8,128)(2,1)}, bf16[640,2048]{1,0:T(8,128)(2,1)}) async-done(((bf16[640,2048]{1,0:T(8,128)(2,1)}, bf16[640,2048]{1,0:T(8,128)(2,1)}), (bf16[640,2048]{1,0:T(8,128)(2,1)}, bf16[640,2048]{1,0:T(8,128)(2,1)})) %all-reduce.12.cloned.1.call-update) | async-done | bytes 5242896 | tf_op jit(solution)/shard_map/psum | solution.py:127
  1033.4 63.0 %all-reduce.2 = (f32[2048]{0:T(1024)S(1)}, f32[2048]{0:T(1024)S(1)}) all-reduce(f32[2048]{0:T(1024)S(1)} %get-tuple-element.37, f32[2048]{0:T(1024)S(1)} %copy-done.20), channel_id=2, replica_groups=mesh['seq'=16,'mp'=2] {'seq'}, use_global_device_ids=true, to_apply=%region_14.15.clone | all-reduce | flops 4096 | bytes 32768
  1097.6 6.0 add_convert_fusion.1
  1108.3 31.9 %reduce-scatter.8.cloned.1.call-done = f32[128,1024]{1,0:T(8,128)} async-done(((f32[2048,1024]{1,0:T(8,128)}), f32[128,1024]{1,0:T(8,128)}) %reduce-scatter.8.cloned.1.call-update) | async-done | bytes 524304 | tf_op jit(solution)/shard_map/reduce_scatter | solution.py:194
  1140.2 109.7 %reduce-scatter.14.cloned.1.call-done = f32[1024,128]{1,0:T(8,128)} async-done(((f32[1024,2048]{1,0:T(8,128)}), f32[1024,128]{1,0:T(8,128)}) %reduce-scatter.14.cloned.1.call-update) | async-done | bytes 524304 | tf_op jit(solution)/shard_map/reduce_scatter | solution.py:197
  1249.8 109.6 %reduce-scatter.12.cloned.1.call-done = f32[128,1024]{1,0:T(8,128)} async-done(((f32[2048,1024]{1,0:T(8,128)}), f32[128,1024]{1,0:T(8,128)}) %reduce-scatter.12.cloned.1.call-update) | async-done | bytes 524304 | tf_op jit(solution)/shard_map/reduce_scatter | solution.py:196
  1359.5 109.4 %reduce-scatter.10.cloned.1.call-done = f32[128,1024]{1,0:T(8,128)} async-done(((f32[2048,1024]{1,0:T(8,128)}), f32[128,1024]{1,0:T(8,128)}) %reduce-scatter.10.cloned.1.call-update) | async-done | bytes 524304 | tf_op jit(solution)/shard_map/reduce_scatter | solution.py:195
  1468.9 227.6 %reduce-scatter.16.cloned.1.call-done = f32[128,2752]{0,1:T(8,128)} async-done(((f32[2048,2752]{0,1:T(8,128)}), f32[128,2752]{0,1:T(8,128)}) %reduce-scatter.16.cloned.1.call-update) | async-done | bytes 1409040 | tf_op jit(solution)/shard_map/reduce_scatter | solution.py:199
  1696.5 227.0 %reduce-scatter.18.cloned.1.call-done = f32[128,2752]{0,1:T(8,128)} async-done(((f32[2048,2752]{0,1:T(8,128)}), f32[128,2752]{0,1:T(8,128)}) %reduce-scatter.18.cloned.1.call-update) | async-done | bytes 1409040 | tf_op jit(solution)/shard_map/reduce_scatter | solution.py:200
  1923.4 226.9 %reduce-scatter.20.cloned.1.call-done = f32[2752,128]{1,0:T(8,128)} async-done(((f32[2752,2048]{1,0:T(8,128)}), f32[2752,128]{1,0:T(8,128)}) %reduce-scatter.20.cloned.1.call-update) | async-done | bytes 1409040 | tf_op jit(solution)/shard_map/reduce_scatter | solution.py:201
  (171 shorter events, 64.3 us)
Async XLA Ops:
  7.2 7.6 copy-start.28
  7.2 30.7 %copy-start.29 = (s32[5]{0:T(128)S(1)}, s32[5]{0:T(128)}, u32[]{:S(2)}) copy-start(s32[5]{0:T(128)} %param.17) | copy-start | bytes 64
  7.2 31.1 %copy-start.1 = (bf16[640,2048]{1,0:T(8,128)(2,1)S(1)}, bf16[640,2048]{1,0:T(8,128)(2,1)}, u32[]{:S(2)}) copy-start(bf16[640,2048]{1,0:T(8,128)(2,1)} %param.16) | copy-start | bytes 7864324
  7.2 56.9 %all-gather.14.cloned.1.call-start = ((), (), s32[]{:S(2)}) async-start(), calls=%async_computation.9 | async-start | bytes 4456448 | tf_op jit(solution)/shard_map/all_gather | solution.py:41
  9.2 106.9 %all-gather.10.cloned.1.call-start = ((), (), s32[]{:S(2)}) async-start(), calls=%async_computation.7 | async-start | bytes 4456448 | tf_op jit(solution)/shard_map/all_gather | solution.py:42
  11.1 157.0 %all-gather.12.cloned.1.call-start = ((), (), s32[]{:S(2)}) async-start(), calls=%async_computation.8 | async-start | bytes 4456448 | tf_op jit(solution)/shard_map/all_gather | solution.py:40
  12.9 209.5 %all-gather.16.cloned.1.call-start = ((), (), s32[]{:S(2)}) async-start(), calls=%async_computation.10 | async-start | bytes 4456448 | tf_op jit(solution)/shard_map/all_gather | solution.py:43
  14.8 344.3 %all-reduce.8.cloned.1.call-start = ((), (), s32[]{:S(2)}) async-start(), calls=%async_computation.11 | async-start | bytes 10485760 | tf_op jit(solution)/shard_map/psum | solution.py:116
  37.9 130.2 %copy-start.16 = (f32[16,1,128]{2,1,0:T(1,128)}, f32[16,1,128]{2,1,0:T(1,128)S(1)}, u32[]{:S(2)}) copy-start(f32[16,1,128]{2,1,0:T(1,128)S(1)} %convert_element_type.190) | copy-start | bytes 24580
  38.9 129.2 %copy-start.18 = (f32[640]{0:T(1024)}, f32[640]{0:T(1024)S(1)}, u32[]{:S(2)}) copy-start(f32[640]{0:T(1024)S(1)} %add_rsqrt_fusion.1) | copy-start | bytes 7684
  70.3 103.1 %collective-permute-start.1 = (bf16[64,1024]{1,0:T(8,128)(2,1)S(1)}, bf16[64,1024]{1,0:T(8,128)(2,1)}, u32[]{:S(2)}, u32[]{:S(2)}) collective-permute-start(bf16[64,1024]{1,0:T(8,128)(2,1)S(1)} %slice.88), channel_id=1, source_target_pairs={{0,2},{2,4},{4,6},{6,8},{8,10},{10,12},{12,14},{14,16},{16,18},{18... | collective-permute-start | bytes 393224 | tf_op jit(solution)/shard_map/ppermute | solution.py:18
  122.2 67.2 %collective-permute-start = (bf16[64,1024]{1,0:T(8,128)(2,1)S(1)}, bf16[64,1024]{1,0:T(8,128)(2,1)S(1)}, u32[]{:S(2)}, u32[]{:S(2)}) collective-permute-start(bf16[64,1024]{1,0:T(8,128)(2,1)S(1)} %slice.87), channel_id=1, source_target_pairs={{0,2},{2,4},{4,6},{6,8},{8,10},{10,12},{12,14},{14,16},{16,18},{18... | collective-permute-start | bytes 393224 | tf_op jit(solution)/shard_map/ppermute | solution.py:18
  173.3 7.9 copy-start.33
  181.2 8.2 copy-start.9
  230.2 7.3 copy-start.30
  230.3 227.4 %all-gather.18.cloned.1.call-start = ((), (), s32[]{:S(2)}) async-start(), calls=%async_computation.12 | async-start | bytes 11976704 | tf_op jit(solution)/shard_map/all_gather | solution.py:50
  232.6 322.0 %all-gather.20.cloned.1.call-start = ((), (), s32[]{:S(2)}) async-start(), calls=%async_computation.13 | async-start | bytes 11976704 | tf_op jit(solution)/shard_map/all_gather | solution.py:51
  235.1 415.8 %all-gather.22.cloned.1.call-start = ((), (), s32[]{:S(2)}) async-start(), calls=%async_computation.14 | async-start | bytes 11976704 | tf_op jit(solution)/shard_map/all_gather | solution.py:52
  237.5 584.9 %all-reduce.10.cloned.1.call-start = ((), (), s32[]{:S(2)}) async-start(), calls=%async_computation.15 | async-start | bytes 10485760 | tf_op jit(solution)/shard_map/psum | solution.py:139
  365.1 189.4 %copy-start.6 = (bf16[640,2048]{1,0:T(8,128)(2,1)}, bf16[640,2048]{1,0:T(8,128)(2,1)S(1)}, u32[]{:S(2)}) copy-start(bf16[640,2048]{1,0:T(8,128)(2,1)S(1)} %multiply_convert_fusion.4) | copy-start | bytes 7864324
  670.3 13.4 copy-start.36
  670.3 13.4 copy-start.35
  670.3 13.4 copy-start.24
  693.5 336.5 %all-reduce.12.cloned.1.call-start = ((), (), s32[]{:S(2)}) async-start(), calls=%async_computation.23 | async-start | bytes 10485760 | tf_op jit(solution)/shard_map/psum | solution.py:127
  706.6 121.8 %copy-start.7 = (bf16[640,2048]{1,0:T(8,128)(2,1)S(1)}, bf16[640,2048]{1,0:T(8,128)(2,1)}, u32[]{:S(2)}) copy-start(bf16[640,2048]{1,0:T(8,128)(2,1)} %param.27) | copy-start | bytes 7864324
  822.3 6.1 copy-start.4
  828.4 6.5 copy-start.27
  837.9 10.8 copy-start.11
  837.9 13.3 copy-start.10
  837.9 25.5 %slice-start = ((s8[14417920]{0:T(1024)(128)(4,1)}), s8[4194304]{0:T(1024)(128)(4,1)S(1)}, s32[]{:S(2)}) async-start(s8[14417920]{0:T(1024)(128)(4,1)} %bitcast.102), calls=%async_computation.24 | async-start | bytes 8388608
  837.9 25.4 %slice-start.1 = ((s8[14417920]{0:T(1024)(128)(4,1)}), s8[1835008]{0:T(1024)(128)(4,1)S(1)}, s32[]{:S(2)}) async-start(s8[14417920]{0:T(1024)(128)(4,1)} %bitcast.102), calls=%async_computation.25 | async-start | bytes 3670016
  849.6 13.7 slice-start.2
  849.6 13.7 slice-start.3
  849.6 33.5 %collective-permute-start.3 = (bf16[64,8,128]{2,0,1:T(8,128)(2,1)S(1)}, bf16[64,8,128]{2,0,1:T(8,128)(2,1)S(1)}, u32[]{:S(2)}, u32[]{:S(2)}) collective-permute-start(bf16[64,8,128]{2,0,1:T(8,128)(2,1)S(1)} %slice.104), channel_id=1, source_target_pairs={{2,0},{4,2},{6,4},{8,6},{10,8},{12,10},{14,12},{16,14},{18,16},{20... | collective-permute-start | bytes 393224 | tf_op jit(solution)/shard_map/ppermute | solution.py:18
  863.4 7.6 copy-start.34
  873.1 9.8 copy-start.15
  873.1 11.5 collective-permute-start.2
  886.4 5.3 copy-start.12
  886.4 5.3 copy-start.13
  897.9 242.2 %reduce-scatter.8.cloned.1.call-start = ((), (), s32[]{:S(2)}) async-start(), calls=%async_computation.16 | async-start | bytes 8912896 | tf_op jit(solution)/shard_map/reduce_scatter | solution.py:194
  907.0 342.8 %reduce-scatter.14.cloned.1.call-start = ((), (), s32[]{:S(2)}) async-start(), calls=%async_computation.19 | async-start | bytes 8912896 | tf_op jit(solution)/shard_map/reduce_scatter | solution.py:197
  916.8 442.7 %reduce-scatter.12.cloned.1.call-start = ((), (), s32[]{:S(2)}) async-start(), calls=%async_computation.18 | async-start | bytes 8912896 | tf_op jit(solution)/shard_map/reduce_scatter | solution.py:196
  924.3 544.6 %reduce-scatter.10.cloned.1.call-start = ((), (), s32[]{:S(2)}) async-start(), calls=%async_computation.17 | async-start | bytes 8912896 | tf_op jit(solution)/shard_map/reduce_scatter | solution.py:195
  931.9 764.6 %reduce-scatter.16.cloned.1.call-start = ((), (), s32[]{:S(2)}) async-start(), calls=%async_computation.20 | async-start | bytes 23953408 | tf_op jit(solution)/shard_map/reduce_scatter | solution.py:199
  947.5 975.9 %reduce-scatter.18.cloned.1.call-start = ((), (), s32[]{:S(2)}) async-start(), calls=%async_computation.21 | async-start | bytes 23953408 | tf_op jit(solution)/shard_map/reduce_scatter | solution.py:200
  963.0 1187.3 %reduce-scatter.20.cloned.1.call-start = ((), (), s32[]{:S(2)}) async-start(), calls=%async_computation.22 | async-start | bytes 23953408 | tf_op jit(solution)/shard_map/reduce_scatter | solution.py:201
  979.0 54.4 %copy-start.20 = (f32[2048]{0:T(1024)S(1)}, f32[2048]{0:T(1024)}, u32[]{:S(2)}) copy-start(f32[2048]{0:T(1024)} %get-tuple-element.35) | copy-start | bytes 24580
  1097.6 6.0 copy-start.5
  (14 other events, 41.2 us)
Sparse Core Ops, SparseCore 0:
  10.8 53.2 all-gather.13
  66.8 49.2 all-gather.9
  118.8 49.2 all-gather.11
  170.6 51.6 all-gather.15
  230.4 128.6 all-reduce.7
  361.9 95.7 all-gather.17
  460.6 93.8 all-gather.19
  557.0 93.8 all-gather.21
  693.6 128.7 all-reduce.9
  898.0 131.9 all-reduce.11
  1035.2 104.9 reduce-scatter.7
  1145.2 104.5 reduce-scatter.13
  1255.0 104.4 reduce-scatter.11
  1364.5 104.3 reduce-scatter.9
  1474.1 222.3 reduce-scatter.15
  1701.7 221.6 reduce-scatter.17
  1928.7 221.6 reduce-scatter.19
where the time goes:
time: 2160 us
  waiting for transfers between devices  1700 us (79%)
  matrix products  250 us (12%)
  blocking collectives  105 us (5%)
  other arithmetic  60.5 us (3%)
    reduce_scatter x1, waiting for transfers between devices, per_device(): lax.psum_scatter(grad_wgate, 'seq', scatter_dimension=0, tiled=True)  228 us
    reduce_scatter x1, waiting for transfers between devices, per_device(): lax.psum_scatter(grad_wupper, 'seq', scatter_dimension=0, tiled=True)  227 us
    reduce_scatter x1, waiting for transfers between devices, per_device(): lax.psum_scatter(grad_down, 'seq', scatter_dimension=1, tiled=True)  227 us
    psum x1, waiting for transfers between devices, per_device(): lax.psum(mat_nt(grad_gate, wg_full) + mat_nt(grad_upper, wu_full), 'mp')  116 us
    reduce_scatter x1, waiting for transfers between devices, per_device(): lax.psum_scatter(grad_wout, 'seq', scatter_dimension=1, tiled=True)  110 us
    reduce_scatter x1, waiting for transfers between devices, per_device(): lax.psum_scatter(grad_wvalue, 'seq', scatter_dimension=0, tiled=True)  110 us
    reduce_scatter x1, waiting for transfers between devices, per_device(): lax.psum_scatter(grad_wkey, 'seq', scatter_dimension=0, tiled=True)  109 us
    psum x1, waiting for transfers between devices, per_device(): branch = lax.psum(mat_nn(mixed, wo_full), 'mp')  103 us
  transfers between devices with their start and end apart: 21, of which 17 were waited for; matrix products, arithmetic and copies ran while one was open for 10% of the time, Pallas kernels for 0%

commit v1 on v0

v1 whole, which is shorter than its diff:
```python
import functools
import math

import jax
import jax.numpy as jnp
from jax import lax
from jax.experimental import pallas as pl
from jax.experimental.pallas import tpu as pltpu
from jax.sharding import PartitionSpec as P

HEAD_DIM = 128
WINDOW = 64
EPSILON = 1e-06
BF16 = jnp.bfloat16
F32 = jnp.float32


def mat_nn(left, right):
    return jnp.dot(left, right, preferred_element_type=F32)


def mat_nt(left, right):
    return lax.dot_general(left, right, (((1,), (1,)), ((), ())), preferred_element_type=F32)


def mat_tn(left, right):
    return lax.dot_general(left, right, (((0,), (0,)), ((), ())), preferred_element_type=F32)


def shift_pairs(count, steps):
    return [(s, s + steps) for s in range(max(0, -steps), min(count, count - steps))]


def flip_pairs(count, bit):
    return [(s, s ^ bit) for s in range(count)]


def ring_pairs(count):
    return [(s, (s + 4) % count) for s in range(count)]


def relative_blocks(count):
    me = lax.axis_index("seq")
    place = jnp.arange(count, dtype=jnp.int32)
    outers = count // 4
    inner, middle, outer = place // (2 * outers), (place // outers) % 2, place % outers
    return (
        ((me // 4 + outer) % outers) * 4 + ((me // 2 + middle) % 2) * 2 + (me + inner) % 2
    ).astype(jnp.int32)


def rolled(values, steps, axis):
    return lax.dynamic_slice_in_dim(
        jnp.concatenate([values, values], axis), steps, values.shape[axis], axis
    )


def copy_block(order_ref, in_ref, out_ref):
    out_ref[...] = in_ref[...]


def to_relative(values, order):
    rows, columns = values.shape
    count = order.shape[0]
    width = columns // count
    if width % 128:
        me, outers = lax.axis_index("seq"), count // 4
        turned = rolled(values.reshape(rows, outers, 2, 2, width), me // 4, 1)
        turned = rolled(rolled(turned, (me // 2) % 2, 2), me % 2, 3)
        return jnp.transpose(turned, (0, 3, 2, 1, 4)).reshape(rows, columns)
    return pl.pallas_call(
        copy_block,
        grid_spec=pltpu.PrefetchScalarGridSpec(
            num_scalar_prefetch=1,
            grid=(count,),
            in_specs=[pl.BlockSpec((rows, width), lambda i, order: (0, order[i]))],
            out_specs=pl.BlockSpec((rows, width), lambda i, order: (0, i)),
        ),
        out_shape=jax.ShapeDtypeStruct(values.shape, values.dtype),
        cost_estimate=pl.CostEstimate(flops=0, bytes_accessed=4 * rows * columns, transcendentals=0),
    )(order, values)


def sum_to_owner(partial, kind=BF16):
    count = lax.axis_size("seq")
    outers = count // 4
    block = partial.shape[0] // count
    rest = partial.shape[1:]
    partial = partial.astype(kind).reshape((2, 2 * outers * block) + rest)
    got = lax.ppermute(partial[1], "seq", flip_pairs(count, 1))
    paired = (partial[0].astype(F32) + got.astype(F32)).astype(kind)
    paired = paired.reshape((2, outers * block) + rest)
    got = lax.ppermute(paired[1], "seq", flip_pairs(count, 2))
    four = (paired[0].astype(F32) + got.astype(F32)).astype(kind).reshape((outers, block) + rest)
    total = four[outers - 1]
    for r in range(outers - 2, -1, -1):
        got = lax.ppermute(total, "seq", ring_pairs(count))
        total = four[r].astype(F32) + got.astype(F32)
        if r:
            total = total.astype(kind)
    return total.astype(F32)


def sum_mp(partial):
    own = lax.optimization_barrier(partial.astype(BF16))
    count = lax.axis_size("mp")
    if count != 2:
        return lax.psum(own.astype(F32), "mp")
    other = lax.ppermute(own, "mp", [(0, 1), (1, 0)])
    return own.astype(F32) + other.astype(F32)


def attend(q_ref, k_ref, v_ref, bias_ref, out_ref):
    scale = 1.0 / math.sqrt(HEAD_DIM)
    for i in range(q_ref.shape[0] // WINDOW):
        rows, keys = slice(i * WINDOW, (i + 1) * WINDOW), slice(i * WINDOW, (i + 2) * WINDOW)
        scores = mat_nt(q_ref[rows], k_ref[keys]) * scale + bias_ref[rows]
        top = jnp.max(scores, axis=1, keepdims=True)
        weights = jnp.exp(scores - top)
        probs = weights / jnp.sum(weights, axis=1, keepdims=True)
        out_ref[rows] = mat_nn(probs.astype(BF16), v_ref[keys]).astype(BF16)


def attend_back(q_ref, k_ref, v_ref, bias_ref, da_ref, dq_ref, dk_ref, dv_ref):
    scale = 1.0 / math.sqrt(HEAD_DIM)
    steps = q_ref.shape[0] // WINDOW
    dk_low = dv_low = None
    for i in range(steps):
        rows, keys = slice(i * WINDOW, (i + 1) * WINDOW), slice(i * WINDOW, (i + 2) * WINDOW)
        query, key, value, da = q_ref[rows], k_ref[keys], v_ref[keys], da_ref[rows]
        scores = mat_nt(query, key) * scale + bias_ref[rows]
        top = jnp.max(scores, axis=1, keepdims=True)
        weights = jnp.exp(scores - top)
        probs = weights / jnp.sum(weights, axis=1, keepdims=True)
        dp = mat_nt(da, value)
        inner = jnp.sum(probs * dp, axis=1, keepdims=True)
        ds = (probs * (dp - inner)).astype(BF16)
        dv = mat_tn(probs.astype(BF16), da)
        dk = mat_tn(ds, query) * scale
        dq_ref[rows] = (mat_nn(ds, key) * scale).astype(BF16)
        if i:
            dk_ref[rows] = dk[:WINDOW] + dk_low
            dv_ref[rows] = dv[:WINDOW] + dv_low
        else:
            dk_ref[rows] = dk[:WINDOW]
            dv_ref[rows] = dv[:WINDOW]
        dk_low, dv_low = dk[WINDOW:], dv[WINDOW:]
    dk_ref[steps * WINDOW :] = dk_low
    dv_ref[steps * WINDOW :] = dv_low


def head_spec(rows):
    return pl.BlockSpec((rows, HEAD_DIM), lambda h: (0, h))


def attention_forward(queries, key_ext, value_ext, bias):
    tokens, width = queries.shape
    ext = tokens + WINDOW
    return pl.pallas_call(
        attend,
        grid=(width // HEAD_DIM,),
        in_specs=[
            head_spec(tokens),
            head_spec(ext),
            head_spec(ext),
            pl.BlockSpec((tokens, 2 * WINDOW), lambda h: (0, 0)),
        ],
        out_specs=head_spec(tokens),
        out_shape=jax.ShapeDtypeStruct((tokens, width), BF16),
        cost_estimate=pl.CostEstimate(
            flops=8 * tokens * width * WINDOW, bytes_accessed=8 * tokens * width, transcendentals=tokens * width
        ),
    )(queries, key_ext, value_ext, bias)


def attention_backward(queries, key_ext, value_ext, bias, da):
    tokens, width = queries.shape
    ext = tokens + WINDOW
    return pl.pallas_call(
        attend_back,
        grid=(width // HEAD_DIM,),
        in_specs=[
            head_spec(tokens),
            head_spec(ext),
            head_spec(ext),
            pl.BlockSpec((tokens, 2 * WINDOW), lambda h: (0, 0)),
            head_spec(tokens),
        ],
        out_specs=(head_spec(tokens), head_spec(ext), head_spec(ext)),
        out_shape=(
            jax.ShapeDtypeStruct((tokens, width), BF16),
            jax.ShapeDtypeStruct((ext, width), F32),
            jax.ShapeDtypeStruct((ext, width), F32),
        ),
        cost_estimate=pl.CostEstimate(
            flops=20 * tokens * width * WINDOW, bytes_accessed=20 * tokens * width, transcendentals=tokens * width
        ),
    )(queries, key_ext, value_ext, bias, da)


def norm_back(grad_normed, unit_rows, inverse_rows, gain):
    scaled = grad_normed * gain
    return inverse_rows * (scaled - unit_rows * jnp.mean(scaled * unit_rows, axis=1, keepdims=True))


def gather(shards):
    return lax.all_gather(jnp.concatenate([s.astype(BF16) for s in shards], 1), "seq", axis=0, tiled=True)


def per_device(
    x_in, lengths, g_attn, w_query, w_key, w_value, w_out, g_ffn, w_gate, w_up, w_down, cotangent
):
    tokens = x_in.shape[0]
    width = w_query.shape[1]
    ff = w_gate.shape[1]
    count = lax.axis_size("seq")
    cut = (ff // 2 + 127) // 128 * 128
    cuts = ((0, cut), (cut, ff))

    gains = lax.all_gather(jnp.stack([g_attn, g_ffn], 1).astype(BF16), "seq", axis=0, tiled=True)
    gain_one, gain_two = gains[:, 0].astype(F32), gains[:, 1].astype(F32)
    w_out_t, w_down_t = w_out.T, w_down.T
    attn_w = gather((w_query, w_key, w_value, w_out_t))
    ffn_w = [gather((w_gate[:, a:b], w_up[:, a:b], w_down_t[:, a:b])) for a, b in cuts]
    wqkv, wo_t = attn_w[:, : 3 * width], attn_w[:, 3 * width :]

    order = relative_blocks(count)
    first_place = lax.axis_index("seq") * tokens
    row = jnp.arange(tokens, dtype=jnp.int32)[:, None]
    column = jnp.arange(2 * WINDOW, dtype=jnp.int32)[None, :]
    key_place = row // WINDOW * WINDOW + column - WINDOW
    ends = [lengths[0]]
    for i in range(1, lengths.shape[0] - 1):
        ends.append(ends[-1] + lengths[i])
    seg_row = sum(((first_place + row) >= e).astype(jnp.int32) for e in ends)
    seg_key = sum(((first_place + key_place) >= e).astype(jnp.int32) for e in ends)
    allowed = (
        (key_place <= row)
        & (key_place > row - WINDOW)
        & (first_place + key_place >= 0)
        & (seg_row == seg_key)
    )
    bias = jnp.where(allowed, 0.0, -1e30).astype(F32)

    x_full = x_in.astype(F32)
    inverse_one = lax.rsqrt(jnp.mean(x_full * x_full, axis=1, keepdims=True) + EPSILON)
    unit_one = x_full * inverse_one
    normed = (unit_one * gain_one).astype(BF16)
    normed_rel = to_relative(normed, order)
    cot_rel = to_relative(cotangent, order)

    qkv = mat_nn(normed, wqkv).astype(BF16)
    queries = qkv[:, :width]
    tail = lax.ppermute(qkv[tokens - WINDOW :, width:], "seq", shift_pairs(count, 1))
    kv_ext = jnp.concatenate([tail, qkv[:, width:]], 0)
    key_ext, value_ext = kv_ext[:, :width], kv_ext[:, width:]
    mixed = attention_forward(queries, key_ext, value_ext, bias)
    middle = x_full + sum_mp(mat_nt(mixed, wo_t))
    inverse_two = lax.rsqrt(jnp.mean(middle * middle, axis=1, keepdims=True) + EPSILON)
    unit_two = middle * inverse_two
    normed_two = (unit_two * gain_two).astype(BF16)
    normed_two_rel = to_relative(normed_two, order)

    ffn_out = grad_normed_two = 0.0
    ffn_sums = []
    for (a, b), w in zip(cuts, ffn_w):
        n = b - a
        grad_hidden = mat_nn(cotangent, w[:, 2 * n :])
        gate_up = mat_nn(normed_two, w[:, : 2 * n])
        gate, up = gate_up[:, :n], gate_up[:, n:]
        sigma = jax.nn.sigmoid(gate)
        silu = gate * sigma
        hidden = (silu * up).astype(BF16)
        ffn_out = ffn_out + mat_nt(hidden, w[:, 2 * n :])
        grad_gate = (grad_hidden * up * sigma * (1.0 + gate * (1.0 - sigma))).astype(BF16)
        grad_up = (grad_hidden * silu).astype(BF16)
        grad_gate_up = jnp.concatenate([grad_gate, grad_up], 1)
        grad_normed_two = grad_normed_two + mat_nt(grad_gate_up, w[:, : 2 * n])
        grads = jnp.concatenate(
            [mat_tn(normed_two_rel, grad_gate_up).astype(BF16), mat_tn(cot_rel, hidden).astype(BF16)], 1
        )
        ffn_sums.append(sum_to_owner(grads))
    grad_normed_two = sum_mp(grad_normed_two)
    result = middle + sum_mp(ffn_out)
    grad_gain_two = jnp.sum(grad_normed_two * unit_two, axis=0)
    grad_middle = cotangent.astype(F32) + norm_back(grad_normed_two, unit_two, inverse_two, gain_two)
    grad_branch = grad_middle.astype(BF16)
    grad_branch_rel = to_relative(grad_branch, order)
    grad_wout_t = mat_tn(grad_branch_rel, mixed).astype(BF16)
    da = mat_nn(grad_branch, wo_t).astype(BF16)
    grad_query, dk_ext, dv_ext = attention_backward(queries, key_ext, value_ext, bias, da)
    back = lax.ppermute(
        jnp.concatenate([dk_ext[:WINDOW], dv_ext[:WINDOW]], 1).astype(BF16), "seq", shift_pairs(count, -1)
    ).astype(F32)

    def owned(ext, returned):
        return jnp.concatenate(
            [ext[WINDOW:tokens].astype(BF16), (ext[tokens:] + returned).astype(BF16)], 0
        )

    grad_key = owned(dk_ext, back[:, :width])
    grad_value = owned(dv_ext, back[:, width:])
    grad_qkv = jnp.concatenate([grad_query, grad_key, grad_value], 1)
    out_sum = sum_to_owner(grad_wout_t)
    qkv_sum = sum_to_owner(mat_tn(normed_rel, grad_qkv).astype(BF16))
    grad_normed = sum_mp(mat_nt(grad_qkv, wqkv))
    grad_gain_one = jnp.sum(grad_normed * unit_one, axis=0)
    grad_input = grad_middle + norm_back(grad_normed, unit_one, inverse_one, gain_one)
    gain_parts = jnp.stack([grad_gain_one, grad_gain_two], 0)
    gain_blocks = jnp.swapaxes(gain_parts.reshape(2, count, -1), 0, 1)
    chosen = order[:, None] == jnp.arange(count, dtype=jnp.int32)[None, :]
    gain_rel = jnp.sum(jnp.where(chosen[:, :, None, None], gain_blocks[None], 0.0), axis=1)
    gain_sums = sum_to_owner(gain_rel, F32)[0]

    def columns(part):
        pieces = []
        for (a, b), s in zip(cuts, ffn_sums):
            pieces.append(s[:, part * (b - a) : (part + 1) * (b - a)])
        return jnp.concatenate(pieces, 1)

    return (
        result.astype(BF16),
        grad_input.astype(BF16),
        gain_sums[0],
        qkv_sum[:, :width],
        qkv_sum[:, width : 2 * width],
        qkv_sum[:, 2 * width :],
        out_sum.T,
        gain_sums[1],
        columns(0),
        columns(1),
        columns(2).T,
    )


def solution(mesh):
    placed = (
        P("seq", None),
        P(),
        P("seq"),
        P("seq", "mp"),
        P("seq", "mp"),
        P("seq", "mp"),
        P("mp", "seq"),
        P("seq"),
        P("seq", "mp"),
        P("seq", "mp"),
        P("mp", "seq"),
        P("seq", None),
    )
    return jax.shard_map(
        per_device,
        mesh=mesh,
        in_specs=placed,
        out_specs=(
            P("seq", None),
            P("seq", None),
            P("seq"),
            P("seq", "mp"),
            P("seq", "mp"),
            P("seq", "mp"),
            P("mp", "seq"),
            P("seq"),
            P("seq", "mp"),
            P("seq", "mp"),
            P("mp", "seq"),
        ),
        check_vma=False,
    )
```

time: 2160 us -> 1120 us (0.52)
  waiting for transfers between devices: 1700 us -> 589 us
  Pallas kernels: 0 us -> 109 us
  blocking collectives: 105 us -> 23.1 us
  matrix products: 250 us -> 180 us
  other arithmetic: 60.5 us -> 110 us
  local copies, waits for them, and re-layouts: 14.5 us -> 47.6 us
  starting transfers between devices: 8.83 us -> 34.2 us
    reduce_scatter x7 -> x0, waiting for transfers between devices: 1040 us -> none  [the longest x1 228 us: per_device(): lax.psum_scatter(grad_wgate, 'seq', scatter_dimension=0, tiled=True)]
    ppermute x4 -> x31, waiting for transfers between devices: 0.01 us -> 413 us  [the longest x5 187 us: sum_to_owner(): got = lax.ppermute(paired[1], 'seq', flip_pairs(count, 2))]
    psum x3 -> x0, waiting for transfers between devices: 268 us -> none  [the longest x1 116 us: per_device(): lax.psum(mat_nt(grad_gate, wg_full) + mat_nt(grad_upper, wu_full), 'mp')]
    all_gather x7 -> x3, waiting for transfers between devices: 393 us -> 176 us  [gather(): lax.all_gather(jnp.concatenate([s.astype(BF16) for s in shards], 1), 'seq...]
    pallas_call x0 -> x6, Pallas kernels: none -> 109 us  [the longest x4 42 us: to_relative(): pl.pallas_call(copy_block, grid_spec=pltpu.PrefetchScalarGridSpec(num_sca...]
    unnamed x1 -> x0, blocking collectives: 63 us -> none
    dot_general x13 -> x6, matrix products: 110 us -> 63.6 us  [mat_nn(): return jnp.dot(left, right, preferred_element_type=F32)]
    convert_element_type x13 -> x24, other arithmetic: 33 us -> 66.2 us  [the longest x4 25.7 us: sum_to_owner(): paired = (partial[0].astype(F32) + got.astype(F32)).astype(kind)]
  transfers between devices with their start and end apart: 21 -> 34, of which waited for: 17 -> 20; matrix products, arithmetic and copies ran while one was open for 10% -> 24% of each run, Pallas kernels for 0% -> 10%
where the time goes in v1:
time: 1120 us; the launch traced here: 1110 us
  waiting for transfers between devices  589 us (53%)
  matrix products  180 us (16%)
  other arithmetic  110 us (10%)
  Pallas kernels  109 us (10%)
  local copies, waits for them, and re-layouts  47.6 us (4%)
  starting transfers between devices  34.2 us (3%)
  blocking collectives  23.1 us (2%)
  between operations  17.9 us (2%)
    ppermute x5, waiting for transfers between devices, sum_to_owner(): got = lax.ppermute(paired[1], 'seq', flip_pairs(count, 2))  187 us
    all_gather x3, waiting for transfers between devices, gather(): lax.all_gather(jnp.concatenate([s.astype(BF16) for s in shards], 1), 'seq...  176 us
    ppermute x15, waiting for transfers between devices, sum_to_owner(): got = lax.ppermute(total, 'seq', ring_pairs(count))  149 us
    ppermute x4, waiting for transfers between devices, sum_mp(): other = lax.ppermute(own, 'mp', [(0, 1), (1, 0)])  77 us
    dot_general x6, matrix products, mat_nn(): return jnp.dot(left, right, preferred_element_type=F32)  63.6 us
    dot_general x6, matrix products, mat_nt(): lax.dot_general(left, right, (((1,), (1,)), ((), ())), preferred_element_...  60.4 us
    dot_general x6, matrix products, mat_tn(): lax.dot_general(left, right, (((0,), (0,)), ((), ())), preferred_element_...  55.7 us
    pallas_call x4, Pallas kernels, to_relative(): pl.pallas_call(copy_block, grid_spec=pltpu.PrefetchScalarGridSpec(num_sca...  42 us
  transfers between devices with their start and end apart: 34, of which 20 were waited for; matrix products, arithmetic and copies ran while one was open for 24% of the time, Pallas kernels for 10%

profile of v1, /device:TPU:0, one launch (start us, length us, event | category | flops | bytes accessed | tf_op | source)
XLA Modules:
  0.0 1110.1 jit_solution(10625849097843379254)
XLA Ops:
  25.6 23.1 %all_gather.12 = bf16[2048,2]{0,1:T(2,128)(2,1)S(1)} all-gather(bf16[128,2]{0,1:T(2,128)(2,1)S(1)} %pad_maximum_fusion.15), channel_id=1, replica_groups=mesh['seq'=16,'mp'=2] {'seq'}, dimensions={0}, use_global_device_ids=true | all-gather | bytes 8704 | tf_op jit(solution)/shard_map/all_gather | solution.py:220
  52.8 93.6 %all-gather.4.cloned.1.call-done = bf16[2048,4096]{0,1:T(8,128)(2,1)} async-done(((bf16[128,4096]{0,1:T(8,128)(2,1)}), bf16[2048,4096]{0,1:T(8,128)(2,1)}) %all-gather.4.cloned.1.call-update) | async-done | bytes 16777232 | tf_op jit(solution)/shard_map/all_gather | solution.py:207
  146.4 12.1 %fusion.36 = bf16[640,3072]{1,0:T(8,128)(2,1)S(1)} fusion(bf16[640,2048]{1,0:T(8,128)(2,1)} %fusion.18.in_ref, bf16[2048,4096]{0,1:T(8,128)(2,1)} %all-gather.4.cloned.1.call-done), kind=kOutput, calls=%fused_computation.66 | convolution fusion | flops 8055029760 | bytes 19136512 | tf_op jit(solution)/shard_map/dot_general | solution.py:19
  165.8 28.4 %shard_map.203 = bf16[640,1024]{1,0:T(8,128)(2,1)} custom-call(bf16[640,1024]{1,0:T(8,128)(2,1)} %slice.402.q_ref, bf16[704,1024]{1,0:T(8,128)(2,1)} %get-tuple-element.76.k_ref, bf16[704,1024]{1,0:T(8,128)(2,1)} %get-tuple-element.75.v_ref, f32[640,128]{1,0:T(8,128)} %fusion.76.bias_ref), custom_call_target="tpu_custom_call" | custom-call | flops 335544320 | bytes 5242880 | tf_op jit(solution)/shard_map/pallas_call | solution.py:159
  194.3 7.0 fusion.58
  203.2 10.6 shard_map.205
  213.8 10.5 shard_map.208
  224.3 32.0 %collective-permute-done.1 = bf16[640,2048]{1,0:T(8,128)(2,1)} collective-permute-done((bf16[640,2048]{1,0:T(8,128)(2,1)}, bf16[640,2048]{1,0:T(8,128)(2,1)}, u32[]{:S(2)}, u32[]{:S(2)}) %collective-permute-start.1) | collective-permute-done | bytes 2621472 | tf_op jit(solution)/shard_map/ppermute | solution.py:109
  264.5 10.3 shard_map.207
  279.0 11.6 %fusion.10 = f32[640,2688]{1,0:T(8,128)S(1)} fusion(bf16[640,2048]{1,0:T(8,128)(2,1)} %multiply_convert_fusion.in_ref, bf16[2048,4032]{0,1:T(8,128)(2,1)} %all-gather.8.cloned.1.call-done), kind=kOutput, calls=%fused_computation.20 | convolution fusion | flops 7046430720 | bytes 20512768 | tf_op jit(solution)/shard_map/dot_general | solution.py:19
  290.6 9.6 fusion.45
  300.2 78.5 %all-gather.6.cloned.1.call-done = bf16[2048,4224]{0,1:T(8,128)(2,1)} async-done(((bf16[128,4224]{0,1:T(8,128)(2,1)}), bf16[2048,4224]{0,1:T(8,128)(2,1)}) %all-gather.6.cloned.1.call-update) | async-done | bytes 17301520 | tf_op jit(solution)/shard_map/all_gather | solution.py:207
  378.7 14.8 %fusion.6 = f32[640,2816]{1,0:T(8,128)} fusion(bf16[640,2048]{1,0:T(8,128)(2,1)} %multiply_convert_fusion.in_ref, bf16[2048,4224]{0,1:T(8,128)(2,1)} %all-gather.6.cloned.1.call-done), kind=kOutput, calls=%fused_computation.16 | convolution fusion | flops 7381975040 | bytes 21364736 | tf_op jit(solution)/shard_map/dot_general | solution.py:19
  393.5 9.4 fusion.49
  402.9 9.9 fusion.4
  412.8 12.9 %add_convert_fusion.6 = bf16[640,2048]{1,0:T(8,128)(2,1)} fusion(f32[640,2048]{1,0:T(8,128)S(1)} %fusion.4, bf16[2048,4032]{0,1:T(8,128)(2,1)} %all-gather.8.cloned.1.call-done, bf16[640,1344]{1,0:T(8,128)(2,1)} %get-tuple-element.70, bf16[640,1344]{1,0:T(8,128)(2,1)} %get-tuple-element.69), kind=kOutput, calls=%fused_computation.51 | convolution fusion | flops 7055933440 | bytes 22478848 | tf_op jit(solution)/shard_map/dot_general | solution.py:23
  427.1 6.4 convolution_convert_fusion.3
  433.5 6.9 convolution_convert_fusion.4
  440.4 12.4 %convolution_convert_fusion = bf16[2048,2688]{0,1:T(8,128)(2,1)} fusion(bf16[640,2048]{1,0:T(8,128)(2,1)S(1)} %copy-done.21, bf16[640,1344]{1,0:T(8,128)(2,1)S(1)} %copy-done.46, bf16[640,1344]{1,0:T(8,128)(2,1)S(1)} %copy-done.45), kind=kOutput, calls=%fused_computation.7 | convolution fusion | flops 7058817024 | bytes 17072128 | tf_op jit(solution)/shard_map/dot_general | solution.py:27
  452.8 7.7 pad_maximum_fusion.1
  460.5 11.5 %convolution_convert_fusion.1 = bf16[2048,2816]{1,0:T(8,128)(2,1)S(1)} fusion(bf16[640,2048]{1,0:T(8,128)(2,1)} %shard_map.207, bf16[640,1408]{1,0:T(8,128)(2,1)} %get-tuple-element.68, bf16[640,1408]{1,0:T(8,128)(2,1)S(1)} %copy-done.48), kind=kOutput, calls=%fused_computation.8 | convolution fusion | flops 7394951168 | bytes 17760256 | tf_op jit(solution)/shard_map/dot_general | solution.py:27
  472.1 7.0 pad_maximum_fusion
  480.2 4.9 collective-permute-done.3
  489.3 5.4 fusion.103.in_ref
  494.7 10.6 shard_map.206
  505.3 6.1 fusion.63.da_ref
  511.5 38.5 %shard_map.204 = (bf16[640,1024]{1,0:T(8,128)(2,1)}, f32[704,1024]{1,0:T(8,128)}, f32[704,1024]{1,0:T(8,128)}) custom-call(bf16[640,1024]{1,0:T(8,128)(2,1)} %slice.402.q_ref, bf16[704,1024]{1,0:T(8,128)(2,1)} %get-tuple-element.76.k_ref, bf16[704,1024]{1,0:T(8,128)(2,1)} %get-tuple-element.75.v_ref, f32[640,128]{1,0:T(8,128)} %fusion.76.bias_ref, ...), custom_call_target="tpu_custom_call" | custom-call | flops 838860800 | bytes 13107200 | tf_op jit(solution)/shard_map/pallas_call | solution.py:179
  562.9 13.0 %fusion.55 = bf16[640,2048]{1,0:T(8,128)(2,1)S(1)} fusion(bf16[2048,4096]{0,1:T(8,128)(2,1)} %all-gather.4.cloned.1.call-done, bf16[64,1024]{1,0:T(8,128)(2,1)S(1)} %get-tuple-element.87, bf16[576,1024]{1,0:T(8,128)(2,1)S(1)} %slice.427, bf16[64,1024]{1,0:T(8,128)(2,1)S(1)} %get-tuple-element.86, bf16[576,1024]{1,0:T(8,128)(2,1)S(1)} %slice.423, ...), kind=kOutput, calls=%fused_computation.94 | convolution fusion | flops 8074035200 | bytes 19136512 | tf_op jit(solution)/shard_map/dot_general | solution.py:23
  577.4 14.9 %convolution_convert_fusion.2 = bf16[2048,3072]{1,0:T(8,128)(2,1)} fusion(bf16[640,2048]{1,0:T(8,128)(2,1)S(1)} %copy-done.19, bf16[64,1024]{1,0:T(8,128)(2,1)S(1)} %get-tuple-element.87, bf16[576,1024]{1,0:T(8,128)(2,1)} %copy-done.25, bf16[64,1024]{1,0:T(8,128)(2,1)S(1)} %get-tuple-element.86, bf16[576,1024]{1,0:T(8,128)(2,1)S(1)} %slice.423, ...), kind=kOutput, calls=%fused_computation.9 | convolution fusion | flops 8079015936 | bytes 19136512 | tf_op jit(solution)/shard_map/dot_general | solution.py:27
  592.3 6.0 slice.438
  598.4 8.9 fusion.28
  607.3 27.7 %collective-permute-done.5 = bf16[640,2048]{1,0:T(8,128)(2,1)S(1)} collective-permute-done((bf16[640,2048]{1,0:T(8,128)(2,1)S(1)}, bf16[640,2048]{1,0:T(8,128)(2,1)S(1)}, u32[]{:S(2)}, u32[]{:S(2)}) %collective-permute-start.5) | collective-permute-done | bytes 2621472 | tf_op jit(solution)/shard_map/ppermute | solution.py:109
  642.3 8.7 add_convert_fusion.8
  650.9 15.2 %collective-permute-done.7 = f32[4,2,128]{2,1,0:T(2,128)S(1)} collective-permute-done((f32[4,2,128]{2,1,0:T(2,128)S(1)}, f32[4,2,128]{2,1,0:T(2,128)S(1)}, u32[]{:S(2)}, u32[]{:S(2)}) %collective-permute-start.7) | collective-permute-done | bytes 4128 | tf_op jit(solution)/shard_map/ppermute | solution.py:93
  673.1 5.1 collective-permute-done.18
  678.4 6.1 add_convert_fusion.1
  690.3 10.0 add_convert_fusion.2
  705.3 6.8 add_convert_fusion
  717.3 12.4 %collective-permute-done.2 = bf16[640,2048]{1,0:T(8,128)(2,1)} collective-permute-done((bf16[640,2048]{1,0:T(8,128)(2,1)}, bf16[640,2048]{1,0:T(8,128)(2,1)}, u32[]{:S(2)}, u32[]{:S(2)}) %collective-permute-start.2) | collective-permute-done | bytes 2621472 | tf_op jit(solution)/shard_map/ppermute | solution.py:109
  731.1 11.5 %fusion.23 = (bf16[640,2048]{1,0:T(8,128)(2,1)}, bf16[640,2048]{1,0:T(8,128)(2,1)}) fusion(bf16[640,2048]{1,0:T(8,128)(2,1)S(1)} %copy-done.2, bf16[640,2048]{1,0:T(8,128)(2,1)} %copy-done.11, bf16[640,2048]{1,0:T(8,128)(2,1)} %copy-done.10, f32[640]{0:T(1024)S(1)} %broadcast_multiply_fusion, f32[2048]{0:T(1024)S(1)} %bitcast.80, f32[640]{0:T(1024)S(1)} %copy-done.33, ...), kind=kLoop, calls=%fused_computation.43 | loop fusion | flops 34078720 | bytes 31483904 | tf_op jit(solution)/shard_map/convert_element_type | solution.py:323
  753.0 96.1 %collective-permute-done.12 = bf16[512,3072]{1,0:T(8,128)(2,1)} collective-permute-done((bf16[512,3072]{1,0:T(8,128)(2,1)}, bf16[512,3072]{1,0:T(8,128)(2,1)}, u32[]{:S(2)}, u32[]{:S(2)}) %collective-permute-start.12) | collective-permute-done | bytes 3145760 | tf_op jit(solution)/shard_map/ppermute | solution.py:93
  864.2 75.4 %collective-permute-done.22 = bf16[512,4224]{1,0:T(8,128)(2,1)} collective-permute-done((bf16[512,4224]{1,0:T(8,128)(2,1)}, bf16[512,4224]{1,0:T(8,128)(2,1)}, u32[]{:S(2)}, u32[]{:S(2)}) %collective-permute-start.22) | collective-permute-done | bytes 4325408 | tf_op jit(solution)/shard_map/ppermute | solution.py:93
  950.1 38.5 %collective-permute-done.14 = bf16[128,3072]{1,0:T(8,128)(2,1)S(1)} collective-permute-done((bf16[128,3072]{1,0:T(8,128)(2,1)S(1)}, bf16[128,3072]{1,0:T(8,128)(2,1)S(1)}, u32[]{:S(2)}, u32[]{:S(2)}) %collective-permute-start.14) | collective-permute-done | bytes 786464 | tf_op jit(solution)/shard_map/ppermute | solution.py:97
  991.7 19.0 %collective-permute-done.29 = bf16[128,4032]{0,1:T(8,128)(2,1)S(1)} collective-permute-done((bf16[128,4032]{0,1:T(8,128)(2,1)S(1)}, bf16[128,4032]{0,1:T(8,128)(2,1)S(1)}, u32[]{:S(2)}, u32[]{:S(2)}) %collective-permute-start.29) | collective-permute-done | bytes 1032224 | tf_op jit(solution)/shard_map/ppermute | solution.py:97
  1011.1 16.5 %collective-permute-done.15 = bf16[128,3072]{1,0:T(8,128)(2,1)S(1)} collective-permute-done((bf16[128,3072]{1,0:T(8,128)(2,1)S(1)}, bf16[128,3072]{1,0:T(8,128)(2,1)S(1)}, u32[]{:S(2)}, u32[]{:S(2)}) %collective-permute-start.15) | collective-permute-done | bytes 786464 | tf_op jit(solution)/shard_map/ppermute | solution.py:97
  1029.0 21.8 %collective-permute-done.24 = bf16[128,4224]{1,0:T(8,128)(2,1)S(1)} collective-permute-done((bf16[128,4224]{1,0:T(8,128)(2,1)S(1)}, bf16[128,4224]{1,0:T(8,128)(2,1)S(1)}, u32[]{:S(2)}, u32[]{:S(2)}) %collective-permute-start.24) | collective-permute-done | bytes 1081376 | tf_op jit(solution)/shard_map/ppermute | solution.py:97
  1052.1 20.8 %collective-permute-done.30 = bf16[128,4032]{0,1:T(8,128)(2,1)S(1)} collective-permute-done((bf16[128,4032]{0,1:T(8,128)(2,1)S(1)}, bf16[128,4032]{0,1:T(8,128)(2,1)S(1)}, u32[]{:S(2)}, u32[]{:S(2)}) %collective-permute-start.30) | collective-permute-done | bytes 1032224 | tf_op jit(solution)/shard_map/ppermute | solution.py:97
  1074.9 18.1 %collective-permute-done.25 = bf16[128,4224]{1,0:T(8,128)(2,1)} collective-permute-done((bf16[128,4224]{1,0:T(8,128)(2,1)}, bf16[128,4224]{1,0:T(8,128)(2,1)}, u32[]{:S(2)}, u32[]{:S(2)}) %collective-permute-start.25) | collective-permute-done | bytes 1081376 | tf_op jit(solution)/shard_map/ppermute | solution.py:97
  (276 shorter events, 148.0 us)
Async XLA Ops:
  7.2 139.2 %all-gather.4.cloned.1.call-start = ((), (), s32[]{:S(2)}) async-start(), calls=%async_computation | async-start | bytes 17825792 | tf_op jit(solution)/shard_map/all_gather | solution.py:207
  13.1 265.9 %all-gather.8.cloned.1.call-start = ((), (), s32[]{:S(2)}) async-start(), calls=%async_computation.2 | async-start | bytes 17547264 | tf_op jit(solution)/shard_map/all_gather | solution.py:207
  19.0 359.7 %all-gather.6.cloned.1.call-start = ((), (), s32[]{:S(2)}) async-start(), calls=%async_computation.1 | async-start | bytes 18382848 | tf_op jit(solution)/shard_map/all_gather | solution.py:207
  50.1 210.1 %copy-start.26 = (f32[2048,1]{0,1:T(1,128)}, f32[2048,1]{0,1:T(1,128)S(1)}, u32[]{:S(2)}) copy-start(f32[2048,1]{0,1:T(1,128)S(1)} %get-tuple-element.88) | copy-start | bytes 24580
  158.5 5.5 collective-permute-start
  201.2 55.1 %collective-permute-start.1 = (bf16[640,2048]{1,0:T(8,128)(2,1)}, bf16[640,2048]{1,0:T(8,128)(2,1)}, u32[]{:S(2)}, u32[]{:S(2)}) collective-permute-start(bf16[640,2048]{1,0:T(8,128)(2,1)} %fusion.58), channel_id=1, source_target_pairs={{0,1},{1,0},{2,3},{3,2},{4,5},{5,4},{6,7},{7,6},{8,9},{9,8},{10,11... | collective-permute-start | bytes 7864328 | tf_op jit(solution)/shard_map/ppermute | solution.py:109
  425.7 59.4 %collective-permute-start.3 = (bf16[640,2048]{1,0:T(8,128)(2,1)}, bf16[640,2048]{1,0:T(8,128)(2,1)}, u32[]{:S(2)}, u32[]{:S(2)}) collective-permute-start(bf16[640,2048]{1,0:T(8,128)(2,1)} %add_convert_fusion.6), channel_id=1, source_target_pairs={{0,1},{1,0},{2,3},{3,2},{4,5},{5,4},{6,7},{7,6},{8,9},{9,8},{10,11... | collective-permute-start | bytes 7864328 | tf_op jit(solution)/shard_map/ppermute | solution.py:109
  452.8 32.3 %slice-start = ((s8[5242880]{0:T(1024)(128)(4,1)}), s8[1048576]{0:T(1024)(128)(4,1)S(1)}, s32[]{:S(2)}) async-start(s8[5242880]{0:T(1024)(128)(4,1)} %bitcast.66), calls=%async_computation.3 | async-start | bytes 2097152
  460.5 217.8 %collective-permute-start.26 = (bf16[1024,4032]{0,1:T(8,128)(2,1)}, bf16[1024,4032]{0,1:T(8,128)(2,1)}, u32[]{:S(2)}, u32[]{:S(2)}) collective-permute-start(bf16[1024,4032]{0,1:T(8,128)(2,1)} %pad_maximum_fusion.1), channel_id=1, source_target_pairs={{0,2},{2,0},{4,6},{6,4},{8,10},{10,8},{12,14},{14,12},{16,18},{18,... | collective-permute-start | bytes 24772616 | tf_op jit(solution)/shard_map/ppermute | solution.py:90
  479.6 224.7 %collective-permute-start.21 = (bf16[1024,4224]{1,0:T(8,128)(2,1)}, bf16[1024,4224]{1,0:T(8,128)(2,1)}, u32[]{:S(2)}, u32[]{:S(2)}) collective-permute-start(bf16[1024,4224]{1,0:T(8,128)(2,1)} %pad_maximum_fusion), channel_id=1, source_target_pairs={{0,2},{2,0},{4,6},{6,4},{8,10},{10,8},{12,14},{14,12},{16,18},{18,... | collective-permute-start | bytes 25952264 | tf_op jit(solution)/shard_map/ppermute | solution.py:90
  552.9 8.9 collective-permute-start.4
  560.7 76.5 %collective-permute-start.16 = (bf16[1024,1024]{1,0:T(8,128)(2,1)}, bf16[1024,1024]{1,0:T(8,128)(2,1)}, u32[]{:S(2)}, u32[]{:S(2)}) collective-permute-start(bf16[1024,1024]{1,0:T(8,128)(2,1)} %slice.449), channel_id=1, source_target_pairs={{0,2},{2,0},{4,6},{6,4},{8,10},{10,8},{12,14},{14,12},{16,18},{18,... | collective-permute-start | bytes 6291464 | tf_op jit(solution)/shard_map/ppermute | solution.py:90
  576.0 59.0 %copy-start.10 = (bf16[640,2048]{1,0:T(8,128)(2,1)}, bf16[640,2048]{1,0:T(8,128)(2,1)S(1)}, u32[]{:S(2)}) copy-start(bf16[640,2048]{1,0:T(8,128)(2,1)S(1)} %fusion.55) | copy-start | bytes 7864324
  576.0 59.0 %collective-permute-start.5 = (bf16[640,2048]{1,0:T(8,128)(2,1)S(1)}, bf16[640,2048]{1,0:T(8,128)(2,1)S(1)}, u32[]{:S(2)}, u32[]{:S(2)}) collective-permute-start(bf16[640,2048]{1,0:T(8,128)(2,1)S(1)} %fusion.55), channel_id=1, source_target_pairs={{0,1},{1,0},{2,3},{3,2},{4,5},{5,4},{6,7},{7,6},{8,9},{9,8},{10,11... | collective-permute-start | bytes 7864328 | tf_op jit(solution)/shard_map/ppermute | solution.py:109
  598.3 91.0 %collective-permute-start.11 = (bf16[1024,3072]{1,0:T(8,128)(2,1)}, bf16[1024,3072]{1,0:T(8,128)(2,1)}, u32[]{:S(2)}, u32[]{:S(2)}) collective-permute-start(bf16[1024,3072]{1,0:T(8,128)(2,1)} %slice.438), channel_id=1, source_target_pairs={{0,2},{2,0},{4,6},{6,4},{8,10},{10,8},{12,14},{14,12},{16,18},{18,... | collective-permute-start | bytes 18874376 | tf_op jit(solution)/shard_map/ppermute | solution.py:90
  598.3 36.7 %copy-start.2 = (bf16[640,2048]{1,0:T(8,128)(2,1)S(1)}, bf16[640,2048]{1,0:T(8,128)(2,1)}, u32[]{:S(2)}) copy-start(bf16[640,2048]{1,0:T(8,128)(2,1)} %param.12) | copy-start | bytes 7864324
  598.3 36.7 %copy-start.29 = (f32[2048,1]{0,1:T(1,128)S(1)}, f32[2048,1]{0,1:T(1,128)}, u32[]{:S(2)}) copy-start(f32[2048,1]{0,1:T(1,128)} %copy-done.28) | copy-start | bytes 24580
  598.4 36.7 %copy-start.33 = (f32[640]{0:T(1024)S(1)}, f32[640]{0:T(1024)}, u32[]{:S(2)}) copy-start(f32[640]{0:T(1024)} %copy-done.32) | copy-start | bytes 7684
  637.1 4.4 collective-permute-start.6
  640.0 28.0 %collective-permute-start.17 = (bf16[512,1024]{1,0:T(8,128)(2,1)S(1)}, bf16[512,1024]{1,0:T(8,128)(2,1)S(1)}, u32[]{:S(2)}, u32[]{:S(2)}) collective-permute-start(bf16[512,1024]{1,0:T(8,128)(2,1)S(1)} %slice.451), channel_id=1, source_target_pairs={{0,4},{2,6},{4,0},{6,2},{8,12},{10,14},{12,8},{14,10},{16,20},{18,... | collective-permute-start | bytes 3145736 | tf_op jit(solution)/shard_map/ppermute | solution.py:93
  641.5 36.8 %slice-start.4 = ((s8[11010048]{0:T(1024)(128)(4,1)}), s8[4194304]{0:T(1024)(128)(4,1)S(1)}, s32[]{:S(2)}) async-start(s8[11010048]{0:T(1024)(128)(4,1)} %bitcast.70), calls=%async_computation.7 | async-start | bytes 8388608
  641.6 36.8 %slice-start.5 = ((s8[11010048]{0:T(1024)(128)(4,1)}), s8[4194304]{0:T(1024)(128)(4,1)S(1)}, s32[]{:S(2)}) async-start(s8[11010048]{0:T(1024)(128)(4,1)} %bitcast.70), calls=%async_computation.8 | async-start | bytes 8388608
  641.6 36.8 %slice-start.6 = ((s8[11010048]{0:T(1024)(128)(4,1)}), s8[2621440]{0:T(1024)(128)(4,1)S(1)}, s32[]{:S(2)}) async-start(s8[11010048]{0:T(1024)(128)(4,1)} %bitcast.70), calls=%async_computation.9 | async-start | bytes 5242880
  641.6 24.6 %collective-permute-start.7 = (f32[4,2,128]{2,1,0:T(2,128)S(1)}, f32[4,2,128]{2,1,0:T(2,128)S(1)}, u32[]{:S(2)}, u32[]{:S(2)}) collective-permute-start(f32[4,2,128]{2,1,0:T(2,128)S(1)} %slice.432), channel_id=1, source_target_pairs={{0,4},{2,6},{4,0},{6,2},{8,12},{10,14},{12,8},{14,10},{16,20},{18,... | collective-permute-start | bytes 12296 | tf_op jit(solution)/shard_map/ppermute | solution.py:93
  666.2 5.6 collective-permute-start.8
  668.5 9.8 collective-permute-start.18
  671.7 58.0 %collective-permute-start.2 = (bf16[640,2048]{1,0:T(8,128)(2,1)}, bf16[640,2048]{1,0:T(8,128)(2,1)}, u32[]{:S(2)}, u32[]{:S(2)}) collective-permute-start(bf16[640,2048]{1,0:T(8,128)(2,1)} %add_convert_fusion.8), channel_id=1, source_target_pairs={{0,1},{1,0},{2,3},{3,2},{4,5},{5,4},{6,7},{7,6},{8,9},{9,8},{10,11... | collective-permute-start | bytes 7864328 | tf_op jit(solution)/shard_map/ppermute | solution.py:109
  678.2 64.4 %collective-permute-start.9 = (f32[1,2,128]{2,1,0:T(2,128)S(1)}, f32[1,2,128]{2,1,0:T(2,128)S(1)}, u32[]{:S(2)}, u32[]{:S(2)}) collective-permute-start(f32[1,2,128]{2,1,0:T(2,128)S(1)} %slice_add_fusion.4), channel_id=1, source_target_pairs={{0,8},{2,10},{4,12},{6,14},{8,16},{10,18},{12,20},{14,22},{16,24},... | collective-permute-start | bytes 3080 | tf_op jit(solution)/shard_map/ppermute | solution.py:97
  678.3 64.4 %collective-permute-start.19 = (bf16[128,1024]{1,0:T(8,128)(2,1)S(1)}, bf16[128,1024]{1,0:T(8,128)(2,1)}, u32[]{:S(2)}, u32[]{:S(2)}) collective-permute-start(bf16[128,1024]{1,0:T(8,128)(2,1)S(1)} %add_convert_fusion.18), channel_id=1, source_target_pairs={{0,8},{2,10},{4,12},{6,14},{8,16},{10,18},{12,20},{14,22},{16,24},... | collective-permute-start | bytes 786440 | tf_op jit(solution)/shard_map/ppermute | solution.py:97
  689.3 166.7 %collective-permute-start.27 = (bf16[512,4032]{0,1:T(8,128)(2,1)}, bf16[512,4032]{0,1:T(8,128)(2,1)}, u32[]{:S(2)}, u32[]{:S(2)}) collective-permute-start(bf16[512,4032]{0,1:T(8,128)(2,1)} %slice.468), channel_id=1, source_target_pairs={{0,4},{2,6},{4,0},{6,2},{8,12},{10,14},{12,8},{14,10},{16,20},{18,... | collective-permute-start | bytes 12386312 | tf_op jit(solution)/shard_map/ppermute | solution.py:93
  700.3 30.8 %slice-start.2 = ((s8[5242880]{0:T(1024)(128)(4,1)}), s8[4194304]{0:T(1024)(128)(4,1)S(1)}, s32[]{:S(2)}) async-start(s8[5242880]{0:T(1024)(128)(4,1)} %bitcast.68), calls=%async_computation.5 | async-start | bytes 8388608
  704.3 144.8 %collective-permute-start.12 = (bf16[512,3072]{1,0:T(8,128)(2,1)}, bf16[512,3072]{1,0:T(8,128)(2,1)}, u32[]{:S(2)}, u32[]{:S(2)}) collective-permute-start(bf16[512,3072]{1,0:T(8,128)(2,1)} %slice.440), channel_id=1, source_target_pairs={{0,4},{2,6},{4,0},{6,2},{8,12},{10,14},{12,8},{14,10},{16,20},{18,... | collective-permute-start | bytes 9437192 | tf_op jit(solution)/shard_map/ppermute | solution.py:93
  729.7 209.9 %collective-permute-start.22 = (bf16[512,4224]{1,0:T(8,128)(2,1)}, bf16[512,4224]{1,0:T(8,128)(2,1)}, u32[]{:S(2)}, u32[]{:S(2)}) collective-permute-start(bf16[512,4224]{1,0:T(8,128)(2,1)} %slice.459), channel_id=1, source_target_pairs={{0,4},{2,6},{4,0},{6,2},{8,12},{10,14},{12,8},{14,10},{16,20},{18,... | collective-permute-start | bytes 12976136 | tf_op jit(solution)/shard_map/ppermute | solution.py:93
  742.7 5.5 collective-permute-start.10
  743.8 8.2 collective-permute-start.20
  849.1 90.5 %slice-start.7 = ((s8[8650752]{0:T(1024)(128)(4,1)}), s8[4194304]{0:T(1024)(128)(4,1)S(1)}, s32[]{:S(2)}) async-start(s8[8650752]{0:T(1024)(128)(4,1)} %bitcast.72), calls=%async_computation.10 | async-start | bytes 8388608
  849.1 90.5 %slice-start.8 = ((s8[8650752]{0:T(1024)(128)(4,1)}), s8[4194304]{0:T(1024)(128)(4,1)S(1)}, s32[]{:S(2)}) async-start(s8[8650752]{0:T(1024)(128)(4,1)} %bitcast.72), calls=%async_computation.11 | async-start | bytes 8388608
  854.2 85.4 %slice-start.9 = ((s8[8650752]{0:T(1024)(128)(4,1)}), s8[262144]{0:T(1024)(128)(4,1)S(1)}, s32[]{:S(2)}) async-start(s8[8650752]{0:T(1024)(128)(4,1)} %bitcast.72), calls=%async_computation.12 | async-start | bytes 524288
  854.2 90.1 %collective-permute-start.13 = (bf16[128,3072]{1,0:T(8,128)(2,1)}, bf16[128,3072]{1,0:T(8,128)(2,1)}, u32[]{:S(2)}, u32[]{:S(2)}) collective-permute-start(bf16[128,3072]{1,0:T(8,128)(2,1)} %slice.444), channel_id=1, source_target_pairs={{0,8},{2,10},{4,12},{6,14},{8,16},{10,18},{12,20},{14,22},{16,24},... | collective-permute-start | bytes 2359304 | tf_op jit(solution)/shard_map/ppermute | solution.py:97
  860.7 88.2 %collective-permute-start.28 = (bf16[128,4032]{0,1:T(8,128)(2,1)S(1)}, bf16[128,4032]{0,1:T(8,128)(2,1)S(1)}, u32[]{:S(2)}, u32[]{:S(2)}) collective-permute-start(bf16[128,4032]{0,1:T(8,128)(2,1)S(1)} %slice.472), channel_id=1, source_target_pairs={{0,8},{2,10},{4,12},{6,14},{8,16},{10,18},{12,20},{14,22},{16,24},... | collective-permute-start | bytes 3096584 | tf_op jit(solution)/shard_map/ppermute | solution.py:97
  943.0 107.7 %copy-start.9 = (bf16[512,4224]{1,0:T(8,128)(2,1)}, bf16[512,4224]{1,0:T(8,128)(2,1)S(1)}, u32[]{:S(2)}) copy-start(bf16[512,4224]{1,0:T(8,128)(2,1)S(1)} %add_convert_fusion.3) | copy-start | bytes 12976132
  943.1 45.8 %collective-permute-start.23 = (bf16[128,4224]{1,0:T(8,128)(2,1)S(1)}, bf16[128,4224]{1,0:T(8,128)(2,1)S(1)}, u32[]{:S(2)}, u32[]{:S(2)}) collective-permute-start(bf16[128,4224]{1,0:T(8,128)(2,1)S(1)} %slice.463), channel_id=1, source_target_pairs={{0,8},{2,10},{4,12},{6,14},{8,16},{10,18},{12,20},{14,22},{16,24},... | collective-permute-start | bytes 3244040 | tf_op jit(solution)/shard_map/ppermute | solution.py:97
  945.8 42.8 %collective-permute-start.14 = (bf16[128,3072]{1,0:T(8,128)(2,1)S(1)}, bf16[128,3072]{1,0:T(8,128)(2,1)S(1)}, u32[]{:S(2)}, u32[]{:S(2)}) collective-permute-start(bf16[128,3072]{1,0:T(8,128)(2,1)S(1)} %add_convert_fusion.16), channel_id=1, source_target_pairs={{0,8},{2,10},{4,12},{6,14},{8,16},{10,18},{12,20},{14,22},{16,24},... | collective-permute-start | bytes 2359304 | tf_op jit(solution)/shard_map/ppermute | solution.py:97
  949.2 61.6 %collective-permute-start.29 = (bf16[128,4032]{0,1:T(8,128)(2,1)S(1)}, bf16[128,4032]{0,1:T(8,128)(2,1)S(1)}, u32[]{:S(2)}, u32[]{:S(2)}) collective-permute-start(bf16[128,4032]{0,1:T(8,128)(2,1)S(1)} %add_convert_fusion.14), channel_id=1, source_target_pairs={{0,8},{2,10},{4,12},{6,14},{8,16},{10,18},{12,20},{14,22},{16,24},... | collective-permute-start | bytes 3096584 | tf_op jit(solution)/shard_map/ppermute | solution.py:97
  988.8 38.8 %collective-permute-start.15 = (bf16[128,3072]{1,0:T(8,128)(2,1)S(1)}, bf16[128,3072]{1,0:T(8,128)(2,1)S(1)}, u32[]{:S(2)}, u32[]{:S(2)}) collective-permute-start(bf16[128,3072]{1,0:T(8,128)(2,1)S(1)} %add_convert_fusion.15), channel_id=1, source_target_pairs={{0,8},{2,10},{4,12},{6,14},{8,16},{10,18},{12,20},{14,22},{16,24},... | collective-permute-start | bytes 2359304 | tf_op jit(solution)/shard_map/ppermute | solution.py:97
  989.2 61.6 %collective-permute-start.24 = (bf16[128,4224]{1,0:T(8,128)(2,1)S(1)}, bf16[128,4224]{1,0:T(8,128)(2,1)S(1)}, u32[]{:S(2)}, u32[]{:S(2)}) collective-permute-start(bf16[128,4224]{1,0:T(8,128)(2,1)S(1)} %add_convert_fusion.11), channel_id=1, source_target_pairs={{0,8},{2,10},{4,12},{6,14},{8,16},{10,18},{12,20},{14,22},{16,24},... | collective-permute-start | bytes 3244040 | tf_op jit(solution)/shard_map/ppermute | solution.py:97
  1011.0 61.9 %collective-permute-start.30 = (bf16[128,4032]{0,1:T(8,128)(2,1)S(1)}, bf16[128,4032]{0,1:T(8,128)(2,1)S(1)}, u32[]{:S(2)}, u32[]{:S(2)}) collective-permute-start(bf16[128,4032]{0,1:T(8,128)(2,1)S(1)} %add_convert_fusion.13), channel_id=1, source_target_pairs={{0,8},{2,10},{4,12},{6,14},{8,16},{10,18},{12,20},{14,22},{16,24},... | collective-permute-start | bytes 3096584 | tf_op jit(solution)/shard_map/ppermute | solution.py:97
  1052.0 41.0 %collective-permute-start.25 = (bf16[128,4224]{1,0:T(8,128)(2,1)}, bf16[128,4224]{1,0:T(8,128)(2,1)}, u32[]{:S(2)}, u32[]{:S(2)}) collective-permute-start(bf16[128,4224]{1,0:T(8,128)(2,1)} %add_convert_fusion.10), channel_id=1, source_target_pairs={{0,8},{2,10},{4,12},{6,14},{8,16},{10,18},{12,20},{14,22},{16,24},... | collective-permute-start | bytes 3244040 | tf_op jit(solution)/shard_map/ppermute | solution.py:97
  (45 other events, 407.3 us)
Sparse Core Ops, SparseCore 0:
  13.2 133.0 all-gather.3
  148.5 130.4 all-gather.7
  281.1 97.5 all-gather.5

commit v2 on v1

v2 whole, which is shorter than its diff:
```python
import functools
import math

import jax
import jax.numpy as jnp
from jax import lax
from jax.experimental import pallas as pl
from jax.experimental.pallas import tpu as pltpu
from jax.sharding import PartitionSpec as P

HEAD_DIM = 128
WINDOW = 64
EPSILON = 1e-06
BF16 = jnp.bfloat16
F32 = jnp.float32
ANYWHERE = pl.BlockSpec(memory_space=pl.ANY)
HINT = 0.5


def cost(flops, bytes_accessed, transcendentals):
    return pl.CostEstimate(
        flops=int(HINT * flops),
        bytes_accessed=int(HINT * bytes_accessed),
        transcendentals=int(HINT * transcendentals),
    )


def mat_nn(left, right):
    return jnp.dot(left, right, preferred_element_type=F32)


def mat_nt(left, right):
    return lax.dot_general(left, right, (((1,), (1,)), ((), ())), preferred_element_type=F32)


def mat_tn(left, right):
    return lax.dot_general(left, right, (((0,), (0,)), ((), ())), preferred_element_type=F32)


def shift_pairs(count, steps):
    return [(s, s + steps) for s in range(max(0, -steps), min(count, count - steps))]


def flip_pairs(count, bit):
    return [(s, s ^ bit) for s in range(count)]


def relative_blocks(count):
    me = lax.axis_index("seq")
    place = jnp.arange(count, dtype=jnp.int32)
    outers = count // 4
    inner, middle, outer = place // (2 * outers), (place // outers) % 2, place % outers
    return (outer * 4 + ((me // 2 + middle) % 2) * 2 + (me + inner) % 2).astype(jnp.int32)


def rolled(values, steps, axis):
    return lax.dynamic_slice_in_dim(
        jnp.concatenate([values, values], axis), steps, values.shape[axis], axis
    )


def turn_blocks(pieces, order_ref, *refs):
    blocks = order_ref.shape[0] // 2
    first = 0
    for in_ref in refs[:pieces]:
        last = first + in_ref.shape[0]
        for half, out_ref in enumerate(refs[-2:]):
            for i in range(blocks):
                start = pl.multiple_of(order_ref[half * blocks + i] * 128, 128)
                out_ref[i * 128 : (i + 1) * 128, first:last] = in_ref[:, pl.ds(start, 128)].T
        first = last


def relative_turned(pieces, order, *after):
    rows, columns = sum(p.shape[0] for p in pieces), pieces[0].shape[1]
    count = order.shape[0]
    width = columns // count
    kind = pieces[0].dtype
    if width % 128:
        values = jnp.concatenate(pieces, 0)
        me, outers = lax.axis_index("seq"), count // 4
        turned = rolled(values.reshape(rows, outers, 2, 2, width), (me // 2) % 2, 2)
        turned = rolled(turned, me % 2, 3)
        return tuple(jnp.transpose(turned, (3, 2, 1, 4, 0)).reshape(2, columns // 2, rows))
    whole = pl.BlockSpec(memory_space=pltpu.VMEM)
    return pl.pallas_call(
        functools.partial(turn_blocks, len(pieces)),
        in_specs=[pl.BlockSpec(memory_space=pltpu.SMEM)] + [whole] * len(pieces) + [ANYWHERE] * len(after),
        out_specs=(whole, whole),
        out_shape=(jax.ShapeDtypeStruct((columns // 2, rows), kind),) * 2,
        cost_estimate=cost(flops=0, bytes_accessed=4 * rows * columns, transcendentals=0),
        compiler_params=pltpu.CompilerParams(vmem_limit_bytes=32 << 20),
    )(order, *pieces, *after)


def to_core(values):
    return lax.ppermute(values, "seq", flip_pairs(lax.axis_size("seq"), 1))


def to_middle(values):
    return lax.ppermute(values, "seq", flip_pairs(lax.axis_size("seq"), 2))


def sum_outer(values):
    outers = lax.axis_size("seq") // 4
    groups = [[o * 4 + place for o in range(outers)] for place in range(4)]
    return lax.psum_scatter(values, "seq", scatter_dimension=0, axis_index_groups=groups, tiled=True)


def add_block(keep_ref, got_ref, *refs):
    refs[-1][...] = (keep_ref[...].astype(F32) + got_ref[...].astype(F32)).astype(BF16)


def column_block(columns, most=1024):
    return next(w for w in range(most, 0, -128) if columns % w == 0)


def add_middle(part, after=()):
    keep, got = part[0], to_middle(part[1])
    rows, columns = keep.shape
    wide = column_block(columns)
    spec = pl.BlockSpec((rows, wide), lambda j: (0, j))
    return pl.pallas_call(
        add_block,
        grid=(columns // wide,),
        in_specs=[spec] * 2 + [ANYWHERE] * len(after),
        out_specs=spec,
        out_shape=jax.ShapeDtypeStruct((rows, columns), BF16),
        cost_estimate=cost(flops=rows * columns, bytes_accessed=6 * rows * columns, transcendentals=0),
        compiler_params=pltpu.CompilerParams(vmem_limit_bytes=32 << 20),
    )(keep, got, *after)


def sum_small(partial):
    count = lax.axis_size("seq")
    outers = count // 4
    rest = partial.shape[1:]
    partial = partial.reshape((2, 2 * outers) + rest)
    pair = partial[0] + to_core(partial[1])
    pair = pair.reshape((2, outers) + rest)
    four = pair[0] + to_middle(pair[1])
    outer = lax.axis_index("seq") // 4
    total = lax.dynamic_index_in_dim(four, outer, 0, keepdims=False)
    for step in range(1, outers):
        sent = lax.dynamic_index_in_dim(four, (outer + step) % outers, 0, keepdims=False)
        total = total + lax.ppermute(sent, "seq", [(s, (s + 4 * step) % count) for s in range(count)])
    return total


def bands(steps):
    return [
        (slice(i * WINDOW, (i + 1) * WINDOW), slice(i * WINDOW, (i + 2) * WINDOW)) for i in range(steps)
    ]


def band_probs(query, key, bias, steps):
    scale = 1.0 / math.sqrt(HEAD_DIM)
    scores = jnp.concatenate([mat_nt(query[rows], key[keys]) for rows, keys in bands(steps)], 0)
    scores = scores * scale + bias
    weights = jnp.exp(scores - jnp.max(scores, axis=1, keepdims=True))
    return weights / jnp.sum(weights, axis=1, keepdims=True)


def attend(q_ref, k_ref, v_ref, k_tail_ref, v_tail_ref, bias_ref, out_ref):
    steps = q_ref.shape[0] // WINDOW
    key = jnp.concatenate([k_tail_ref[...], k_ref[...]], 0)
    value = jnp.concatenate([v_tail_ref[...], v_ref[...]], 0)
    probs = band_probs(q_ref[...], key, bias_ref[...], steps).astype(BF16)
    for rows, keys in bands(steps):
        out_ref[rows] = mat_nn(probs[rows], value[keys]).astype(BF16)


def attend_back(heads, pieces, q_ref, k_ref, v_ref, k_tail_ref, v_tail_ref, bias_ref, *refs):
    dq_ref, dkv_ref, edge_send_ref, edge_keep_ref = refs[-4:]
    da = jnp.concatenate([r[...] for r in refs[:pieces]], 0)
    scale = 1.0 / math.sqrt(HEAD_DIM)
    head = pl.program_id(0)
    steps = q_ref.shape[0] // WINDOW
    query = q_ref[...]
    key = jnp.concatenate([k_tail_ref[...], k_ref[...]], 0)
    value = jnp.concatenate([v_tail_ref[...], v_ref[...]], 0)
    probs = band_probs(query, key, bias_ref[...], steps)
    dp = jnp.concatenate([mat_nt(da[rows], value[keys]) for rows, keys in bands(steps)], 0)
    inner = jnp.sum(probs * dp, axis=1, keepdims=True)
    ds = (probs * (dp - inner)).astype(BF16)
    probs = probs.astype(BF16)

    def place(part):
        return pl.ds(pl.multiple_of((part * heads + head) * HEAD_DIM, HEAD_DIM), HEAD_DIM)

    low = None
    for i, (rows, keys) in enumerate(bands(steps)):
        dq_ref[rows] = (mat_nn(ds[rows], key[keys]) * scale).astype(BF16)
        both = (mat_tn(ds[rows], query[rows]) * scale, mat_tn(probs[rows], da[rows]))
        for part in range(2):
            first = both[part][:WINDOW] if low is None else both[part][:WINDOW] + low[part]
            if i:
                dkv_ref[bands(steps)[i - 1][0], place(part)] = first.astype(BF16)
            else:
                edge_send_ref[:, place(part)] = first.astype(BF16)
        low = [b[WINDOW:] for b in both]
    for part in range(2):
        edge_keep_ref[:, place(part)] = low[part]


def head_spec(rows, first=0):
    return pl.BlockSpec((rows, HEAD_DIM), lambda h: (0, first + h))


def once(shape):
    return pl.BlockSpec(shape, lambda j: (0, 0), pipeline_mode=pl.Buffered(1))


def attention_specs(tokens, heads):
    return [
        head_spec(tokens),
        head_spec(tokens, heads),
        head_spec(tokens, 2 * heads),
        head_spec(WINDOW),
        head_spec(WINDOW, heads),
        once((tokens, 2 * WINDOW)),
    ]


def attention_forward(qkv, tail, bias):
    tokens, heads = qkv.shape[0], qkv.shape[1] // (3 * HEAD_DIM)
    width = heads * HEAD_DIM
    return pl.pallas_call(
        attend,
        grid=(heads,),
        in_specs=attention_specs(tokens, heads),
        out_specs=head_spec(tokens),
        out_shape=jax.ShapeDtypeStruct((tokens, width), BF16),
        cost_estimate=cost(
            flops=8 * tokens * width * WINDOW, bytes_accessed=8 * tokens * width, transcendentals=tokens * width
        ),
        compiler_params=pltpu.CompilerParams(vmem_limit_bytes=32 << 20),
    )(qkv, qkv, qkv, tail, tail, bias)


def attention_backward(qkv, tail, bias, da, *after):
    tokens, heads = qkv.shape[0], qkv.shape[1] // (3 * HEAD_DIM)
    width = heads * HEAD_DIM
    return pl.pallas_call(
        functools.partial(attend_back, heads, len(da)),
        grid=(heads,),
        in_specs=attention_specs(tokens, heads)
        + [head_spec(d.shape[0]) for d in da]
        + [ANYWHERE] * len(after),
        out_specs=(
            head_spec(tokens),
            once((tokens, 2 * width)),
            once((WINDOW, 2 * width)),
            once((WINDOW, 2 * width)),
        ),
        out_shape=(
            jax.ShapeDtypeStruct((tokens, width), BF16),
            jax.ShapeDtypeStruct((tokens, 2 * width), BF16),
            jax.ShapeDtypeStruct((WINDOW, 2 * width), BF16),
            jax.ShapeDtypeStruct((WINDOW, 2 * width), F32),
        ),
        cost_estimate=cost(
            flops=20 * tokens * width * WINDOW, bytes_accessed=14 * tokens * width, transcendentals=tokens * width
        ),
        compiler_params=pltpu.CompilerParams(vmem_limit_bytes=40 << 20),
    )(qkv, qkv, qkv, tail, tail, bias, *da, *after)


def multiply(turned, pieces, *refs):
    w_ref = refs[pieces]
    total, first = None, 0
    for x_ref in refs[:pieces]:
        last = first + x_ref.shape[1]
        term = mat_nt(x_ref[...], w_ref[:, first:last]) if turned else mat_nn(x_ref[...], w_ref[...])
        total = term if total is None else total + term
        first = last
    refs[-1][...] = total.astype(BF16)


def rows_times(pieces, weights, columns, first=0, turned=False, wide=512, after=()):
    tokens, d = pieces[0].shape[0], sum(p.shape[1] for p in pieces)
    if turned:
        out = weights.shape[0]
        spec = pl.BlockSpec((wide, columns), lambda j: (j, first // columns))
    else:
        out = columns
        spec = pl.BlockSpec((d, wide), lambda j: (0, first // wide + j))
    return pl.pallas_call(
        functools.partial(multiply, turned, len(pieces)),
        grid=(out // wide,),
        in_specs=[once(p.shape) for p in pieces] + [spec] + [ANYWHERE] * len(after),
        out_specs=pl.BlockSpec((tokens, wide), lambda j: (0, j)),
        out_shape=jax.ShapeDtypeStruct((tokens, out), BF16),
        cost_estimate=cost(
            flops=2 * tokens * d * out, bytes_accessed=2 * (tokens * (d + out) + d * out), transcendentals=0
        ),
        compiler_params=pltpu.CompilerParams(vmem_limit_bytes=48 << 20),
    )(*pieces, weights, *after)


PARTS = ((512, 3), (640, 2))


def feed(block, steps, first_row, h_ref, dm_ref, wgu_ref, wd_ref, *refs):
    j = pl.program_id(0)
    carried = first_row is not None
    if carried:
        m_in, dh_in = refs[:2]
        wide_ref, hidden_ref, m_out, dh_out, m_sum, dh_sum = refs[-6:]
    else:
        wide_ref, hidden_ref, m_sum, dh_sum = refs[-4:]
    gate_up = mat_nn(h_ref[...], wgu_ref[...])
    gate, up = gate_up[:, :block], gate_up[:, block:]
    dhidden = mat_nn(dm_ref[...], wd_ref[...])
    sigma = jax.nn.sigmoid(gate)
    silu = gate * sigma
    hidden = (silu * up).astype(BF16)
    dup = (dhidden * silu).astype(BF16)
    dgate = (dhidden * up * (sigma * (1.0 + gate * (1.0 - sigma)))).astype(BF16)
    dgate_up = jnp.concatenate([dgate, dup], 1)
    wide_ref[...] = dgate_up
    hidden_ref[...] = hidden

    @pl.when(j == 0)
    def _():
        if carried:
            rows = pl.ds(first_row, m_sum.shape[0])
            pltpu.sync_copy(m_in.at[rows], m_sum)
            pltpu.sync_copy(dh_in.at[rows], dh_sum)
        else:
            m_sum[...] = jnp.zeros_like(m_sum)
            dh_sum[...] = jnp.zeros_like(dh_sum)

    width = 512
    for c in range(0, m_sum.shape[1], width):
        part = slice(c, c + width)
        dh_sum[:, part] += mat_nt(dgate_up, wgu_ref[part])
        m_sum[:, part] += mat_nt(hidden, wd_ref[part])

    if carried:

        @pl.when(j == steps - 1)
        def _():
            m_out[...] = m_sum[...].astype(BF16)
            dh_out[...] = dh_sum[...].astype(BF16)


def feed_forward(rows, dm, weights, part, carry=(), place=0, count=1, after=()):
    d = rows.shape[1]
    block, steps = part
    wide = steps * block
    carried = bool(carry)
    tokens = count * 128 if carried else rows.shape[0]
    row_spec = once((tokens, d))
    if carried:
        rows, dm = rows[place * 128 : place * 128 + tokens], dm[place * 128 : place * 128 + tokens]
    kind = BF16 if carried else F32
    return pl.pallas_call(
        functools.partial(feed, block, steps, place * 128 if carried else None),
        grid=(steps,),
        in_specs=[
            row_spec,
            row_spec,
            pl.BlockSpec((d, 2 * block), lambda j: (0, j)),
            pl.BlockSpec((d, block), lambda j: (0, 2 * steps + j)),
        ]
        + [ANYWHERE] * (len(carry) + len(after)),
        out_specs=(
            pl.BlockSpec((tokens, 2 * block), lambda j: (0, j)),
            pl.BlockSpec((tokens, block), lambda j: (0, j)),
            row_spec,
            row_spec,
        ),
        out_shape=(
            jax.ShapeDtypeStruct((tokens, 2 * wide), BF16),
            jax.ShapeDtypeStruct((tokens, wide), BF16),
            jax.ShapeDtypeStruct((tokens, d), kind),
            jax.ShapeDtypeStruct((tokens, d), kind),
        ),
        scratch_shapes=[pltpu.VMEM((tokens, d), F32)] * 2 if carried else [],
        cost_estimate=cost(
            flops=12 * tokens * d * wide, bytes_accessed=6 * d * wide + 24 * tokens * d, transcendentals=tokens * wide
        ),
        compiler_params=pltpu.CompilerParams(vmem_limit_bytes=60 << 20),
    )(rows, dm, weights, weights, *carry, *after)


def grad_block(pieces, outers, left_ref, left_got_ref, *refs):
    keep_ref, send_ref = refs[-2:]
    total = None
    for side, left in enumerate((left_ref, left_got_ref)):
        first = 0
        for right in refs[side * pieces : (side + 1) * pieces]:
            last = first + right.shape[0]
            term = mat_nn(left[:, first:last], right[...])
            total = term if total is None else total + term
            first = last
    total = total.astype(BF16)
    half = total.shape[0] // 2
    if not outers:
        keep_ref[...] = total[:half]
        send_ref[...] = total[half:]
        return
    block = half // outers
    for i in range(2 * outers):
        first = (i % 2) * half + (i // 2) * block
        send_ref[i * block : (i + 1) * block] = total[first : first + block]


def weight_grad(left, right, after=(), first=0, columns=None, outers=0):
    d, tokens = left[0].shape
    columns = columns or right[0][0].shape[1]
    wide = next(w for w in (640, 512, 256, 128) if columns % w == 0 and first % w == 0)
    pieces = tuple(right[0]) + tuple(right[1])
    outs = (jax.ShapeDtypeStruct((d, columns), BF16),)
    if not outers:
        outs = (jax.ShapeDtypeStruct((d // 2, columns), BF16),) * 2
    return pl.pallas_call(
        functools.partial(grad_block, len(right[0]), outers),
        grid=(columns // wide,),
        in_specs=[once((d, tokens))] * 2
        + [pl.BlockSpec((p.shape[0], wide), lambda j: (0, first // wide + j)) for p in pieces]
        + [ANYWHERE] * len(after),
        out_specs=(pl.BlockSpec((d // len(outs), wide), lambda j: (0, j)),) * len(outs),
        out_shape=outs,
        cost_estimate=cost(
            flops=4 * tokens * d * columns, bytes_accessed=2 * (d + 2 * tokens) * columns + 4 * d * tokens, transcendentals=0
        ),
        compiler_params=pltpu.CompilerParams(vmem_limit_bytes=48 << 20),
    )(*left, *pieces, *after)


def middle_back(own_ref, got_ref, middle_ref, dm_ref, gain_ref, wo_ref, *refs):
    grad_ref, low_ref, da_ref, gain_out = refs[-4:]
    rows = middle_ref[...]
    inverse = lax.rsqrt(jnp.mean(rows * rows, axis=1, keepdims=True) + EPSILON)
    unit = rows * inverse
    dh = own_ref[...].astype(F32) + got_ref[...].astype(F32)
    grad = dm_ref[...].astype(F32) + norm_back(dh, unit, inverse, gain_ref[...])
    grad_ref[...] = grad
    low = grad.astype(BF16)
    low_ref[...] = low
    da_ref[...] = mat_nn(low, wo_ref[...]).astype(BF16)
    part = jnp.sum(dh * unit, axis=0, keepdims=True)

    @pl.when(pl.program_id(0) == 0)
    def _():
        gain_out[...] = part

    @pl.when(pl.program_id(0) > 0)
    def _():
        gain_out[...] += part


def middle_gradient(own, got, middle, dm, gain, weights, width, place, after=()):
    tokens, d = own.shape

    def rows(first, n=d):
        return pl.BlockSpec((128, n), lambda i: (first + i, 0))

    return pl.pallas_call(
        middle_back,
        grid=(tokens // 128,),
        in_specs=[
            rows(0),
            rows(0),
            rows(place),
            rows(place),
            once((1, d)),
            pl.BlockSpec((d, width), lambda i: (0, 3), pipeline_mode=pl.Buffered(1)),
        ]
        + [ANYWHERE] * len(after),
        out_specs=(rows(0), rows(0), rows(0, width), once((1, d))),
        out_shape=(
            jax.ShapeDtypeStruct((tokens, d), F32),
            jax.ShapeDtypeStruct((tokens, d), BF16),
            jax.ShapeDtypeStruct((tokens, width), BF16),
            jax.ShapeDtypeStruct((1, d), F32),
        ),
        cost_estimate=cost(
            flops=2 * tokens * d * width, bytes_accessed=2 * d * width + 16 * tokens * d, transcendentals=0
        ),
        compiler_params=pltpu.CompilerParams(vmem_limit_bytes=48 << 20),
    )(own, got, middle, dm, gain, weights, *after)


def norm_back(grad_normed, unit_rows, inverse_rows, gain):
    scaled = grad_normed * gain
    return inverse_rows * (scaled - unit_rows * jnp.mean(scaled * unit_rows, axis=1, keepdims=True))


def gather(shards):
    return lax.all_gather(jnp.concatenate(shards, 1), "seq", axis=0, tiled=True)


def per_device(
    x_in, lengths, g_attn, w_query, w_key, w_value, w_out, g_ffn, w_gate, w_up, w_down, cotangent
):
    tokens = x_in.shape[0]
    width = w_query.shape[1]
    ff = w_gate.shape[1]
    count = lax.axis_size("seq")
    def rounded(shard, a=0, b=None):
        shard = shard.astype(BF16)
        b = shard.shape[1] if b is None else b
        pad = max(0, b - shard.shape[1])
        return jnp.pad(shard[:, a:b], ((0, 0), (0, pad)))

    def zeros(n):
        return jnp.zeros((w_query.shape[0], n), BF16)

    w_down_t = w_down.astype(BF16).T
    gains_here = rounded(jnp.stack([g_attn, g_ffn], 1), 0, 128)
    attn_w = gather(
        (rounded(w_query), rounded(w_key), rounded(w_value), w_out.astype(BF16).T, gains_here)
    )
    ffn_w = []
    a = 0
    for block, steps in PARTS:
        wide = [rounded(w, a + j * block, a + (j + 1) * block) for j in range(steps) for w in (w_gate, w_up)]
        wide.append(rounded(w_down_t, a, a + steps * block))
        spare = 4224 - 3 * steps * block
        ffn_w.append(gather(wide + ([zeros(spare)] if spare > 0 else [])))
        a += steps * block
    gains = attn_w[:, 4 * width : 4 * width + 2].T.astype(F32)
    gain_one, gain_two = gains[0], gains[1]

    order = relative_blocks(count)
    first_place = lax.axis_index("seq") * tokens
    row = jnp.arange(tokens, dtype=jnp.int32)[:, None]
    column = jnp.arange(2 * WINDOW, dtype=jnp.int32)[None, :]
    key_place = row // WINDOW * WINDOW + column - WINDOW
    ends = [lengths[0]]
    for i in range(1, lengths.shape[0] - 1):
        ends.append(ends[-1] + lengths[i])
    seg_row = sum(((first_place + row) >= e).astype(jnp.int32) for e in ends)
    seg_key = sum(((first_place + key_place) >= e).astype(jnp.int32) for e in ends)
    allowed = (
        (key_place <= row)
        & (key_place > row - WINDOW)
        & (first_place + key_place >= 0)
        & (seg_row == seg_key)
    )
    bias = jnp.where(allowed, 0.0, -1e30).astype(F32)

    x_full = x_in.astype(F32)
    inverse_one = lax.rsqrt(jnp.mean(x_full * x_full, axis=1, keepdims=True) + EPSILON)
    unit_one = x_full * inverse_one
    def both_halves(pieces, *after):
        own, other = relative_turned(pieces, order, *after)
        return own, to_core(other)

    def both_cores(*pieces):
        return pieces, tuple(to_core(p) for p in pieces)

    def to_mp(own):
        return lax.ppermute(own, "mp", [(0, 1), (1, 0)])

    cot_turned = both_halves((cotangent,))
    normed = (unit_one * gain_one).astype(BF16)
    normed_turned = both_halves((normed,))

    qkv = rows_times((normed,), attn_w, 3 * width)
    tail = lax.ppermute(qkv[tokens - WINDOW :, width:], "seq", shift_pairs(count, 1))
    mixed = attention_forward(qkv, tail, bias)
    mixed_both = both_cores(mixed)
    branch = rows_times((mixed,), attn_w, width, 3 * width, True)
    middle = x_full + (branch.astype(F32) + to_mp(branch).astype(F32))
    inverse_two = lax.rsqrt(jnp.mean(middle * middle, axis=1, keepdims=True) + EPSILON)
    normed_two = (middle * inverse_two * gain_two).astype(BF16)
    normed_two_turned = both_halves((normed_two,))

    after = (mixed_both[1][0], cot_turned[1], normed_turned[1])
    one, two = (block * steps for block, steps in PARTS)
    wide_acts, hidden, *carry = feed_forward(normed_two, cotangent, ffn_w[0], PARTS[0], after=after)
    wide_acts = both_cores(wide_acts)
    one_a = weight_grad(normed_two_turned, wide_acts, (), 0, one)
    one_c = weight_grad(cot_turned, both_cores(hidden), one_a, outers=count // 4)
    one_b = weight_grad(normed_two_turned, wide_acts, one_c, one, one)
    one_c = sum_outer(one_c[0])
    places = ((0, (tokens // 128 + 1) // 2), ((tokens // 128 + 1) // 2, tokens // 256))
    after = one_b
    halves = []
    for place, blocks in places:
        halves.append(feed_forward(normed_two, cotangent, ffn_w[1], PARTS[1], tuple(carry), place, blocks, after))
        if not place:
            one_a = add_middle(one_a, (halves[0][0],))
            after = (one_a,)
    wide_acts, hidden, m_halves, dh_halves = zip(*halves)
    after = (wide_acts[1],)
    wide_acts, hidden = both_cores(*wide_acts), both_cores(*hidden)
    middles = []
    for (place, _), dh in zip(places, dh_halves):
        middles.append(
            middle_gradient(dh, to_mp(dh), middle, cotangent, gain_two[None], attn_w, width, place, after)
        )
        if not place:
            one_b = add_middle(one_b, (middles[0][1], one_c))
            two_a = weight_grad(normed_two_turned, wide_acts, (one_b,), 0, two)
            after = two_a
    grad_gain_two = sum(m[3][0] for m in middles)
    two_b = weight_grad(normed_two_turned, wide_acts, (middles[1][1],), two, two)
    two_a = add_middle(two_a, two_b)
    half = one_c.shape[0] // 2
    one_c = one_c[:half].astype(F32) + to_middle(one_c[half:]).astype(F32)
    one_a, one_b = sum_outer(one_a), sum_outer(one_b)
    branch_turned = both_halves([m[1] for m in middles], two_a)
    grad_q, grad_kv, edge_send, edge_keep = attention_backward(
        qkv, tail, bias, [m[2] for m in middles], branch_turned[0]
    )
    two_c = weight_grad(cot_turned, hidden, (edge_keep,))
    two_b = add_middle(two_b, two_c)
    after = (two_b, one_a)
    two_a, two_b = sum_outer(two_a), sum_outer(two_b)
    two_c = add_middle(two_c, after)
    q_part = weight_grad(normed_turned, both_cores(grad_q), (two_c, one_b))
    out_part = weight_grad(branch_turned, mixed_both, q_part)
    two_c = sum_outer(two_c)
    late, _ = lax.optimization_barrier((m_halves, branch_turned[0]))
    late = jnp.concatenate(late, 0)
    late_got = to_mp(late)
    edge_keep, _ = lax.optimization_barrier((edge_keep, out_part[0]))
    back = lax.ppermute(edge_send, "seq", shift_pairs(count, -1))
    last_rows = (edge_keep + back.astype(F32)).astype(BF16)
    grad_kv = lax.dynamic_update_slice(grad_kv, last_rows, (tokens - WINDOW, 0))
    kv_both = both_cores(grad_kv)
    k_part = weight_grad(normed_turned, kv_both, (late_got, *out_part), 0, width)
    v_part = weight_grad(normed_turned, kv_both, k_part, width, width)
    q_part = add_middle(q_part, (*v_part, two_a))
    own = rows_times((grad_q, grad_kv), attn_w, 3 * width, 0, True, after=(q_part,))
    own_got = to_mp(own)
    out_part = add_middle(out_part, (own, two_b))
    k_part = add_middle(k_part, (out_part, two_c))
    v_part = add_middle(v_part, (k_part, own_got))
    q_sum, out_sum = sum_outer(q_part).astype(F32), sum_outer(out_part).astype(F32)
    k_sum, v_sum = sum_outer(k_part).astype(F32), sum_outer(v_part).astype(F32)
    grad_normed = own.astype(F32) + own_got.astype(F32)
    grad_gain_one = jnp.sum(own.astype(F32) * unit_one, axis=0)
    grad_gain_one = grad_gain_one + to_mp(grad_gain_one)
    grad_middle = jnp.concatenate([m[0] for m in middles], 0)
    grad_input = grad_middle + norm_back(grad_normed, unit_one, inverse_one, gain_one)
    result = middle + (late.astype(F32) + late_got.astype(F32))
    gain_parts = jnp.stack([grad_gain_one, grad_gain_two], 0)
    gain_blocks = jnp.swapaxes(gain_parts.reshape(2, count, -1), 0, 1)
    chosen = order[:, None] == jnp.arange(count, dtype=jnp.int32)[None, :]
    gain_rel = jnp.sum(jnp.where(chosen[:, :, None, None], gain_blocks[None], 0.0), axis=1)
    gain_sums = sum_small(gain_rel)

    wide_one, wide_two = jnp.concatenate([one_a, one_b], 1), jnp.concatenate([two_a, two_b], 1)

    def columns(which):
        pieces = []
        for (block, steps), wide in zip(PARTS, (wide_one, wide_two)):
            pieces += [wide[:, (2 * j + which) * block : (2 * j + which + 1) * block] for j in range(steps)]
        return jnp.concatenate(pieces, 1)[:, :ff].astype(F32)

    grad_gate, grad_up = columns(0), columns(1)
    grad_down = jnp.concatenate([one_c, two_c.astype(F32)], 1)[:, :ff].astype(F32)

    return (
        result.astype(BF16),
        grad_input.astype(BF16),
        gain_sums[0],
        q_sum,
        k_sum,
        v_sum,
        out_sum.T,
        gain_sums[1],
        grad_gate,
        grad_up,
        grad_down.T,
    )


def solution(mesh):
    placed = (
        P("seq", None),
        P(),
        P("seq"),
        P("seq", "mp"),
        P("seq", "mp"),
        P("seq", "mp"),
        P("mp", "seq"),
        P("seq"),
        P("seq", "mp"),
        P("seq", "mp"),
        P("mp", "seq"),
        P("seq", None),
    )
    return jax.shard_map(
        per_device,
        mesh=mesh,
        in_specs=placed,
        out_specs=(
            P("seq", None),
            P("seq", None),
            P("seq"),
            P("seq", "mp"),
            P("seq", "mp"),
            P("seq", "mp"),
            P("mp", "seq"),
            P("seq"),
            P("seq", "mp"),
            P("seq", "mp"),
            P("mp", "seq"),
        ),
        check_vma=False,
    )
```

time: 1120 us -> 726 us (0.65)
  waiting for transfers between devices: 589 us -> 251 us
  matrix products: 180 us -> 0 us
  Pallas kernels: 109 us -> 233 us
  other arithmetic: 110 us -> 46.6 us
  local copies, waits for them, and re-layouts: 47.6 us -> 111 us
  blocking collectives: 23.1 us -> 0 us
  starting transfers between devices: 34.2 us -> 56.1 us
    ppermute x30 -> x35, waiting for transfers between devices: 413 us -> 162 us  [the longest x6 104 us: to_mp(): return lax.ppermute(own, 'mp', [(0, 1), (1, 0)])]
    dot_general x18 -> x0, matrix products: 180 us -> none  [the longest x6 63.6 us: mat_nn(): return jnp.dot(left, right, preferred_element_type=F32)]
    pallas_call x6 -> x33, Pallas kernels: 109 us -> 233 us  [the longest x3 81.1 us: feed_forward(): pl.pallas_call(functools.partial(feed, block, steps, place * 128 if carri...]
    all_gather x3, waiting for transfers between devices: 176 us -> 81.8 us  [gather(): return lax.all_gather(jnp.concatenate(shards, 1), 'seq', axis=0, tiled=True)]
    unnamed x125 -> x253, local copies, waits for them, and re-layouts: 20.3 us -> 96 us
    convert_element_type x22 -> x10, other arithmetic: 52.5 us -> 20.9 us  [the longest x1 7.05 us: per_device(): result.astype(BF16)]
    all_gather x1 -> x0, blocking collectives: 23.1 us -> none  [per_device(): lax.all_gather(jnp.stack([g_attn, g_ffn], 1).astype(BF16), 'seq', axis=0,...]
    concatenate x9 -> x0, other arithmetic: 22.2 us -> none  [the longest x2 14.7 us: per_device(): jnp.concatenate([mat_tn(normed_two_rel, grad_gate_up).astype(BF16), mat_t...]
  transfers between devices with their start and end apart: 34 -> 49, of which waited for: 20 -> 17; matrix products, arithmetic and copies ran while one was open for 24% -> 11% of each run, Pallas kernels for 10% -> 33%
where the time goes in v2:
time: 726 us; the launch traced here: 716 us
  waiting for transfers between devices  251 us (35%)
  Pallas kernels  233 us (32%)
  local copies, waits for them, and re-layouts  111 us (15%)
  starting transfers between devices  56.1 us (8%)
  other arithmetic  46.6 us (6%)
  between operations  18.2 us (3%)
    ppermute x6, waiting for transfers between devices, to_mp(): return lax.ppermute(own, 'mp', [(0, 1), (1, 0)])  104 us
    unnamed x253, local copies, waits for them, and re-layouts  96 us
    all_gather x3, waiting for transfers between devices, gather(): return lax.all_gather(jnp.concatenate(shards, 1), 'seq', axis=0, tiled=True)  81.8 us
    pallas_call x3, Pallas kernels, feed_forward(): pl.pallas_call(functools.partial(feed, block, steps, place * 128 if carri...  81.1 us
    pallas_call x10, Pallas kernels, weight_grad(): pl.pallas_call(functools.partial(grad_block, len(right[0]), outers), grid...  68.4 us
    ppermute x11, waiting for transfers between devices, to_middle(): return lax.ppermute(values, 'seq', flip_pairs(lax.axis_size('seq'), 2))  44.4 us
    pallas_call x3, Pallas kernels, rows_times(): pl.pallas_call(functools.partial(multiply, turned, len(pieces)), grid=(ou...  33 us
    ppermute x11, starting transfers between devices, to_middle(): return lax.ppermute(values, 'seq', flip_pairs(lax.axis_size('seq'), 2))  21.4 us
  transfers between devices with their start and end apart: 49, of which 17 were waited for; matrix products, arithmetic and copies ran while one was open for 11% of the time, Pallas kernels for 33%

profile of v2, /device:TPU:0, one launch (start us, length us, event | category | flops | bytes accessed | tf_op | source)
XLA Modules:
  0.0 715.7 jit_solution(13781193513480953090)
XLA Ops:
  27.2 79.9 %all-gather.4.cloned.1.call-done.refs_1_.wo_ref.refs_2_ = bf16[2048,4224]{1,0:T(8,128)(2,1)} async-done(((bf16[128,4224]{1,0:T(8,128)(2,1)}), bf16[2048,4224]{1,0:T(8,128)(2,1)}) %all-gather.4.cloned.1.call-update) | async-done | bytes 17301520 | tf_op jit(solution)/shard_map/all_gather | solution.py:493
  110.2 13.9 %shard_map.203.q_ref.k_ref.v_ref = bf16[640,3072]{1,0:T(8,128)(2,1)} custom-call(bf16[640,2048]{1,0:T(8,128)(2,1)S(1)} %fusion.5.refs_0_, bf16[2048,4224]{1,0:T(8,128)(2,1)} %all-gather.4.cloned.1.call-done.refs_1_.wo_ref.refs_2_), custom_call_target="tpu_custom_call" | custom-call | flops 4026531840 | bytes 9568256 | tf_op jit(solution)/shard_map/pallas_call | solution.py:288
  131.2 6.5 shard_map.204.refs_0_
  139.1 6.8 shard_map.205
  149.8 7.9 %collective-permute-start.3 = (bf16[1024,640]{1,0:T(8,128)(2,1)S(1)}, bf16[1024,640]{1,0:T(8,128)(2,1)S(1)}, u32[]{:S(2)}, u32[]{:S(2)}) collective-permute-start(bf16[1024,640]{1,0:T(8,128)(2,1)S(1)} %get-tuple-element.64), channel_id=1, source_target_pairs={{0,2},{2,0},{4,6},{6,4},{8,10},{10,8},{12,14},{14,12},{16,18},{18,... | collective-permute-start | bytes 3932168 | tf_op jit(solution)/shard_map/ppermute | solution.py:97
  160.5 38.3 %collective-permute-done.1 = bf16[640,2048]{1,0:T(8,128)(2,1)} collective-permute-done((bf16[640,2048]{1,0:T(8,128)(2,1)}, bf16[640,2048]{1,0:T(8,128)(2,1)}, u32[]{:S(2)}, u32[]{:S(2)}) %collective-permute-start.1) | collective-permute-done | bytes 2621472 | tf_op jit(solution)/shard_map/ppermute | solution.py:557
  198.8 4.7 multiply_reduce_fusion
  208.7 37.1 %shard_map.208 = (bf16[640,3072]{1,0:T(8,128)(2,1)}, bf16[640,1536]{1,0:T(8,128)(2,1)}, f32[640,2048]{1,0:T(8,128)}, f32[640,2048]{1,0:T(8,128)}) custom-call(bf16[640,2048]{1,0:T(8,128)(2,1)} %multiply_convert_fusion.h_ref.refs_0_, bf16[640,2048]{1,0:T(8,128)(2,1)} %dm_ref.5, bf16[2048,4608]{1,0:T(8,128)(2,1)} %all-gather.8.cloned.1.call-done.wgu_ref.wd_ref, ...), custom_call_target="tpu_custom_call" | custom-call | flops 12079595520 | bytes 25165824 | tf_op jit(solution)/shard_map/pallas_call | solution.py:358
  245.8 7.3 %collective-permute-start.6 = (bf16[640,3072]{1,0:T(8,128)(2,1)}, bf16[640,3072]{1,0:T(8,128)(2,1)S(1)}, u32[]{:S(2)}, u32[]{:S(2)}) collective-permute-start(bf16[640,3072]{1,0:T(8,128)(2,1)} %get-tuple-element.70.refs_0_), channel_id=1, source_target_pairs={{0,2},{2,0},{4,6},{6,4},{8,10},{10,8},{12,14},{14,12},{16,18},{18,... | collective-permute-start | bytes 11796488 | tf_op jit(solution)/shard_map/ppermute | solution.py:97
  255.0 9.9 %collective-permute-done.5.left_got_ref = bf16[1024,640]{1,0:T(8,128)(2,1)S(1)} collective-permute-done((bf16[1024,640]{1,0:T(8,128)(2,1)S(1)}, bf16[1024,640]{1,0:T(8,128)(2,1)S(1)}, u32[]{:S(2)}, u32[]{:S(2)}) %collective-permute-start.5) | collective-permute-done | bytes 1310752 | tf_op jit(solution)/shard_map/ppermute | solution.py:97
  267.9 7.0 shard_map.210
  275.0 7.7 %shard_map.211.refs_2_ = bf16[1024,1536]{1,0:T(8,128)(2,1)} custom-call(bf16[1024,640]{1,0:T(8,128)(2,1)S(1)} %copy-done.44, bf16[1024,640]{1,0:T(8,128)(2,1)S(1)} %copy-done.20, bf16[640,1536]{1,0:T(8,128)(2,1)} %get-tuple-element.72.refs_0_, bf16[640,1536]{1,0:T(8,128)(2,1)} %collective-permute-done.7.refs_1_, ...), custom_call_target="tpu_custom_call" | custom-call | flops 2013265920 | bytes 4849664 | tf_op jit(solution)/shard_map/pallas_call | solution.py:418
  285.1 9.3 %collective-permute-start.8 = (bf16[512,1536]{1,0:T(8,128)(2,1)}, bf16[512,1536]{1,0:T(8,128)(2,1)}, u32[]{:S(2)}, u32[]{:S(2)}) collective-permute-start(bf16[512,1536]{1,0:T(8,128)(2,1)} %copy-done.70), channel_id=1, source_target_pairs={{0,4},{2,6},{4,0},{6,2},{8,12},{10,14},{12,8},{14,10},{16,20},{18,... | collective-permute-start | bytes 4718600 | tf_op jit(solution)/shard_map/ppermute | solution.py:101
  298.0 7.3 %shard_map.212 = (bf16[512,1536]{1,0:T(8,128)(2,1)S(1)}, bf16[512,1536]{1,0:T(8,128)(2,1)S(1)}) custom-call(bf16[1024,640]{1,0:T(8,128)(2,1)S(1)} %copy-done.12, bf16[1024,640]{1,0:T(8,128)(2,1)S(1)} %copy-done.15, bf16[640,3072]{1,0:T(8,128)(2,1)} %get-tuple-element.70.refs_0_, bf16[640,3072]{1,0:T(8,128)(2,1)} %copy-done.99, ...), custom_call_target="tpu_custom_call" | custom-call | flops 2013265920 | bytes 4849664 | tf_op jit(solution)/shard_map/pallas_call | solution.py:418
  309.6 24.9 %shard_map.213 = (bf16[384,2560]{1,0:T(8,128)(2,1)}, bf16[384,1280]{1,0:T(8,128)(2,1)}, bf16[384,2048]{1,0:T(8,128)(2,1)}, bf16[384,2048]{1,0:T(8,128)(2,1)}) custom-call(bf16[384,2048]{1,0:T(8,128)(2,1)} %slice.188.h_ref, bf16[384,2048]{1,0:T(8,128)(2,1)} %slice.148.dm_ref, bf16[2048,4224]{1,0:T(8,128)(2,1)} %all-gather.6.cloned.1.call-done.wgu_ref.wd_ref, ...), custom_call_target="tpu_custom_call" | custom-call | flops 6039797760 | bytes 17301504 | tf_op jit(solution)/shard_map/pallas_call | solution.py:358
  346.9 19.0 %shard_map.215 = (bf16[256,2560]{1,0:T(8,128)(2,1)}, bf16[256,1280]{1,0:T(8,128)(2,1)}, bf16[256,2048]{1,0:T(8,128)(2,1)}, bf16[256,2048]{1,0:T(8,128)(2,1)}) custom-call(bf16[256,2048]{1,0:T(8,128)(2,1)} %slice.201.h_ref, bf16[256,2048]{1,0:T(8,128)(2,1)} %slice.162.dm_ref, bf16[2048,4224]{1,0:T(8,128)(2,1)} %all-gather.6.cloned.1.call-done.wgu_ref.wd_ref, ...), custom_call_target="tpu_custom_call" | custom-call | flops 4026531840 | bytes 14155776 | tf_op jit(solution)/shard_map/pallas_call | solution.py:358
  365.9 10.5 %collective-permute-done.9.got_ref = bf16[384,2048]{1,0:T(8,128)(2,1)} collective-permute-done((bf16[384,2048]{1,0:T(8,128)(2,1)}, bf16[384,2048]{1,0:T(8,128)(2,1)}, u32[]{:S(2)}, u32[]{:S(2)}) %collective-permute-start.9) | collective-permute-done | bytes 1572896 | tf_op jit(solution)/shard_map/ppermute | solution.py:557
  377.8 8.7 %shard_map.216 = (f32[384,2048]{1,0:T(8,128)}, bf16[384,2048]{1,0:T(8,128)(2,1)S(1)}, bf16[384,1024]{1,0:T(8,128)(2,1)S(1)}, f32[1,2048]{1,0:T(1,128)S(1)}) custom-call(bf16[384,2048]{1,0:T(8,128)(2,1)S(1)} %copy-done.74, bf16[384,2048]{1,0:T(8,128)(2,1)} %collective-permute-done.9.got_ref, f32[640,2048]{1,0:T(8,128)} %copy-done.97, ...), custom_call_target="tpu_custom_call" | custom-call | flops 805306368 | bytes 8388608 | tf_op jit(solution)/shard_map/pallas_call | solution.py:461
  395.6 3.2 collective-permute-done.12.refs_3_
  400.0 6.6 shard_map.218
  408.7 23.3 %collective-permute-done.10.got_ref = bf16[256,2048]{1,0:T(8,128)(2,1)S(1)} collective-permute-done((bf16[256,2048]{1,0:T(8,128)(2,1)S(1)}, bf16[256,2048]{1,0:T(8,128)(2,1)S(1)}, u32[]{:S(2)}, u32[]{:S(2)}) %collective-permute-start.10) | collective-permute-done | bytes 1048608 | tf_op jit(solution)/shard_map/ppermute | solution.py:557
  432.0 6.4 shard_map.219
  438.4 7.5 %shard_map.220 = (bf16[512,1280]{1,0:T(8,128)(2,1)S(1)}, bf16[512,1280]{1,0:T(8,128)(2,1)S(1)}) custom-call(bf16[1024,640]{1,0:T(8,128)(2,1)S(1)} %copy-done.13, bf16[1024,640]{1,0:T(8,128)(2,1)} %copy-done.14, bf16[384,2560]{1,0:T(8,128)(2,1)} %get-tuple-element.78.refs_0_, bf16[256,2560]{1,0:T(8,128)(2,1)} %get-tuple-element.81.refs_0_.refs_1_, ...), custom_call_target="tpu_custom_call" | custom-call | flops 1677721600 | bytes 4259840 | tf_op jit(solution)/shard_map/pallas_call | solution.py:418
  457.1 11.2 %shard_map.223 = (bf16[640,1024]{1,0:T(8,128)(2,1)}, bf16[640,2048]{1,0:T(8,128)(2,1)S(1)}, bf16[64,2048]{1,0:T(8,128)(2,1)S(1)}, f32[64,2048]{1,0:T(8,128)S(1)}) custom-call(bf16[640,3072]{1,0:T(8,128)(2,1)S(1)} %copy-done.1, bf16[640,3072]{1,0:T(8,128)(2,1)S(1)} %copy-done.1, bf16[640,3072]{1,0:T(8,128)(2,1)S(1)} %copy-done.1, ...), custom_call_target="tpu_custom_call" | custom-call | flops 419430400 | bytes 4587520 | tf_op jit(solution)/shard_map/pallas_call | solution.py:244
  469.0 8.1 %shard_map.224 = (bf16[512,1280]{1,0:T(8,128)(2,1)S(1)}, bf16[512,1280]{1,0:T(8,128)(2,1)}) custom-call(bf16[1024,640]{1,0:T(8,128)(2,1)} %copy-done.43, bf16[1024,640]{1,0:T(8,128)(2,1)} %copy-done.19, bf16[384,1280]{1,0:T(8,128)(2,1)S(1)} %copy-done.88, bf16[256,1280]{1,0:T(8,128)(2,1)S(1)} %copy-done.91, ...), custom_call_target="tpu_custom_call" | custom-call | flops 1677721600 | bytes 4259840 | tf_op jit(solution)/shard_map/pallas_call | solution.py:418
  477.5 2.8 collective-permute-done.21.got_ref
  485.9 2.8 constant_dynamic-update-slice_fusion.3
  491.2 18.9 %collective-permute-done.20.got_ref = bf16[512,1280]{1,0:T(8,128)(2,1)} collective-permute-done((bf16[512,1280]{1,0:T(8,128)(2,1)}, bf16[512,1280]{1,0:T(8,128)(2,1)}, u32[]{:S(2)}, u32[]{:S(2)}) %collective-permute-start.20) | collective-permute-done | bytes 1310752 | tf_op jit(solution)/shard_map/ppermute | solution.py:101
  520.0 5.1 shard_map.227
  525.2 6.2 shard_map.228
  533.5 2.6 collective-permute-start.23
  536.1 13.6 %collective-permute-done.15.refs_2_ = bf16[640,2048]{1,0:T(8,128)(2,1)} collective-permute-done((bf16[640,2048]{1,0:T(8,128)(2,1)}, bf16[640,2048]{1,0:T(8,128)(2,1)}, u32[]{:S(2)}, u32[]{:S(2)}) %collective-permute-start.15) | collective-permute-done | bytes 2621472 | tf_op jit(solution)/shard_map/ppermute | solution.py:557
  553.5 6.5 shard_map.229
  559.9 6.3 shard_map.230
  572.1 12.3 %shard_map.232.refs_0_ = bf16[640,2048]{1,0:T(8,128)(2,1)S(1)} custom-call(bf16[640,1024]{1,0:T(8,128)(2,1)} %get-tuple-element.96.refs_0_, bf16[640,2048]{1,0:T(8,128)(2,1)} %copy-done.8, bf16[2048,4224]{1,0:T(8,128)(2,1)} %all-gather.4.cloned.1.call-done.refs_1_.wo_ref.refs_2_, bf16[512,1024]{1,0:T(8,128)(2,1)S(1)} %copy-done.31), custom_call_target="tpu_custom_call" | custom-call | flops 4026531840 | bytes 9568256 | tf_op jit(solution)/shard_map/pallas_call | solution.py:288
  590.4 2.6 collective-permute-start.35
  596.4 5.9 collective-permute-done.35
  610.3 7.0 add_convert_fusion
  617.4 12.8 %collective-permute-done.32.got_ref = bf16[512,1024]{1,0:T(8,128)(2,1)} collective-permute-done((bf16[512,1024]{1,0:T(8,128)(2,1)}, bf16[512,1024]{1,0:T(8,128)(2,1)}, u32[]{:S(2)}, u32[]{:S(2)}) %collective-permute-start.32) | collective-permute-done | bytes 1048608 | tf_op jit(solution)/shard_map/ppermute | solution.py:101
  641.2 2.9 copy.80
  644.1 2.9 copy.81
  647.1 17.8 %collective-permute-done.25.refs_1_ = bf16[640,2048]{1,0:T(8,128)(2,1)} collective-permute-done((bf16[640,2048]{1,0:T(8,128)(2,1)S(1)}, bf16[640,2048]{1,0:T(8,128)(2,1)}, u32[]{:S(2)}, u32[]{:S(2)}) %collective-permute-start.25) | collective-permute-done | bytes 2621472 | tf_op jit(solution)/shard_map/ppermute | solution.py:557
  664.9 4.6 fusion.11
  672.0 2.9 copy.82
  684.6 3.0 collective-permute-done.28
  687.7 4.5 collective-permute-start.30
  692.2 6.1 fusion.10
  700.6 6.4 reduce-scatter.27.cloned.1.call-done
  (412 shorter events, 168.0 us)
Async XLA Ops:
  7.2 99.9 %all-gather.4.cloned.1.call-start = ((), (), s32[]{:S(2)}) async-start(), calls=%async_computation.10 | async-start | bytes 18382848 | tf_op jit(solution)/shard_map/all_gather | solution.py:493
  12.7 195.0 %all-gather.8.cloned.1.call-start = ((), (), s32[]{:S(2)}) async-start(), calls=%async_computation.12 | async-start | bytes 20054016 | tf_op jit(solution)/shard_map/all_gather | solution.py:493
  17.8 291.8 %all-gather.6.cloned.1.call-start = ((), (), s32[]{:S(2)}) async-start(), calls=%async_computation.11 | async-start | bytes 18382848 | tf_op jit(solution)/shard_map/all_gather | solution.py:493
  23.3 365.3 %reduce-scatter.11.cloned.1.call-start = ((), (), s32[]{:S(2)}) async-start(), calls=%async_computation.13 | async-start | bytes 3932160 | tf_op jit(solution)/shard_map/reduce_scatter | solution.py:107
  125.1 4.0 collective-permute-start
  145.9 52.8 %collective-permute-start.1 = (bf16[640,2048]{1,0:T(8,128)(2,1)}, bf16[640,2048]{1,0:T(8,128)(2,1)}, u32[]{:S(2)}, u32[]{:S(2)}) collective-permute-start(bf16[640,2048]{1,0:T(8,128)(2,1)} %shard_map.205), channel_id=1, source_target_pairs={{0,1},{1,0},{2,3},{3,2},{4,5},{5,4},{6,7},{7,6},{8,9},{9,8},{10,11... | collective-permute-start | bytes 7864328 | tf_op jit(solution)/shard_map/ppermute | solution.py:557
  149.8 56.8 %collective-permute-start.3 = (bf16[1024,640]{1,0:T(8,128)(2,1)S(1)}, bf16[1024,640]{1,0:T(8,128)(2,1)S(1)}, u32[]{:S(2)}, u32[]{:S(2)}) collective-permute-start(bf16[1024,640]{1,0:T(8,128)(2,1)S(1)} %get-tuple-element.64), channel_id=1, source_target_pairs={{0,2},{2,0},{4,6},{6,4},{8,10},{10,8},{12,14},{14,12},{16,18},{18,... | collective-permute-start | bytes 3932168 | tf_op jit(solution)/shard_map/ppermute | solution.py:97
  160.0 46.6 %collective-permute-start.4 = (bf16[1024,640]{1,0:T(8,128)(2,1)S(1)}, bf16[1024,640]{1,0:T(8,128)(2,1)S(1)}, u32[]{:S(2)}, u32[]{:S(2)}) collective-permute-start(bf16[1024,640]{1,0:T(8,128)(2,1)S(1)} %get-tuple-element.65), channel_id=1, source_target_pairs={{0,2},{2,0},{4,6},{6,4},{8,10},{10,8},{12,14},{14,12},{16,18},{18,... | collective-permute-start | bytes 3932168 | tf_op jit(solution)/shard_map/ppermute | solution.py:97
  160.0 47.7 %collective-permute-start.2 = (bf16[640,1024]{1,0:T(8,128)(2,1)S(1)}, bf16[640,1024]{1,0:T(8,128)(2,1)}, u32[]{:S(2)}, u32[]{:S(2)}) collective-permute-start(bf16[640,1024]{1,0:T(8,128)(2,1)S(1)} %copy-done.29), channel_id=1, source_target_pairs={{0,2},{2,0},{4,6},{6,4},{8,10},{10,8},{12,14},{14,12},{16,18},{18,... | collective-permute-start | bytes 3932168 | tf_op jit(solution)/shard_map/ppermute | solution.py:97
  245.8 20.1 %collective-permute-start.6 = (bf16[640,3072]{1,0:T(8,128)(2,1)}, bf16[640,3072]{1,0:T(8,128)(2,1)S(1)}, u32[]{:S(2)}, u32[]{:S(2)}) collective-permute-start(bf16[640,3072]{1,0:T(8,128)(2,1)} %get-tuple-element.70.refs_0_), channel_id=1, source_target_pairs={{0,2},{2,0},{4,6},{6,4},{8,10},{10,8},{12,14},{14,12},{16,18},{18,... | collective-permute-start | bytes 11796488 | tf_op jit(solution)/shard_map/ppermute | solution.py:97
  253.1 21.9 %collective-permute-start.7 = (bf16[640,1536]{1,0:T(8,128)(2,1)}, bf16[640,1536]{1,0:T(8,128)(2,1)}, u32[]{:S(2)}, u32[]{:S(2)}) collective-permute-start(bf16[640,1536]{1,0:T(8,128)(2,1)} %get-tuple-element.72.refs_0_), channel_id=1, source_target_pairs={{0,2},{2,0},{4,6},{6,4},{8,10},{10,8},{12,14},{14,12},{16,18},{18,... | collective-permute-start | bytes 5898248 | tf_op jit(solution)/shard_map/ppermute | solution.py:97
  254.5 10.4 %collective-permute-start.5 = (bf16[1024,640]{1,0:T(8,128)(2,1)S(1)}, bf16[1024,640]{1,0:T(8,128)(2,1)S(1)}, u32[]{:S(2)}, u32[]{:S(2)}) collective-permute-start(bf16[1024,640]{1,0:T(8,128)(2,1)S(1)} %get-tuple-element.69), channel_id=1, source_target_pairs={{0,2},{2,0},{4,6},{6,4},{8,10},{10,8},{12,14},{14,12},{16,18},{18,... | collective-permute-start | bytes 3932168 | tf_op jit(solution)/shard_map/ppermute | solution.py:97
  285.1 206.1 %reduce-scatter.13.cloned.1.call-start = ((), (), s32[]{:S(2)}) async-start(), calls=%async_computation.14 | async-start | bytes 1966080 | tf_op jit(solution)/shard_map/reduce_scatter | solution.py:107
  285.1 50.4 %collective-permute-start.8 = (bf16[512,1536]{1,0:T(8,128)(2,1)}, bf16[512,1536]{1,0:T(8,128)(2,1)}, u32[]{:S(2)}, u32[]{:S(2)}) collective-permute-start(bf16[512,1536]{1,0:T(8,128)(2,1)} %copy-done.70), channel_id=1, source_target_pairs={{0,4},{2,6},{4,0},{6,2},{8,12},{10,14},{12,8},{14,10},{16,20},{18,... | collective-permute-start | bytes 4718600 | tf_op jit(solution)/shard_map/ppermute | solution.py:101
  339.8 176.5 %reduce-scatter.15.cloned.1.call-start = ((), (), s32[]{:S(2)}) async-start(), calls=%async_computation.15 | async-start | bytes 1966080 | tf_op jit(solution)/shard_map/reduce_scatter | solution.py:107
  339.9 36.6 %collective-permute-start.9 = (bf16[384,2048]{1,0:T(8,128)(2,1)}, bf16[384,2048]{1,0:T(8,128)(2,1)}, u32[]{:S(2)}, u32[]{:S(2)}) collective-permute-start(bf16[384,2048]{1,0:T(8,128)(2,1)} %get-tuple-element.80.own_ref), channel_id=1, source_target_pairs={{0,1},{1,0},{2,3},{3,2},{4,5},{5,4},{6,7},{7,6},{8,9},{9,8},{10,11... | collective-permute-start | bytes 4718600 | tf_op jit(solution)/shard_map/ppermute | solution.py:557
  341.4 47.2 %collective-permute-start.13 = (bf16[512,1536]{1,0:T(8,128)(2,1)}, bf16[512,1536]{1,0:T(8,128)(2,1)}, u32[]{:S(2)}, u32[]{:S(2)}) collective-permute-start(bf16[512,1536]{1,0:T(8,128)(2,1)} %copy-done.69), channel_id=1, source_target_pairs={{0,4},{2,6},{4,0},{6,2},{8,12},{10,14},{12,8},{14,10},{16,20},{18,... | collective-permute-start | bytes 4718600 | tf_op jit(solution)/shard_map/ppermute | solution.py:101
  346.9 48.7 %collective-permute-start.11 = (bf16[384,2560]{1,0:T(8,128)(2,1)}, bf16[384,2560]{1,0:T(8,128)(2,1)}, u32[]{:S(2)}, u32[]{:S(2)}) collective-permute-start(bf16[384,2560]{1,0:T(8,128)(2,1)} %get-tuple-element.78.refs_0_), channel_id=1, source_target_pairs={{0,2},{2,0},{4,6},{6,4},{8,10},{10,8},{12,14},{14,12},{16,18},{18,... | collective-permute-start | bytes 5898248 | tf_op jit(solution)/shard_map/ppermute | solution.py:97
  395.5 171.8 %reduce-scatter.17.cloned.1.call-start = ((), (), s32[]{:S(2)}) async-start(), calls=%async_computation.16 | async-start | bytes 1638400 | tf_op jit(solution)/shard_map/reduce_scatter | solution.py:107
  406.6 39.2 %collective-permute-start.14 = (bf16[512,1280]{1,0:T(8,128)(2,1)S(1)}, bf16[512,1280]{1,0:T(8,128)(2,1)S(1)}, u32[]{:S(2)}, u32[]{:S(2)}) collective-permute-start(bf16[512,1280]{1,0:T(8,128)(2,1)S(1)} %get-tuple-element.85.refs_1_), channel_id=1, source_target_pairs={{0,4},{2,6},{4,0},{6,2},{8,12},{10,14},{12,8},{14,10},{16,20},{18,... | collective-permute-start | bytes 3932168 | tf_op jit(solution)/shard_map/ppermute | solution.py:101
  407.0 25.0 %collective-permute-start.10 = (bf16[256,2048]{1,0:T(8,128)(2,1)S(1)}, bf16[256,2048]{1,0:T(8,128)(2,1)S(1)}, u32[]{:S(2)}, u32[]{:S(2)}) collective-permute-start(bf16[256,2048]{1,0:T(8,128)(2,1)S(1)} %copy-done.86), channel_id=1, source_target_pairs={{0,1},{1,0},{2,3},{3,2},{4,5},{5,4},{6,7},{7,6},{8,9},{9,8},{10,11... | collective-permute-start | bytes 3145736 | tf_op jit(solution)/shard_map/ppermute | solution.py:557
  449.6 134.9 %reduce-scatter.21.cloned.1.call-start = ((), (), s32[]{:S(2)}) async-start(), calls=%async_computation.18 | async-start | bytes 1638400 | tf_op jit(solution)/shard_map/reduce_scatter | solution.py:107
  449.8 30.5 %collective-permute-start.21 = (bf16[512,1280]{1,0:T(8,128)(2,1)}, bf16[512,1280]{1,0:T(8,128)(2,1)S(1)}, u32[]{:S(2)}, u32[]{:S(2)}) collective-permute-start(bf16[512,1280]{1,0:T(8,128)(2,1)} %copy-done.80), channel_id=1, source_target_pairs={{0,4},{2,6},{4,0},{6,2},{8,12},{10,14},{12,8},{14,10},{16,20},{18,... | collective-permute-start | bytes 3932168 | tf_op jit(solution)/shard_map/ppermute | solution.py:101
  451.5 17.5 %collective-permute-start.18 = (bf16[384,1280]{1,0:T(8,128)(2,1)}, bf16[384,1280]{1,0:T(8,128)(2,1)S(1)}, u32[]{:S(2)}, u32[]{:S(2)}) collective-permute-start(bf16[384,1280]{1,0:T(8,128)(2,1)} %get-tuple-element.101.refs_0_), channel_id=1, source_target_pairs={{0,2},{2,0},{4,6},{6,4},{8,10},{10,8},{12,14},{14,12},{16,18},{18,... | collective-permute-start | bytes 2949128 | tf_op jit(solution)/shard_map/ppermute | solution.py:97
  451.5 17.5 %collective-permute-start.19 = (bf16[256,1280]{1,0:T(8,128)(2,1)}, bf16[256,1280]{1,0:T(8,128)(2,1)S(1)}, u32[]{:S(2)}, u32[]{:S(2)}) collective-permute-start(bf16[256,1280]{1,0:T(8,128)(2,1)} %get-tuple-element.102.refs_1_), channel_id=1, source_target_pairs={{0,2},{2,0},{4,6},{6,4},{8,10},{10,8},{12,14},{14,12},{16,18},{18,... | collective-permute-start | bytes 1966088 | tf_op jit(solution)/shard_map/ppermute | solution.py:97
  477.2 32.9 %collective-permute-start.20 = (bf16[512,1280]{1,0:T(8,128)(2,1)}, bf16[512,1280]{1,0:T(8,128)(2,1)}, u32[]{:S(2)}, u32[]{:S(2)}) collective-permute-start(bf16[512,1280]{1,0:T(8,128)(2,1)} %get-tuple-element.104.refs_1_), channel_id=1, source_target_pairs={{0,4},{2,6},{4,0},{6,2},{8,12},{10,14},{12,8},{14,10},{16,20},{18,... | collective-permute-start | bytes 3932168 | tf_op jit(solution)/shard_map/ppermute | solution.py:101
  477.5 38.8 %collective-permute-start.17 = (bf16[640,1024]{1,0:T(8,128)(2,1)}, bf16[640,1024]{1,0:T(8,128)(2,1)}, u32[]{:S(2)}, u32[]{:S(2)}) collective-permute-start(bf16[640,1024]{1,0:T(8,128)(2,1)} %get-tuple-element.96.refs_0_), channel_id=1, source_target_pairs={{0,2},{2,0},{4,6},{6,4},{8,10},{10,8},{12,14},{14,12},{16,18},{18,... | collective-permute-start | bytes 3932168 | tf_op jit(solution)/shard_map/ppermute | solution.py:97
  484.5 132.9 %reduce-scatter.23.cloned.1.call-start = ((), (), s32[]{:S(2)}) async-start(), calls=%async_computation.19 | async-start | bytes 1638400 | tf_op jit(solution)/shard_map/reduce_scatter | solution.py:107
  484.5 40.6 %collective-permute-start.16 = (bf16[1024,640]{1,0:T(8,128)(2,1)}, bf16[1024,640]{1,0:T(8,128)(2,1)}, u32[]{:S(2)}, u32[]{:S(2)}) collective-permute-start(bf16[1024,640]{1,0:T(8,128)(2,1)} %copy-done.94), channel_id=1, source_target_pairs={{0,2},{2,0},{4,6},{6,4},{8,10},{10,8},{12,14},{14,12},{16,18},{18,... | collective-permute-start | bytes 3932168 | tf_op jit(solution)/shard_map/ppermute | solution.py:97
  484.6 47.8 %collective-permute-start.22 = (bf16[64,2048]{1,0:T(8,128)(2,1)S(1)}, bf16[64,2048]{1,0:T(8,128)(2,1)S(1)}, u32[]{:S(2)}, u32[]{:S(2)}) collective-permute-start(bf16[64,2048]{1,0:T(8,128)(2,1)S(1)} %copy-done.96), channel_id=1, source_target_pairs={{2,0},{4,2},{6,4},{8,6},{10,8},{12,10},{14,12},{16,14},{18,16},{20... | collective-permute-start | bytes 786440 | tf_op jit(solution)/shard_map/ppermute | solution.py:623
  489.8 59.9 %collective-permute-start.15 = (bf16[640,2048]{1,0:T(8,128)(2,1)}, bf16[640,2048]{1,0:T(8,128)(2,1)}, u32[]{:S(2)}, u32[]{:S(2)}) collective-permute-start(bf16[640,2048]{1,0:T(8,128)(2,1)} %constant_dynamic-update-slice_fusion.2), channel_id=1, source_target_pairs={{0,1},{1,0},{2,3},{3,2},{4,5},{5,4},{6,7},{7,6},{8,9},{9,8},{10,11... | collective-permute-start | bytes 7864328 | tf_op jit(solution)/shard_map/ppermute | solution.py:557
  533.4 16.3 %collective-permute-start.24 = (bf16[640,2048]{1,0:T(8,128)(2,1)S(1)}, bf16[640,2048]{1,0:T(8,128)(2,1)}, u32[]{:S(2)}, u32[]{:S(2)}) collective-permute-start(bf16[640,2048]{1,0:T(8,128)(2,1)S(1)} %fusion.25.refs_0_.refs_1_), channel_id=1, source_target_pairs={{0,2},{2,0},{4,6},{6,4},{8,10},{10,8},{12,14},{14,12},{16,18},{18,... | collective-permute-start | bytes 7864328 | tf_op jit(solution)/shard_map/ppermute | solution.py:97
  533.4 146.7 %reduce-scatter.29.cloned.1.call-start = ((), (), s32[]{:S(2)}) async-start(), calls=%async_computation.22 | async-start | bytes 1310720 | tf_op jit(solution)/shard_map/reduce_scatter | solution.py:107
  533.5 33.8 %collective-permute-start.23 = (bf16[512,1024]{1,0:T(8,128)(2,1)}, bf16[512,1024]{1,0:T(8,128)(2,1)}, u32[]{:S(2)}, u32[]{:S(2)}) collective-permute-start(bf16[512,1024]{1,0:T(8,128)(2,1)} %copy-done.87), channel_id=1, source_target_pairs={{0,4},{2,6},{4,0},{6,2},{8,12},{10,14},{12,8},{14,10},{16,20},{18,... | collective-permute-start | bytes 3145736 | tf_op jit(solution)/shard_map/ppermute | solution.py:101
  536.0 48.4 %collective-permute-start.33 = (bf16[512,1024]{1,0:T(8,128)(2,1)}, bf16[512,1024]{1,0:T(8,128)(2,1)}, u32[]{:S(2)}, u32[]{:S(2)}) collective-permute-start(bf16[512,1024]{1,0:T(8,128)(2,1)} %copy-done.84), channel_id=1, source_target_pairs={{0,4},{2,6},{4,0},{6,2},{8,12},{10,14},{12,8},{14,10},{16,20},{18,... | collective-permute-start | bytes 3145736 | tf_op jit(solution)/shard_map/ppermute | solution.py:101
  589.1 93.0 %reduce-scatter.19.cloned.1.call-start = ((), (), s32[]{:S(2)}) async-start(), calls=%async_computation.17 | async-start | bytes 1310720 | tf_op jit(solution)/shard_map/reduce_scatter | solution.py:107
  590.4 12.0 %collective-permute-start.35 = (bf16[128,1536]{1,0:T(8,128)(2,1)}, bf16[128,1536]{1,0:T(8,128)(2,1)}, u32[]{:S(2)}, u32[]{:S(2)}) collective-permute-start(bf16[128,1536]{1,0:T(8,128)(2,1)} %slice.219), channel_id=1, source_target_pairs={{0,4},{2,6},{4,0},{6,2},{8,12},{10,14},{12,8},{14,10},{16,20},{18,... | collective-permute-start | bytes 1179656 | tf_op jit(solution)/shard_map/ppermute | solution.py:101
  596.4 102.5 %reduce-scatter.25.cloned.1.call-start = ((), (), s32[]{:S(2)}) async-start(), calls=%async_computation.20 | async-start | bytes 1310720 | tf_op jit(solution)/shard_map/reduce_scatter | solution.py:107
  605.7 24.5 %collective-permute-start.32 = (bf16[512,1024]{1,0:T(8,128)(2,1)}, bf16[512,1024]{1,0:T(8,128)(2,1)}, u32[]{:S(2)}, u32[]{:S(2)}) collective-permute-start(bf16[512,1024]{1,0:T(8,128)(2,1)} %get-tuple-element.112.refs_3_), channel_id=1, source_target_pairs={{0,4},{2,6},{4,0},{6,2},{8,12},{10,14},{12,8},{14,10},{16,20},{18,... | collective-permute-start | bytes 3145736 | tf_op jit(solution)/shard_map/ppermute | solution.py:101
  607.5 57.4 %collective-permute-start.25 = (bf16[640,2048]{1,0:T(8,128)(2,1)S(1)}, bf16[640,2048]{1,0:T(8,128)(2,1)}, u32[]{:S(2)}, u32[]{:S(2)}) collective-permute-start(bf16[640,2048]{1,0:T(8,128)(2,1)S(1)} %shard_map.232.refs_0_), channel_id=1, source_target_pairs={{0,1},{1,0},{2,3},{3,2},{4,5},{5,4},{6,7},{7,6},{8,9},{9,8},{10,11... | collective-permute-start | bytes 7864328 | tf_op jit(solution)/shard_map/ppermute | solution.py:557
  636.2 70.8 %reduce-scatter.27.cloned.1.call-start = ((), (), s32[]{:S(2)}) async-start(), calls=%async_computation.21 | async-start | bytes 1310720 | tf_op jit(solution)/shard_map/reduce_scatter | solution.py:107
  638.6 36.3 %collective-permute-start.34 = (bf16[512,1024]{1,0:T(8,128)(2,1)}, bf16[512,1024]{1,0:T(8,128)(2,1)}, u32[]{:S(2)}, u32[]{:S(2)}) collective-permute-start(bf16[512,1024]{1,0:T(8,128)(2,1)} %get-tuple-element.114.refs_1_), channel_id=1, source_target_pairs={{0,4},{2,6},{4,0},{6,2},{8,12},{10,14},{12,8},{14,10},{16,20},{18,... | collective-permute-start | bytes 3145736 | tf_op jit(solution)/shard_map/ppermute | solution.py:101
  669.5 10.4 %collective-permute-start.26 = (f32[2048]{0:T(1024)S(1)}, f32[2048]{0:T(1024)S(1)}, u32[]{:S(2)}, u32[]{:S(2)}) collective-permute-start(f32[2048]{0:T(1024)S(1)} %get-tuple-element.172), channel_id=1, source_target_pairs={{0,1},{1,0},{2,3},{3,2},{4,5},{5,4},{6,7},{7,6},{8,9},{9,8},{10,11... | collective-permute-start | bytes 24584 | tf_op jit(solution)/shard_map/ppermute | solution.py:557
  680.0 3.9 collective-permute-start.27
  683.9 3.7 collective-permute-start.28
  687.6 10.7 %collective-permute-start.29 = (f32[2,128]{1,0:T(2,128)S(1)}, f32[2,128]{1,0:T(2,128)S(1)}, u32[]{:S(2)}, u32[]{:S(2)}) collective-permute-start(f32[2,128]{1,0:T(2,128)S(1)} %get-tuple-element.187), channel_id=1, source_target_pairs={{0,8},{2,10},{4,12},{6,14},{8,16},{10,18},{12,20},{14,22},{16,24},... | collective-permute-start | bytes 3080 | tf_op jit(solution)/shard_map/ppermute | solution.py:146
  687.7 10.6 %collective-permute-start.30 = (f32[2,128]{1,0:T(2,128)S(1)}, f32[2,128]{1,0:T(2,128)S(1)}, u32[]{:S(2)}, u32[]{:S(2)}) collective-permute-start(f32[2,128]{1,0:T(2,128)S(1)} %get-tuple-element.189), channel_id=1, source_target_pairs={{0,16},{2,18},{4,20},{6,22},{8,24},{10,26},{12,28},{14,30},{16,0},... | collective-permute-start | bytes 3080 | tf_op jit(solution)/shard_map/ppermute | solution.py:146
  692.2 6.1 collective-permute-start.31
  (116 other events, 696.7 us)
Sparse Core Ops, SparseCore 0:
  12.8 94.2 all-gather.3
  108.7 98.9 all-gather.7
  209.2 100.3 all-gather.5
  311.8 61.4 reduce-scatter.10
  375.4 35.3 reduce-scatter.12
  412.9 34.2 reduce-scatter.14
  449.7 32.8 reduce-scatter.16
  484.9 33.1 reduce-scatter.20
  533.5 31.0 reduce-scatter.22
  589.3 29.6 reduce-scatter.28
  621.3 25.7 reduce-scatter.18
  649.3 25.7 reduce-scatter.24
  679.9 26.9 reduce-scatter.26

commit v3 on v2

--- a/solution.py
+++ b/solution.py
@@ -14,7 +14,7 @@
 BF16 = jnp.bfloat16
 F32 = jnp.float32
 ANYWHERE = pl.BlockSpec(memory_space=pl.ANY)
-HINT = 0.5
+HINT = 0.01
 
 
 def cost(flops, bytes_accessed, transcendentals):
@@ -89,7 +89,7 @@
         out_specs=(whole, whole),
         out_shape=(jax.ShapeDtypeStruct((columns // 2, rows), kind),) * 2,
         cost_estimate=cost(flops=0, bytes_accessed=4 * rows * columns, transcendentals=0),
-        compiler_params=pltpu.CompilerParams(vmem_limit_bytes=32 << 20),
+        compiler_params=pltpu.CompilerParams(vmem_limit_bytes=60 << 20),
     )(order, *pieces, *after)
 
 
@@ -105,6 +105,19 @@
     outers = lax.axis_size("seq") // 4
     groups = [[o * 4 + place for o in range(outers)] for place in range(4)]
     return lax.psum_scatter(values, "seq", scatter_dimension=0, axis_index_groups=groups, tiled=True)
+
+
+def sum_outer_direct(values):
+    count = lax.axis_size("seq")
+    outers = count // 4
+    values = values.reshape(outers, values.shape[0] // outers, values.shape[1])
+    outer = lax.axis_index("seq") // 4
+    total = lax.dynamic_index_in_dim(values, outer, 0, keepdims=False).astype(F32)
+    for step in range(1, outers):
+        sent = lax.dynamic_index_in_dim(values, (outer + step) % outers, 0, keepdims=False)
+        got = lax.ppermute(sent, "seq", [(s, (s + 4 * step) % count) for s in range(count)])
+        total = total + got.astype(F32)
+    return total
 
 
 def add_block(keep_ref, got_ref, *refs):
@@ -127,7 +140,7 @@
         out_specs=spec,
         out_shape=jax.ShapeDtypeStruct((rows, columns), BF16),
         cost_estimate=cost(flops=rows * columns, bytes_accessed=6 * rows * columns, transcendentals=0),
-        compiler_params=pltpu.CompilerParams(vmem_limit_bytes=32 << 20),
+        compiler_params=pltpu.CompilerParams(vmem_limit_bytes=60 << 20),
     )(keep, got, *after)
 
 
@@ -171,36 +184,31 @@
 
 
 def attend_back(heads, pieces, q_ref, k_ref, v_ref, k_tail_ref, v_tail_ref, bias_ref, *refs):
-    dq_ref, dkv_ref, edge_send_ref, edge_keep_ref = refs[-4:]
-    da = jnp.concatenate([r[...] for r in refs[:pieces]], 0)
+    q_next_ref, k_next_ref, v_next_ref = refs[:3]
+    dq_ref, dkv_ref = refs[-2:]
+    da = jnp.concatenate([r[...] for r in refs[3 : 4 + pieces]], 0)
     scale = 1.0 / math.sqrt(HEAD_DIM)
     head = pl.program_id(0)
-    steps = q_ref.shape[0] // WINDOW
-    query = q_ref[...]
-    key = jnp.concatenate([k_tail_ref[...], k_ref[...]], 0)
-    value = jnp.concatenate([v_tail_ref[...], v_ref[...]], 0)
+    steps = da.shape[0] // WINDOW
+    query = jnp.concatenate([q_ref[...], q_next_ref[...]], 0)
+    key = jnp.concatenate([k_tail_ref[...], k_ref[...], k_next_ref[...]], 0)
+    value = jnp.concatenate([v_tail_ref[...], v_ref[...], v_next_ref[...]], 0)
     probs = band_probs(query, key, bias_ref[...], steps)
     dp = jnp.concatenate([mat_nt(da[rows], value[keys]) for rows, keys in bands(steps)], 0)
     inner = jnp.sum(probs * dp, axis=1, keepdims=True)
     ds = (probs * (dp - inner)).astype(BF16)
     probs = probs.astype(BF16)
-
-    def place(part):
-        return pl.ds(pl.multiple_of((part * heads + head) * HEAD_DIM, HEAD_DIM), HEAD_DIM)
-
     low = None
     for i, (rows, keys) in enumerate(bands(steps)):
-        dq_ref[rows] = (mat_nn(ds[rows], key[keys]) * scale).astype(BF16)
+        if i < steps - 1:
+            dq_ref[rows] = (mat_nn(ds[rows], key[keys]) * scale).astype(BF16)
         both = (mat_tn(ds[rows], query[rows]) * scale, mat_tn(probs[rows], da[rows]))
-        for part in range(2):
-            first = both[part][:WINDOW] if low is None else both[part][:WINDOW] + low[part]
-            if i:
-                dkv_ref[bands(steps)[i - 1][0], place(part)] = first.astype(BF16)
-            else:
-                edge_send_ref[:, place(part)] = first.astype(BF16)
+        if i:
+            for part in range(2):
+                columns = pl.ds(pl.multiple_of((part * heads + head) * HEAD_DIM, HEAD_DIM), HEAD_DIM)
+                own_rows = slice((i - 1) * WINDOW, i * WINDOW)
+                dkv_ref[own_rows, columns] = (both[part][:WINDOW] + low[part]).astype(BF16)
         low = [b[WINDOW:] for b in both]
-    for part in range(2):
-        edge_keep_ref[:, place(part)] = low[part]
 
 
 def head_spec(rows, first=0):
@@ -211,14 +219,14 @@
     return pl.BlockSpec(shape, lambda j: (0, 0), pipeline_mode=pl.Buffered(1))
 
 
-def attention_specs(tokens, heads):
+def attention_specs(tokens, heads, extra=0):
     return [
         head_spec(tokens),
         head_spec(tokens, heads),
         head_spec(tokens, 2 * heads),
         head_spec(WINDOW),
         head_spec(WINDOW, heads),
-        once((tokens, 2 * WINDOW)),
+        once((tokens + extra, 2 * WINDOW)),
     ]
 
 
@@ -234,36 +242,30 @@
         cost_estimate=cost(
             flops=8 * tokens * width * WINDOW, bytes_accessed=8 * tokens * width, transcendentals=tokens * width
         ),
-        compiler_params=pltpu.CompilerParams(vmem_limit_bytes=32 << 20),
+        compiler_params=pltpu.CompilerParams(vmem_limit_bytes=60 << 20),
     )(qkv, qkv, qkv, tail, tail, bias)
 
 
-def attention_backward(qkv, tail, bias, da, *after):
+def attention_backward(qkv, tail, bias, following, da, *after):
     tokens, heads = qkv.shape[0], qkv.shape[1] // (3 * HEAD_DIM)
     width = heads * HEAD_DIM
     return pl.pallas_call(
-        functools.partial(attend_back, heads, len(da)),
+        functools.partial(attend_back, heads, len(da) - 1),
         grid=(heads,),
-        in_specs=attention_specs(tokens, heads)
+        in_specs=attention_specs(tokens, heads, WINDOW)
+        + [head_spec(WINDOW, part * heads) for part in range(3)]
         + [head_spec(d.shape[0]) for d in da]
         + [ANYWHERE] * len(after),
-        out_specs=(
-            head_spec(tokens),
-            once((tokens, 2 * width)),
-            once((WINDOW, 2 * width)),
-            once((WINDOW, 2 * width)),
-        ),
+        out_specs=(head_spec(tokens), once((tokens, 2 * width))),
         out_shape=(
             jax.ShapeDtypeStruct((tokens, width), BF16),
             jax.ShapeDtypeStruct((tokens, 2 * width), BF16),
-            jax.ShapeDtypeStruct((WINDOW, 2 * width), BF16),
-            jax.ShapeDtypeStruct((WINDOW, 2 * width), F32),
         ),
         cost_estimate=cost(
             flops=20 * tokens * width * WINDOW, bytes_accessed=14 * tokens * width, transcendentals=tokens * width
         ),
-        compiler_params=pltpu.CompilerParams(vmem_limit_bytes=40 << 20),
-    )(qkv, qkv, qkv, tail, tail, bias, *da, *after)
+        compiler_params=pltpu.CompilerParams(vmem_limit_bytes=60 << 20),
+    )(qkv, qkv, qkv, tail, tail, bias, following, following, following, *da, *after)
 
 
 def multiply(turned, pieces, *refs):
@@ -294,11 +296,11 @@
         cost_estimate=cost(
             flops=2 * tokens * d * out, bytes_accessed=2 * (tokens * (d + out) + d * out), transcendentals=0
         ),
-        compiler_params=pltpu.CompilerParams(vmem_limit_bytes=48 << 20),
+        compiler_params=pltpu.CompilerParams(vmem_limit_bytes=60 << 20),
     )(*pieces, weights, *after)
 
 
-PARTS = ((512, 3), (640, 2))
+PARTS = ((768, 2), (640, 2))
 
 
 def feed(block, steps, first_row, h_ref, dm_ref, wgu_ref, wd_ref, *refs):
@@ -306,12 +308,24 @@
     carried = first_row is not None
     if carried:
         m_in, dh_in = refs[:2]
-        wide_ref, hidden_ref, m_out, dh_out, m_sum, dh_sum = refs[-6:]
+        wide_ref, hidden_ref, m_out, dh_out, m_sum, dh_sum, m_sem, dh_sem = refs[-8:]
+        here = pl.ds(first_row, m_sum.shape[0])
+        copies = (
+            pltpu.make_async_copy(m_in.at[here], m_sum, m_sem),
+            pltpu.make_async_copy(dh_in.at[here], dh_sum, dh_sem),
+        )
+
+        @pl.when(j == 0)
+        def _():
+            for copy in copies:
+                copy.start()
+
     else:
         wide_ref, hidden_ref, m_sum, dh_sum = refs[-4:]
-    gate_up = mat_nn(h_ref[...], wgu_ref[...])
+    taken = slice(first_row or 0, (first_row or 0) + m_sum.shape[0])
+    gate_up = mat_nn(h_ref[taken], wgu_ref[...])
     gate, up = gate_up[:, :block], gate_up[:, block:]
-    dhidden = mat_nn(dm_ref[...], wd_ref[...])
+    dhidden = mat_nn(dm_ref[taken], wd_ref[...])
     sigma = jax.nn.sigmoid(gate)
     silu = gate * sigma
     hidden = (silu * up).astype(BF16)
@@ -324,9 +338,8 @@
     @pl.when(j == 0)
     def _():
         if carried:
-            rows = pl.ds(first_row, m_sum.shape[0])
-            pltpu.sync_copy(m_in.at[rows], m_sum)
-            pltpu.sync_copy(dh_in.at[rows], dh_sum)
+            for copy in copies:
+                copy.wait()
         else:
             m_sum[...] = jnp.zeros_like(m_sum)
             dh_sum[...] = jnp.zeros_like(dh_sum)
@@ -352,15 +365,13 @@
     carried = bool(carry)
     tokens = count * 128 if carried else rows.shape[0]
     row_spec = once((tokens, d))
-    if carried:
-        rows, dm = rows[place * 128 : place * 128 + tokens], dm[place * 128 : place * 128 + tokens]
     kind = BF16 if carried else F32
     return pl.pallas_call(
         functools.partial(feed, block, steps, place * 128 if carried else None),
         grid=(steps,),
         in_specs=[
-            row_spec,
-            row_spec,
+            once(rows.shape),
+            once(rows.shape),
             pl.BlockSpec((d, 2 * block), lambda j: (0, j)),
             pl.BlockSpec((d, block), lambda j: (0, 2 * steps + j)),
         ]
@@ -377,7 +388,7 @@
             jax.ShapeDtypeStruct((tokens, d), kind),
             jax.ShapeDtypeStruct((tokens, d), kind),
         ),
-        scratch_shapes=[pltpu.VMEM((tokens, d), F32)] * 2 if carried else [],
+        scratch_shapes=([pltpu.VMEM((tokens, d), F32)] * 2 + [pltpu.SemaphoreType.DMA] * 2) if carried else [],
         cost_estimate=cost(
             flops=12 * tokens * d * wide, bytes_accessed=6 * d * wide + 24 * tokens * d, transcendentals=tokens * wide
         ),
@@ -426,7 +437,7 @@
         cost_estimate=cost(
             flops=4 * tokens * d * columns, bytes_accessed=2 * (d + 2 * tokens) * columns + 4 * d * tokens, transcendentals=0
         ),
-        compiler_params=pltpu.CompilerParams(vmem_limit_bytes=48 << 20),
+        compiler_params=pltpu.CompilerParams(vmem_limit_bytes=60 << 20),
     )(*left, *pieces, *after)
 
 
@@ -480,7 +491,7 @@
         cost_estimate=cost(
             flops=2 * tokens * d * width, bytes_accessed=2 * d * width + 16 * tokens * d, transcendentals=0
         ),
-        compiler_params=pltpu.CompilerParams(vmem_limit_bytes=48 << 20),
+        compiler_params=pltpu.CompilerParams(vmem_limit_bytes=60 << 20),
     )(own, got, middle, dm, gain, weights, *after)
 
 
@@ -527,7 +538,7 @@
 
     order = relative_blocks(count)
     first_place = lax.axis_index("seq") * tokens
-    row = jnp.arange(tokens, dtype=jnp.int32)[:, None]
+    row = jnp.arange(tokens + WINDOW, dtype=jnp.int32)[:, None]
     column = jnp.arange(2 * WINDOW, dtype=jnp.int32)[None, :]
     key_place = row // WINDOW * WINDOW + column - WINDOW
     ends = [lengths[0]]
@@ -562,7 +573,8 @@
 
     qkv = rows_times((normed,), attn_w, 3 * width)
     tail = lax.ppermute(qkv[tokens - WINDOW :, width:], "seq", shift_pairs(count, 1))
-    mixed = attention_forward(qkv, tail, bias)
+    following = lax.ppermute(qkv[:WINDOW], "seq", shift_pairs(count, -1))
+    mixed = attention_forward(qkv, tail, bias[:tokens])
     mixed_both = both_cores(mixed)
     branch = rows_times((mixed,), attn_w, width, 3 * width, True)
     middle = x_full + (branch.astype(F32) + to_mp(branch).astype(F32))
@@ -570,7 +582,7 @@
     normed_two = (middle * inverse_two * gain_two).astype(BF16)
     normed_two_turned = both_halves((normed_two,))
 
-    after = (mixed_both[1][0], cot_turned[1], normed_turned[1])
+    after = (mixed_both[1][0], cot_turned[1], normed_turned[1], following)
     one, two = (block * steps for block, steps in PARTS)
     wide_acts, hidden, *carry = feed_forward(normed_two, cotangent, ffn_w[0], PARTS[0], after=after)
     wide_acts = both_cores(wide_acts)
@@ -589,51 +601,45 @@
     wide_acts, hidden, m_halves, dh_halves = zip(*halves)
     after = (wide_acts[1],)
     wide_acts, hidden = both_cores(*wide_acts), both_cores(*hidden)
+    half = one_c.shape[0] // 2
+    one_c = one_c[:half].astype(F32) + to_middle(one_c[half:]).astype(F32)
     middles = []
     for (place, _), dh in zip(places, dh_halves):
         middles.append(
             middle_gradient(dh, to_mp(dh), middle, cotangent, gain_two[None], attn_w, width, place, after)
         )
         if not place:
-            one_b = add_middle(one_b, (middles[0][1], one_c))
-            two_a = weight_grad(normed_two_turned, wide_acts, (one_b,), 0, two)
-            after = two_a
+            two_a = weight_grad(normed_two_turned, wide_acts, (middles[0][1],), 0, two)
+            da_next = lax.ppermute(middles[0][2][:WINDOW], "seq", shift_pairs(count, -1))
+            after = (*two_a, da_next, one_c)
     grad_gain_two = sum(m[3][0] for m in middles)
-    two_b = weight_grad(normed_two_turned, wide_acts, (middles[1][1],), two, two)
-    two_a = add_middle(two_a, two_b)
-    half = one_c.shape[0] // 2
-    one_c = one_c[:half].astype(F32) + to_middle(one_c[half:]).astype(F32)
+    one_b = add_middle(one_b, (middles[1][1],))
+    two_b = weight_grad(normed_two_turned, wide_acts, (one_b,), two, two)
     one_a, one_b = sum_outer(one_a), sum_outer(one_b)
-    branch_turned = both_halves([m[1] for m in middles], two_a)
-    grad_q, grad_kv, edge_send, edge_keep = attention_backward(
-        qkv, tail, bias, [m[2] for m in middles], branch_turned[0]
-    )
-    two_c = weight_grad(cot_turned, hidden, (edge_keep,))
+    branch_turned = both_halves([m[1] for m in middles], *two_b)
+    da = [m[2] for m in middles] + [da_next]
+    grad_q, grad_kv = attention_backward(qkv, tail, bias, following, da, branch_turned[0])
+    two_a = add_middle(two_a, (grad_q, one_a))
+    two_c = weight_grad(cot_turned, hidden, (two_a,))
     two_b = add_middle(two_b, two_c)
-    after = (two_b, one_a)
+    after = (two_b,)
     two_a, two_b = sum_outer(two_a), sum_outer(two_b)
-    two_c = add_middle(two_c, after)
-    q_part = weight_grad(normed_turned, both_cores(grad_q), (two_c, one_b))
-    out_part = weight_grad(branch_turned, mixed_both, q_part)
-    two_c = sum_outer(two_c)
     late, _ = lax.optimization_barrier((m_halves, branch_turned[0]))
     late = jnp.concatenate(late, 0)
     late_got = to_mp(late)
-    edge_keep, _ = lax.optimization_barrier((edge_keep, out_part[0]))
-    back = lax.ppermute(edge_send, "seq", shift_pairs(count, -1))
-    last_rows = (edge_keep + back.astype(F32)).astype(BF16)
-    grad_kv = lax.dynamic_update_slice(grad_kv, last_rows, (tokens - WINDOW, 0))
-    kv_both = both_cores(grad_kv)
-    k_part = weight_grad(normed_turned, kv_both, (late_got, *out_part), 0, width)
-    v_part = weight_grad(normed_turned, kv_both, k_part, width, width)
-    q_part = add_middle(q_part, (*v_part, two_a))
-    own = rows_times((grad_q, grad_kv), attn_w, 3 * width, 0, True, after=(q_part,))
+    q_part = weight_grad(normed_turned, both_cores(grad_q), after)
+    kv_part = weight_grad(normed_turned, both_cores(grad_kv), (*q_part, one_b))
+    own = rows_times((grad_q, grad_kv), attn_w, 3 * width, 0, True, after=kv_part)
     own_got = to_mp(own)
-    out_part = add_middle(out_part, (own, two_b))
-    k_part = add_middle(k_part, (out_part, two_c))
-    v_part = add_middle(v_part, (k_part, own_got))
-    q_sum, out_sum = sum_outer(q_part).astype(F32), sum_outer(out_part).astype(F32)
-    k_sum, v_sum = sum_outer(k_part).astype(F32), sum_outer(v_part).astype(F32)
+    out_part = weight_grad(branch_turned, mixed_both, (own, two_a))
+    two_c = add_middle(two_c, (*out_part, late_got))
+    q_part = add_middle(q_part, (two_c,))
+    mixed_sum = sum_outer(jnp.concatenate([two_c, q_part], 1))
+    down_two, q_sum = mixed_sum[:, :two], mixed_sum[:, two:].astype(F32)
+    kv_part = add_middle(kv_part, (q_part, two_b, own_got))
+    kv_sum = sum_outer(kv_part).astype(F32)
+    out_part = add_middle(out_part, (kv_part, mixed_sum))
+    out_sum = sum_outer_direct(out_part)
     grad_normed = own.astype(F32) + own_got.astype(F32)
     grad_gain_one = jnp.sum(own.astype(F32) * unit_one, axis=0)
     grad_gain_one = grad_gain_one + to_mp(grad_gain_one)
@@ -655,15 +661,15 @@
         return jnp.concatenate(pieces, 1)[:, :ff].astype(F32)
 
     grad_gate, grad_up = columns(0), columns(1)
-    grad_down = jnp.concatenate([one_c, two_c.astype(F32)], 1)[:, :ff].astype(F32)
+    grad_down = jnp.concatenate([one_c, down_two.astype(F32)], 1)[:, :ff].astype(F32)
 
     return (
         result.astype(BF16),
         grad_input.astype(BF16),
         gain_sums[0],
         q_sum,
-        k_sum,
-        v_sum,
+        kv_sum[:, :width],
+        kv_sum[:, width:],
         out_sum.T,
         gain_sums[1],
         grad_gate,

time: 726 us -> 703 us (0.968)
  local copies, waits for them, and re-layouts: 111 us -> 47.9 us
  Pallas kernels: 233 us -> 264 us
  waiting for transfers between devices: 251 us -> 261 us
    unnamed x253 -> x76, local copies, waits for them, and re-layouts: 96 us -> 28 us
    ppermute x6, waiting for transfers between devices: 104 us -> 77.7 us  [to_mp(): return lax.ppermute(own, 'mp', [(0, 1), (1, 0)])]
    ppermute x1 -> x5, waiting for transfers between devices: 0.01 us -> 23.5 us  [the longest x3 23.5 us: sum_outer_direct(): lax.ppermute(sent, 'seq', [(s, (s + 4 * step) % count) for s in range(cou...]
    all_gather x3, waiting for transfers between devices: 81.8 us -> 100 us  [gather(): return lax.all_gather(jnp.concatenate(shards, 1), 'seq', axis=0, tiled=True)]
    pallas_call x4, Pallas kernels: 5.11 us -> 16.1 us  [relative_turned(): pl.pallas_call(functools.partial(turn_blocks, len(pieces)), in_specs=[pl....]
    pallas_call x9 -> x8, Pallas kernels: 13.1 us -> 23 us  [add_middle(): pl.pallas_call(add_block, grid=(columns // wide,), in_specs=[spec] * 2 +...]
    reduce_scatter x10 -> x7, waiting for transfers between devices: 6.41 us -> 16.3 us  [sum_outer(): lax.psum_scatter(values, 'seq', scatter_dimension=0, axis_index_groups=gr...]
    ppermute x11 -> x10, waiting for transfers between devices: 44.4 us -> 35.7 us  [to_middle(): return lax.ppermute(values, 'seq', flip_pairs(lax.axis_size('seq'), 2))]
  transfers between devices with their start and end apart: 49 -> 49, of which waited for: 17 -> 14; matrix products, arithmetic and copies ran while one was open for 11% -> 11% of each run, Pallas kernels for 33% -> 38%
where the time goes in v3:
time: 703 us; the launch traced here: 691 us
  Pallas kernels  264 us (38%)
  waiting for transfers between devices  261 us (37%)
  starting transfers between devices  54.3 us (8%)
  local copies, waits for them, and re-layouts  47.9 us (7%)
  other arithmetic  46 us (7%)
  between operations  17.8 us (3%)
    all_gather x3, waiting for transfers between devices, gather(): return lax.all_gather(jnp.concatenate(shards, 1), 'seq', axis=0, tiled=True)  100 us
    pallas_call x3, Pallas kernels, feed_forward(): pl.pallas_call(functools.partial(feed, block, steps, place * 128 if carri...  78.1 us
    ppermute x6, waiting for transfers between devices, to_mp(): return lax.ppermute(own, 'mp', [(0, 1), (1, 0)])  77.7 us
    pallas_call x9, Pallas kernels, weight_grad(): pl.pallas_call(functools.partial(grad_block, len(right[0]), outers), grid...  75.1 us
    ppermute x10, waiting for transfers between devices, to_middle(): return lax.ppermute(values, 'seq', flip_pairs(lax.axis_size('seq'), 2))  35.7 us
    pallas_call x3, Pallas kernels, rows_times(): pl.pallas_call(functools.partial(multiply, turned, len(pieces)), grid=(ou...  33.1 us
    unnamed x76, local copies, waits for them, and re-layouts  28 us
    ppermute x3, waiting for transfers between devices, sum_outer_direct(): lax.ppermute(sent, 'seq', [(s, (s + 4 * step) % count) for s in range(cou...  23.5 us
  transfers between devices with their start and end apart: 49, of which 14 were waited for; matrix products, arithmetic and copies ran while one was open for 11% of the time, Pallas kernels for 38%

profile of v3, /device:TPU:0, one launch (start us, length us, event | category | flops | bytes accessed | tf_op | source)
XLA Modules:
  0.0 690.6 jit_solution(8133682493620158237)
XLA Ops:
  27.2 79.8 %all-gather.4.cloned.1.call-done.refs_1_.wo_ref.refs_2_ = bf16[2048,4224]{1,0:T(8,128)(2,1)} async-done(((bf16[128,4224]{1,0:T(8,128)(2,1)}), bf16[2048,4224]{1,0:T(8,128)(2,1)}) %all-gather.4.cloned.1.call-update) | async-done | bytes 17301520 | tf_op jit(solution)/shard_map/all_gather | solution.py:504
  111.7 13.3 %shard_map.203.q_ref.k_ref.v_ref = bf16[640,3072]{1,0:T(8,128)(2,1)} custom-call(bf16[640,2048]{1,0:T(8,128)(2,1)} %fusion.5.refs_0_, bf16[2048,4224]{1,0:T(8,128)(2,1)} %all-gather.4.cloned.1.call-done.refs_1_.wo_ref.refs_2_), custom_call_target="tpu_custom_call" | custom-call | flops 80530640 | bytes 191365 | tf_op jit(solution)/shard_map/pallas_call | solution.py:290
  131.9 8.9 %shard_map.204.refs_0_ = bf16[640,1024]{1,0:T(8,128)(2,1)} custom-call(bf16[640,3072]{1,0:T(8,128)(2,1)} %shard_map.203.q_ref.k_ref.v_ref, bf16[640,3072]{1,0:T(8,128)(2,1)} %shard_map.203.q_ref.k_ref.v_ref, bf16[640,3072]{1,0:T(8,128)(2,1)} %shard_map.203.q_ref.k_ref.v_ref, bf16[64,2048]{1,0:T(8,128)(2,1)} %copy-done.7, bf16[64,2048]{1,0:T(8,128)(2,1)} %copy-done.7, ...), custom_call_target="tpu_custom_call" | custom-call | flops 3355443 | bytes 52428 | tf_op jit(solution)/shard_map/pallas_call | solution.py:236
  140.8 6.7 shard_map.205
  149.6 4.0 shard_map.206
  153.6 6.6 collective-permute-start.3
  160.2 4.0 shard_map.207
  167.9 33.6 %collective-permute-done.1 = bf16[640,2048]{1,0:T(8,128)(2,1)} collective-permute-done((bf16[640,2048]{1,0:T(8,128)(2,1)}, bf16[640,2048]{1,0:T(8,128)(2,1)}, u32[]{:S(2)}, u32[]{:S(2)}) %collective-permute-start.1) | collective-permute-done | bytes 2621472 | tf_op jit(solution)/shard_map/ppermute | solution.py:568
  201.5 3.8 multiply_reduce_fusion
  211.9 37.4 %shard_map.208 = (bf16[640,3072]{1,0:T(8,128)(2,1)}, bf16[640,1536]{1,0:T(8,128)(2,1)}, f32[640,2048]{1,0:T(8,128)}, f32[640,2048]{1,0:T(8,128)}) custom-call(bf16[640,2048]{1,0:T(8,128)(2,1)} %multiply_convert_fusion.h_ref.refs_0_, bf16[640,2048]{1,0:T(8,128)(2,1)} %dm_ref.9, bf16[2048,4608]{1,0:T(8,128)(2,1)} %all-gather.8.cloned.1.call-done.wgu_ref.wd_ref, ...), custom_call_target="tpu_custom_call" | custom-call | flops 241591904 | bytes 503316 | tf_op jit(solution)/shard_map/pallas_call | solution.py:369
  249.3 4.6 collective-permute-start.7
  254.0 4.1 shard_map.209
  258.5 6.9 collective-permute-done.6.left_got_ref
  266.4 8.9 %shard_map.210 = (bf16[512,1536]{1,0:T(8,128)(2,1)}, bf16[512,1536]{1,0:T(8,128)(2,1)}) custom-call(bf16[1024,640]{1,0:T(8,128)(2,1)} %get-tuple-element.63.left_ref, bf16[1024,640]{1,0:T(8,128)(2,1)} %copy-done.2, bf16[640,3072]{1,0:T(8,128)(2,1)} %get-tuple-element.65.refs_0_, bf16[640,3072]{1,0:T(8,128)(2,1)} %collective-permute-done.7.refs_1_), custom_call_target="tpu_custom_call" | custom-call | flops 40265320 | bytes 96993 | tf_op jit(solution)/shard_map/pallas_call | solution.py:429
  275.3 8.7 %shard_map.211.refs_2_ = bf16[1024,1536]{1,0:T(8,128)(2,1)} custom-call(bf16[1024,640]{1,0:T(8,128)(2,1)} %get-tuple-element.66.left_ref, bf16[1024,640]{1,0:T(8,128)(2,1)} %copy-done.3, bf16[640,1536]{1,0:T(8,128)(2,1)} %get-tuple-element.67.refs_0_, bf16[640,1536]{1,0:T(8,128)(2,1)} %collective-permute-done.8.refs_1_, ...), custom_call_target="tpu_custom_call" | custom-call | flops 40265320 | bytes 96993 | tf_op jit(solution)/shard_map/pallas_call | solution.py:429
  284.0 8.6 %collective-permute-start.9 = (bf16[512,1536]{1,0:T(8,128)(2,1)}, bf16[512,1536]{1,0:T(8,128)(2,1)}, u32[]{:S(2)}, u32[]{:S(2)}) collective-permute-start(bf16[512,1536]{1,0:T(8,128)(2,1)} %get-tuple-element.69.refs_3_), channel_id=1, source_target_pairs={{0,4},{2,6},{4,0},{6,2},{8,12},{10,14},{12,8},{14,10},{16,20},{18,... | collective-permute-start | bytes 4718600 | tf_op jit(solution)/shard_map/ppermute | solution.py:101
  292.6 8.5 %shard_map.212 = (bf16[512,1536]{1,0:T(8,128)(2,1)}, bf16[512,1536]{1,0:T(8,128)(2,1)}) custom-call(bf16[1024,640]{1,0:T(8,128)(2,1)} %get-tuple-element.63.left_ref, bf16[1024,640]{1,0:T(8,128)(2,1)} %copy-done.2, bf16[640,3072]{1,0:T(8,128)(2,1)} %get-tuple-element.65.refs_0_, bf16[640,3072]{1,0:T(8,128)(2,1)} %collective-permute-done.7.refs_1_, ...), custom_call_target="tpu_custom_call" | custom-call | flops 40265320 | bytes 96993 | tf_op jit(solution)/shard_map/pallas_call | solution.py:429
  301.1 18.7 %all-gather.6.cloned.1.call-done.wgu_ref.wd_ref = bf16[2048,4224]{1,0:T(8,128)(2,1)} async-done(((bf16[128,4224]{1,0:T(8,128)(2,1)}), bf16[2048,4224]{1,0:T(8,128)(2,1)}) %all-gather.6.cloned.1.call-update) | async-done | bytes 17301520 | tf_op jit(solution)/shard_map/all_gather | solution.py:504
  319.8 22.7 %shard_map.213 = (bf16[384,2560]{1,0:T(8,128)(2,1)}, bf16[384,1280]{1,0:T(8,128)(2,1)}, bf16[384,2048]{1,0:T(8,128)(2,1)}, bf16[384,2048]{1,0:T(8,128)(2,1)}) custom-call(bf16[640,2048]{1,0:T(8,128)(2,1)} %multiply_convert_fusion.h_ref.refs_0_, bf16[640,2048]{1,0:T(8,128)(2,1)} %dm_ref.9, bf16[2048,4224]{1,0:T(8,128)(2,1)} %all-gather.6.cloned.1.call-done.wgu_ref.wd_ref, ...), custom_call_target="tpu_custom_call" | custom-call | flops 120795952 | bytes 346030 | tf_op jit(solution)/shard_map/pallas_call | solution.py:369
  342.5 3.0 shard_map.214.refs_2_
  347.1 18.0 %shard_map.215 = (bf16[256,2560]{1,0:T(8,128)(2,1)}, bf16[256,1280]{1,0:T(8,128)(2,1)}, bf16[256,2048]{1,0:T(8,128)(2,1)}, bf16[256,2048]{1,0:T(8,128)(2,1)}) custom-call(bf16[640,2048]{1,0:T(8,128)(2,1)} %multiply_convert_fusion.h_ref.refs_0_, bf16[640,2048]{1,0:T(8,128)(2,1)} %dm_ref.9, bf16[2048,4224]{1,0:T(8,128)(2,1)} %all-gather.6.cloned.1.call-done.wgu_ref.wd_ref, ...), custom_call_target="tpu_custom_call" | custom-call | flops 80530640 | bytes 283115 | tf_op jit(solution)/shard_map/pallas_call | solution.py:369
  366.1 16.3 %reduce-scatter.8.cloned.1.call-done = bf16[256,1536]{1,0:T(8,128)(2,1)} async-done(((bf16[1024,1536]{1,0:T(8,128)(2,1)}), bf16[256,1536]{1,0:T(8,128)(2,1)}) %reduce-scatter.8.cloned.1.call-update) | async-done | bytes 786448 | tf_op jit(solution)/shard_map/reduce_scatter | solution.py:107
  387.1 9.6 %shard_map.216 = (f32[384,2048]{1,0:T(8,128)}, bf16[384,2048]{1,0:T(8,128)(2,1)}, bf16[384,1024]{1,0:T(8,128)(2,1)}, f32[1,2048]{1,0:T(1,128)}) custom-call(bf16[384,2048]{1,0:T(8,128)(2,1)} %get-tuple-element.75.own_ref, bf16[384,2048]{1,0:T(8,128)(2,1)} %collective-permute-done.10.got_ref, f32[640,2048]{1,0:T(8,128)} %copy-done, bf16[640,2048]{1,0:T(8,128)(2,1)} %dm_ref.9, ...), custom_call_target="tpu_custom_call" | custom-call | flops 16106127 | bytes 167772 | tf_op jit(solution)/shard_map/pallas_call | solution.py:472
  398.9 8.4 %shard_map.217 = (bf16[512,1280]{1,0:T(8,128)(2,1)}, bf16[512,1280]{1,0:T(8,128)(2,1)}) custom-call(bf16[1024,640]{1,0:T(8,128)(2,1)} %get-tuple-element.63.left_ref, bf16[1024,640]{1,0:T(8,128)(2,1)} %copy-done.2, bf16[384,2560]{1,0:T(8,128)(2,1)} %get-tuple-element.73.refs_0_, bf16[256,2560]{1,0:T(8,128)(2,1)} %get-tuple-element.76.refs_0_.refs_1_, ...), custom_call_target="tpu_custom_call" | custom-call | flops 33554432 | bytes 85196 | tf_op jit(solution)/shard_map/pallas_call | solution.py:429
  407.3 3.4 collective-permute-done.15
  413.4 7.1 %shard_map.218 = (f32[256,2048]{1,0:T(8,128)}, bf16[256,2048]{1,0:T(8,128)(2,1)}, bf16[256,1024]{1,0:T(8,128)(2,1)}, f32[1,2048]{1,0:T(1,128)}) custom-call(bf16[256,2048]{1,0:T(8,128)(2,1)} %get-tuple-element.78.own_ref, bf16[256,2048]{1,0:T(8,128)(2,1)} %collective-permute-done.11.got_ref, f32[640,2048]{1,0:T(8,128)} %copy-done, bf16[640,2048]{1,0:T(8,128)(2,1)} %dm_ref.9, ...), custom_call_target="tpu_custom_call" | custom-call | flops 10737418 | bytes 125829 | tf_op jit(solution)/shard_map/pallas_call | solution.py:472
  420.6 3.0 shard_map.219.refs_4_
  425.4 8.5 %shard_map.220 = (bf16[512,1280]{1,0:T(8,128)(2,1)}, bf16[512,1280]{1,0:T(8,128)(2,1)}) custom-call(bf16[1024,640]{1,0:T(8,128)(2,1)} %get-tuple-element.63.left_ref, bf16[1024,640]{1,0:T(8,128)(2,1)} %copy-done.2, bf16[384,2560]{1,0:T(8,128)(2,1)} %get-tuple-element.73.refs_0_, bf16[256,2560]{1,0:T(8,128)(2,1)} %get-tuple-element.76.refs_0_.refs_1_, ...), custom_call_target="tpu_custom_call" | custom-call | flops 33554432 | bytes 85196 | tf_op jit(solution)/shard_map/pallas_call | solution.py:429
  433.9 3.9 shard_map.221
  437.8 13.1 %shard_map.222 = (bf16[640,1024]{1,0:T(8,128)(2,1)}, bf16[640,2048]{1,0:T(8,128)(2,1)}) custom-call(bf16[640,3072]{1,0:T(8,128)(2,1)} %shard_map.203.q_ref.k_ref.v_ref, bf16[640,3072]{1,0:T(8,128)(2,1)} %shard_map.203.q_ref.k_ref.v_ref, bf16[640,3072]{1,0:T(8,128)(2,1)} %shard_map.203.q_ref.k_ref.v_ref, bf16[64,2048]{1,0:T(8,128)(2,1)} %copy-done.7, ...), custom_call_target="tpu_custom_call" | custom-call | flops 8388608 | bytes 91750 | tf_op jit(solution)/shard_map/pallas_call | solution.py:252
  450.9 3.6 collective-permute-done.23.got_ref
  464.4 8.5 %shard_map.224 = (bf16[512,1280]{1,0:T(8,128)(2,1)}, bf16[512,1280]{1,0:T(8,128)(2,1)}) custom-call(bf16[1024,640]{1,0:T(8,128)(2,1)} %get-tuple-element.66.left_ref, bf16[1024,640]{1,0:T(8,128)(2,1)} %copy-done.3, bf16[384,1280]{1,0:T(8,128)(2,1)} %get-tuple-element.94.refs_0_, bf16[256,1280]{1,0:T(8,128)(2,1)} %get-tuple-element.95.refs_1_, ...), custom_call_target="tpu_custom_call" | custom-call | flops 33554432 | bytes 85196 | tf_op jit(solution)/shard_map/pallas_call | solution.py:429
  472.9 14.3 %collective-permute-done.20.got_ref = bf16[512,1280]{1,0:T(8,128)(2,1)S(1)} collective-permute-done((bf16[512,1280]{1,0:T(8,128)(2,1)}, bf16[512,1280]{1,0:T(8,128)(2,1)S(1)}, u32[]{:S(2)}, u32[]{:S(2)}) %collective-permute-start.20) | collective-permute-done | bytes 1310752 | tf_op jit(solution)/shard_map/ppermute | solution.py:101
  492.9 6.6 shard_map.226
  499.8 10.3 %shard_map.227 = (bf16[512,2048]{1,0:T(8,128)(2,1)}, bf16[512,2048]{1,0:T(8,128)(2,1)}) custom-call(bf16[1024,640]{1,0:T(8,128)(2,1)} %get-tuple-element.93.left_ref, bf16[1024,640]{1,0:T(8,128)(2,1)} %collective-permute-done.4.refs_2_.left_got_ref, bf16[640,2048]{1,0:T(8,128)(2,1)} %get-tuple-element.92.refs_0_.refs_1_, ...), custom_call_target="tpu_custom_call" | custom-call | flops 53687092 | bytes 120586 | tf_op jit(solution)/shard_map/pallas_call | solution.py:429
  510.1 13.0 %shard_map.228.refs_2_ = bf16[640,2048]{1,0:T(8,128)(2,1)} custom-call(bf16[640,1024]{1,0:T(8,128)(2,1)} %get-tuple-element.91.refs_0_, bf16[640,2048]{1,0:T(8,128)(2,1)} %get-tuple-element.92.refs_0_.refs_1_, bf16[2048,4224]{1,0:T(8,128)(2,1)} %all-gather.4.cloned.1.call-done.refs_1_.wo_ref.refs_2_, bf16[512,2048]{1,0:T(8,128)(2,1)} %get-tuple-element.100.refs_3_.keep_ref, ...), custom_call_target="tpu_custom_call" | custom-call | flops 80530640 | bytes 191365 | tf_op jit(solution)/shard_map/pallas_call | solution.py:290
  523.1 6.7 shard_map.229
  532.5 12.6 %collective-permute-done.33.got_ref = bf16[512,1024]{1,0:T(8,128)(2,1)} collective-permute-done((bf16[512,1024]{1,0:T(8,128)(2,1)}, bf16[512,1024]{1,0:T(8,128)(2,1)}, u32[]{:S(2)}, u32[]{:S(2)}) %collective-permute-start.33) | collective-permute-done | bytes 1048608 | tf_op jit(solution)/shard_map/ppermute | solution.py:101
  556.4 7.0 %add_convert_fusion = bf16[640,2048]{1,0:T(8,128)(2,1)} fusion(f32[640,2048]{1,0:T(8,128)} %copy-done, bf16[640,2048]{1,0:T(8,128)(2,1)} %collective-permute-done.17.refs_2_, bf16[640,2048]{1,0:T(8,128)(2,1)} %constant_dynamic-update-slice_fusion.1), kind=kLoop, calls=%fused_computation.17 | loop fusion | flops 6553600 | bytes 13107200 | tf_op jit(solution)/shard_map/convert_element_type | solution.py:667
  565.7 44.1 %collective-permute-done.24.refs_2_ = bf16[640,2048]{1,0:T(8,128)(2,1)} collective-permute-done((bf16[640,2048]{1,0:T(8,128)(2,1)}, bf16[640,2048]{1,0:T(8,128)(2,1)}, u32[]{:S(2)}, u32[]{:S(2)}) %collective-permute-start.24) | collective-permute-done | bytes 2621472 | tf_op jit(solution)/shard_map/ppermute | solution.py:568
  609.7 4.5 fusion.11
  616.3 3.4 shard_map.232.refs_0_
  624.8 3.0 copy.95
  631.7 3.0 collective-permute-start.29
  636.3 6.0 fusion.10
  650.1 2.9 collective-permute-start.38
  655.7 8.4 %collective-permute-done.36 = bf16[128,1024]{0,1:T(8,128)(2,1)} collective-permute-done((bf16[128,1024]{0,1:T(8,128)(2,1)S(1)}, bf16[128,1024]{0,1:T(8,128)(2,1)}, u32[]{:S(2)}, u32[]{:S(2)}) %collective-permute-start.36) | collective-permute-done | bytes 262176 | tf_op jit(solution)/shard_map/ppermute | solution.py:118
  664.1 15.1 %collective-permute-done.37 = bf16[128,1024]{0,1:T(8,128)(2,1)} collective-permute-done((bf16[128,1024]{0,1:T(8,128)(2,1)}, bf16[128,1024]{0,1:T(8,128)(2,1)}, u32[]{:S(2)}, u32[]{:S(2)}) %collective-permute-start.37) | collective-permute-done | bytes 262176 | tf_op jit(solution)/shard_map/ppermute | solution.py:118
  (235 shorter events, 115.6 us)
Async XLA Ops:
  7.2 99.9 %all-gather.4.cloned.1.call-start = ((), (), s32[]{:S(2)}) async-start(), calls=%async_computation.7 | async-start | bytes 18382848 | tf_op jit(solution)/shard_map/all_gather | solution.py:504
  12.7 199.2 %all-gather.8.cloned.1.call-start = ((), (), s32[]{:S(2)}) async-start(), calls=%async_computation.9 | async-start | bytes 20054016 | tf_op jit(solution)/shard_map/all_gather | solution.py:504
  17.8 302.0 %all-gather.6.cloned.1.call-start = ((), (), s32[]{:S(2)}) async-start(), calls=%async_computation.8 | async-start | bytes 18382848 | tf_op jit(solution)/shard_map/all_gather | solution.py:504
  23.4 359.0 %reduce-scatter.8.cloned.1.call-start = ((), (), s32[]{:S(2)}) async-start(), calls=%async_computation.10 | async-start | bytes 3932160 | tf_op jit(solution)/shard_map/reduce_scatter | solution.py:107
  126.0 5.3 collective-permute-start
  147.5 53.9 %collective-permute-start.1 = (bf16[640,2048]{1,0:T(8,128)(2,1)}, bf16[640,2048]{1,0:T(8,128)(2,1)}, u32[]{:S(2)}, u32[]{:S(2)}) collective-permute-start(bf16[640,2048]{1,0:T(8,128)(2,1)} %shard_map.205), channel_id=1, source_target_pairs={{0,1},{1,0},{2,3},{3,2},{4,5},{5,4},{6,7},{7,6},{8,9},{9,8},{10,11... | collective-permute-start | bytes 7864328 | tf_op jit(solution)/shard_map/ppermute | solution.py:568
  153.6 54.8 %collective-permute-start.3 = (bf16[1024,640]{1,0:T(8,128)(2,1)}, bf16[1024,640]{1,0:T(8,128)(2,1)S(1)}, u32[]{:S(2)}, u32[]{:S(2)}) collective-permute-start(bf16[1024,640]{1,0:T(8,128)(2,1)} %get-tuple-element.59), channel_id=1, source_target_pairs={{0,2},{2,0},{4,6},{6,4},{8,10},{10,8},{12,14},{14,12},{16,18},{18,... | collective-permute-start | bytes 3932168 | tf_op jit(solution)/shard_map/ppermute | solution.py:97
  165.3 44.9 %collective-permute-start.4 = (bf16[1024,640]{1,0:T(8,128)(2,1)}, bf16[1024,640]{1,0:T(8,128)(2,1)}, u32[]{:S(2)}, u32[]{:S(2)}) collective-permute-start(bf16[1024,640]{1,0:T(8,128)(2,1)} %get-tuple-element.60), channel_id=1, source_target_pairs={{0,2},{2,0},{4,6},{6,4},{8,10},{10,8},{12,14},{14,12},{16,18},{18,... | collective-permute-start | bytes 3932168 | tf_op jit(solution)/shard_map/ppermute | solution.py:97
  165.4 44.0 %collective-permute-start.5 = (bf16[64,3072]{1,0:T(8,128)(2,1)S(1)}, bf16[64,3072]{1,0:T(8,128)(2,1)S(1)}, u32[]{:S(2)}, u32[]{:S(2)}) collective-permute-start(bf16[64,3072]{1,0:T(8,128)(2,1)S(1)} %slice.195), channel_id=1, source_target_pairs={{2,0},{4,2},{6,4},{8,6},{10,8},{12,10},{14,12},{16,14},{18,16},{20... | collective-permute-start | bytes 1179656 | tf_op jit(solution)/shard_map/ppermute | solution.py:576
  166.7 43.5 %collective-permute-start.2 = (bf16[640,1024]{1,0:T(8,128)(2,1)}, bf16[640,1024]{1,0:T(8,128)(2,1)}, u32[]{:S(2)}, u32[]{:S(2)}) collective-permute-start(bf16[640,1024]{1,0:T(8,128)(2,1)} %shard_map.204.refs_0_), channel_id=1, source_target_pairs={{0,2},{2,0},{4,6},{6,4},{8,10},{10,8},{12,14},{14,12},{16,18},{18,... | collective-permute-start | bytes 3932168 | tf_op jit(solution)/shard_map/ppermute | solution.py:97
  249.3 16.0 %collective-permute-start.7 = (bf16[640,3072]{1,0:T(8,128)(2,1)}, bf16[640,3072]{1,0:T(8,128)(2,1)}, u32[]{:S(2)}, u32[]{:S(2)}) collective-permute-start(bf16[640,3072]{1,0:T(8,128)(2,1)} %get-tuple-element.65.refs_0_), channel_id=1, source_target_pairs={{0,2},{2,0},{4,6},{6,4},{8,10},{10,8},{12,14},{14,12},{16,18},{18,... | collective-permute-start | bytes 11796488 | tf_op jit(solution)/shard_map/ppermute | solution.py:97
  253.9 21.3 %collective-permute-start.8 = (bf16[640,1536]{1,0:T(8,128)(2,1)}, bf16[640,1536]{1,0:T(8,128)(2,1)}, u32[]{:S(2)}, u32[]{:S(2)}) collective-permute-start(bf16[640,1536]{1,0:T(8,128)(2,1)} %get-tuple-element.67.refs_0_), channel_id=1, source_target_pairs={{0,2},{2,0},{4,6},{6,4},{8,10},{10,8},{12,14},{14,12},{16,18},{18,... | collective-permute-start | bytes 5898248 | tf_op jit(solution)/shard_map/ppermute | solution.py:97
  258.1 7.2 %collective-permute-start.6 = (bf16[1024,640]{1,0:T(8,128)(2,1)}, bf16[1024,640]{1,0:T(8,128)(2,1)S(1)}, u32[]{:S(2)}, u32[]{:S(2)}) collective-permute-start(bf16[1024,640]{1,0:T(8,128)(2,1)} %get-tuple-element.64), channel_id=1, source_target_pairs={{0,2},{2,0},{4,6},{6,4},{8,10},{10,8},{12,14},{14,12},{16,18},{18,... | collective-permute-start | bytes 3932168 | tf_op jit(solution)/shard_map/ppermute | solution.py:97
  284.0 170.5 %reduce-scatter.10.cloned.1.call-start = ((), (), s32[]{:S(2)}) async-start(), calls=%async_computation.11 | async-start | bytes 1966080 | tf_op jit(solution)/shard_map/reduce_scatter | solution.py:107
  284.0 58.5 %collective-permute-start.9 = (bf16[512,1536]{1,0:T(8,128)(2,1)}, bf16[512,1536]{1,0:T(8,128)(2,1)}, u32[]{:S(2)}, u32[]{:S(2)}) collective-permute-start(bf16[512,1536]{1,0:T(8,128)(2,1)} %get-tuple-element.69.refs_3_), channel_id=1, source_target_pairs={{0,4},{2,6},{4,0},{6,2},{8,12},{10,14},{12,8},{14,10},{16,20},{18,... | collective-permute-start | bytes 4718600 | tf_op jit(solution)/shard_map/ppermute | solution.py:101
  345.5 154.3 %reduce-scatter.12.cloned.1.call-start = ((), (), s32[]{:S(2)}) async-start(), calls=%async_computation.12 | async-start | bytes 1966080 | tf_op jit(solution)/shard_map/reduce_scatter | solution.py:107
  345.5 52.0 %collective-permute-start.12 = (bf16[384,2560]{1,0:T(8,128)(2,1)}, bf16[384,2560]{1,0:T(8,128)(2,1)}, u32[]{:S(2)}, u32[]{:S(2)}) collective-permute-start(bf16[384,2560]{1,0:T(8,128)(2,1)} %get-tuple-element.73.refs_0_), channel_id=1, source_target_pairs={{0,2},{2,0},{4,6},{6,4},{8,10},{10,8},{12,14},{14,12},{16,18},{18,... | collective-permute-start | bytes 5898248 | tf_op jit(solution)/shard_map/ppermute | solution.py:97
  345.9 37.5 %collective-permute-start.10 = (bf16[384,2048]{1,0:T(8,128)(2,1)}, bf16[384,2048]{1,0:T(8,128)(2,1)}, u32[]{:S(2)}, u32[]{:S(2)}) collective-permute-start(bf16[384,2048]{1,0:T(8,128)(2,1)} %get-tuple-element.75.own_ref), channel_id=1, source_target_pairs={{0,1},{1,0},{2,3},{3,2},{4,5},{5,4},{6,7},{7,6},{8,9},{9,8},{10,11... | collective-permute-start | bytes 4718600 | tf_op jit(solution)/shard_map/ppermute | solution.py:568
  365.1 33.8 %collective-permute-start.13 = (bf16[256,2560]{1,0:T(8,128)(2,1)}, bf16[256,2560]{1,0:T(8,128)(2,1)}, u32[]{:S(2)}, u32[]{:S(2)}) collective-permute-start(bf16[256,2560]{1,0:T(8,128)(2,1)} %get-tuple-element.76.refs_0_.refs_1_), channel_id=1, source_target_pairs={{0,2},{2,0},{4,6},{6,4},{8,10},{10,8},{12,14},{14,12},{16,18},{18,... | collective-permute-start | bytes 3932168 | tf_op jit(solution)/shard_map/ppermute | solution.py:97
  365.2 55.4 %collective-permute-start.16 = (bf16[512,1536]{1,0:T(8,128)(2,1)}, bf16[512,1536]{1,0:T(8,128)(2,1)}, u32[]{:S(2)}, u32[]{:S(2)}) collective-permute-start(bf16[512,1536]{1,0:T(8,128)(2,1)} %get-tuple-element.71.refs_3_), channel_id=1, source_target_pairs={{0,4},{2,6},{4,0},{6,2},{8,12},{10,14},{12,8},{14,10},{16,20},{18,... | collective-permute-start | bytes 4718600 | tf_op jit(solution)/shard_map/ppermute | solution.py:101
  365.3 47.5 %collective-permute-start.11 = (bf16[256,2048]{1,0:T(8,128)(2,1)}, bf16[256,2048]{1,0:T(8,128)(2,1)}, u32[]{:S(2)}, u32[]{:S(2)}) collective-permute-start(bf16[256,2048]{1,0:T(8,128)(2,1)} %get-tuple-element.78.own_ref), channel_id=1, source_target_pairs={{0,1},{1,0},{2,3},{3,2},{4,5},{5,4},{6,7},{7,6},{8,9},{9,8},{10,11... | collective-permute-start | bytes 3145736 | tf_op jit(solution)/shard_map/ppermute | solution.py:568
  383.4 27.3 %collective-permute-start.15 = (bf16[128,1536]{1,0:T(8,128)(2,1)S(1)}, bf16[128,1536]{1,0:T(8,128)(2,1)}, u32[]{:S(2)}, u32[]{:S(2)}) collective-permute-start(bf16[128,1536]{1,0:T(8,128)(2,1)S(1)} %slice.197), channel_id=1, source_target_pairs={{0,4},{2,6},{4,0},{6,2},{8,12},{10,14},{12,8},{14,10},{16,20},{18,... | collective-permute-start | bytes 1179656 | tf_op jit(solution)/shard_map/ppermute | solution.py:101
  397.6 15.1 %collective-permute-start.14 = (bf16[64,1024]{1,0:T(8,128)(2,1)S(1)}, bf16[64,1024]{1,0:T(8,128)(2,1)S(1)}, u32[]{:S(2)}, u32[]{:S(2)}) collective-permute-start(bf16[64,1024]{1,0:T(8,128)(2,1)S(1)} %slice.156), channel_id=1, source_target_pairs={{2,0},{4,2},{6,4},{8,6},{10,8},{12,10},{14,12},{16,14},{18,16},{20... | collective-permute-start | bytes 393224 | tf_op jit(solution)/shard_map/ppermute | solution.py:613
  423.6 99.5 %reduce-scatter.14.cloned.1.call-start = ((), (), s32[]{:S(2)}) async-start(), calls=%async_computation.13 | async-start | bytes 1638400 | tf_op jit(solution)/shard_map/reduce_scatter | solution.py:107
  423.7 30.8 %collective-permute-start.23 = (bf16[512,1280]{1,0:T(8,128)(2,1)}, bf16[512,1280]{1,0:T(8,128)(2,1)}, u32[]{:S(2)}, u32[]{:S(2)}) collective-permute-start(bf16[512,1280]{1,0:T(8,128)(2,1)} %get-tuple-element.80.refs_1_), channel_id=1, source_target_pairs={{0,4},{2,6},{4,0},{6,2},{8,12},{10,14},{12,8},{14,10},{16,20},{18,... | collective-permute-start | bytes 3932168 | tf_op jit(solution)/shard_map/ppermute | solution.py:101
  457.2 106.8 %reduce-scatter.18.cloned.1.call-start = ((), (), s32[]{:S(2)}) async-start(), calls=%async_computation.15 | async-start | bytes 1638400 | tf_op jit(solution)/shard_map/reduce_scatter | solution.py:107
  457.3 29.9 %collective-permute-start.20 = (bf16[512,1280]{1,0:T(8,128)(2,1)}, bf16[512,1280]{1,0:T(8,128)(2,1)S(1)}, u32[]{:S(2)}, u32[]{:S(2)}) collective-permute-start(bf16[512,1280]{1,0:T(8,128)(2,1)} %get-tuple-element.84.refs_3_), channel_id=1, source_target_pairs={{0,4},{2,6},{4,0},{6,2},{8,12},{10,14},{12,8},{14,10},{16,20},{18,... | collective-permute-start | bytes 3932168 | tf_op jit(solution)/shard_map/ppermute | solution.py:101
  459.1 5.1 collective-permute-start.21
  459.1 5.3 collective-permute-start.22
  459.6 40.2 %collective-permute-start.18 = (bf16[640,2048]{1,0:T(8,128)(2,1)}, bf16[640,2048]{1,0:T(8,128)(2,1)}, u32[]{:S(2)}, u32[]{:S(2)}) collective-permute-start(bf16[640,2048]{1,0:T(8,128)(2,1)} %get-tuple-element.92.refs_0_.refs_1_), channel_id=1, source_target_pairs={{0,2},{2,0},{4,6},{6,4},{8,10},{10,8},{12,14},{14,12},{16,18},{18,... | collective-permute-start | bytes 7864328 | tf_op jit(solution)/shard_map/ppermute | solution.py:97
  463.4 66.3 %collective-permute-start.17 = (bf16[640,2048]{1,0:T(8,128)(2,1)}, bf16[640,2048]{1,0:T(8,128)(2,1)}, u32[]{:S(2)}, u32[]{:S(2)}) collective-permute-start(bf16[640,2048]{1,0:T(8,128)(2,1)} %constant_dynamic-update-slice_fusion.1), channel_id=1, source_target_pairs={{0,1},{1,0},{2,3},{3,2},{4,5},{5,4},{6,7},{7,6},{8,9},{9,8},{10,11... | collective-permute-start | bytes 7864328 | tf_op jit(solution)/shard_map/ppermute | solution.py:568
  464.2 28.7 %collective-permute-start.19 = (bf16[640,1024]{1,0:T(8,128)(2,1)}, bf16[640,1024]{1,0:T(8,128)(2,1)}, u32[]{:S(2)}, u32[]{:S(2)}) collective-permute-start(bf16[640,1024]{1,0:T(8,128)(2,1)} %get-tuple-element.91.refs_0_), channel_id=1, source_target_pairs={{0,2},{2,0},{4,6},{6,4},{8,10},{10,8},{12,14},{14,12},{16,18},{18,... | collective-permute-start | bytes 3932168 | tf_op jit(solution)/shard_map/ppermute | solution.py:97
  490.9 152.0 %reduce-scatter.16.cloned.1.call-start = ((), (), s32[]{:S(2)}) async-start(), calls=%async_computation.14 | async-start | bytes 2949120 | tf_op jit(solution)/shard_map/reduce_scatter | solution.py:107
  491.0 32.1 %collective-permute-start.32 = (bf16[1024,640]{1,0:T(8,128)(2,1)}, bf16[1024,640]{1,0:T(8,128)(2,1)}, u32[]{:S(2)}, u32[]{:S(2)}) collective-permute-start(bf16[1024,640]{1,0:T(8,128)(2,1)} %get-tuple-element.104), channel_id=1, source_target_pairs={{0,2},{2,0},{4,6},{6,4},{8,10},{10,8},{12,14},{14,12},{16,18},{18,... | collective-permute-start | bytes 3932168 | tf_op jit(solution)/shard_map/ppermute | solution.py:97
  491.1 38.7 %collective-permute-start.31 = (bf16[512,1280]{1,0:T(8,128)(2,1)}, bf16[512,1280]{1,0:T(8,128)(2,1)}, u32[]{:S(2)}, u32[]{:S(2)}) collective-permute-start(bf16[512,1280]{1,0:T(8,128)(2,1)} %get-tuple-element.97.refs_1_), channel_id=1, source_target_pairs={{0,4},{2,6},{4,0},{6,2},{8,12},{10,14},{12,8},{14,10},{16,20},{18,... | collective-permute-start | bytes 3932168 | tf_op jit(solution)/shard_map/ppermute | solution.py:101
  499.5 45.6 %collective-permute-start.33 = (bf16[512,1024]{1,0:T(8,128)(2,1)}, bf16[512,1024]{1,0:T(8,128)(2,1)}, u32[]{:S(2)}, u32[]{:S(2)}) collective-permute-start(bf16[512,1024]{1,0:T(8,128)(2,1)} %get-tuple-element.99.refs_3_), channel_id=1, source_target_pairs={{0,4},{2,6},{4,0},{6,2},{8,12},{10,14},{12,8},{14,10},{16,20},{18,... | collective-permute-start | bytes 3145736 | tf_op jit(solution)/shard_map/ppermute | solution.py:101
  550.6 130.6 %reduce-scatter.20.cloned.1.call-start = ((), (), s32[]{:S(2)}) async-start(), calls=%async_computation.16 | async-start | bytes 2621440 | tf_op jit(solution)/shard_map/reduce_scatter | solution.py:107
  550.9 58.8 %collective-permute-start.24 = (bf16[640,2048]{1,0:T(8,128)(2,1)}, bf16[640,2048]{1,0:T(8,128)(2,1)}, u32[]{:S(2)}, u32[]{:S(2)}) collective-permute-start(bf16[640,2048]{1,0:T(8,128)(2,1)} %shard_map.228.refs_2_), channel_id=1, source_target_pairs={{0,1},{1,0},{2,3},{3,2},{4,5},{5,4},{6,7},{7,6},{8,9},{9,8},{10,11... | collective-permute-start | bytes 7864328 | tf_op jit(solution)/shard_map/ppermute | solution.py:568
  554.6 61.7 %collective-permute-start.34 = (bf16[512,2048]{1,0:T(8,128)(2,1)}, bf16[512,2048]{1,0:T(8,128)(2,1)}, u32[]{:S(2)}, u32[]{:S(2)}) collective-permute-start(bf16[512,2048]{1,0:T(8,128)(2,1)} %get-tuple-element.101.refs_4_), channel_id=1, source_target_pairs={{0,4},{2,6},{4,0},{6,2},{8,12},{10,14},{12,8},{14,10},{16,20},{18,... | collective-permute-start | bytes 6291464 | tf_op jit(solution)/shard_map/ppermute | solution.py:101
  563.4 79.5 %collective-permute-start.35 = (bf16[512,1024]{1,0:T(8,128)(2,1)}, bf16[512,1024]{1,0:T(8,128)(2,1)}, u32[]{:S(2)}, u32[]{:S(2)}) collective-permute-start(bf16[512,1024]{1,0:T(8,128)(2,1)} %get-tuple-element.106.refs_1_), channel_id=1, source_target_pairs={{0,4},{2,6},{4,0},{6,2},{8,12},{10,14},{12,8},{14,10},{16,20},{18,... | collective-permute-start | bytes 3145736 | tf_op jit(solution)/shard_map/ppermute | solution.py:101
  614.3 5.5 collective-permute-start.25
  620.6 7.3 %collective-permute-start.26 = (f32[8,2,128]{2,1,0:T(2,128)S(1)}, f32[8,2,128]{2,1,0:T(2,128)S(1)}, u32[]{:S(2)}, u32[]{:S(2)}) collective-permute-start(f32[8,2,128]{2,1,0:T(2,128)S(1)} %slice.199), channel_id=1, source_target_pairs={{0,2},{2,0},{4,6},{6,4},{8,10},{10,8},{12,14},{14,12},{16,18},{18,... | collective-permute-start | bytes 24584 | tf_op jit(solution)/shard_map/ppermute | solution.py:97
  631.6 10.8 %collective-permute-start.28 = (f32[2,128]{1,0:T(2,128)S(1)}, f32[2,128]{1,0:T(2,128)S(1)}, u32[]{:S(2)}, u32[]{:S(2)}) collective-permute-start(f32[2,128]{1,0:T(2,128)S(1)} %get-tuple-element.183), channel_id=1, source_target_pairs={{0,8},{2,10},{4,12},{6,14},{8,16},{10,18},{12,20},{14,22},{16,24},... | collective-permute-start | bytes 3080 | tf_op jit(solution)/shard_map/ppermute | solution.py:159
  631.7 10.6 %collective-permute-start.29 = (f32[2,128]{1,0:T(2,128)S(1)}, f32[2,128]{1,0:T(2,128)S(1)}, u32[]{:S(2)}, u32[]{:S(2)}) collective-permute-start(f32[2,128]{1,0:T(2,128)S(1)} %get-tuple-element.185), channel_id=1, source_target_pairs={{0,16},{2,18},{4,20},{6,22},{8,24},{10,26},{12,28},{14,30},{16,0},... | collective-permute-start | bytes 3080 | tf_op jit(solution)/shard_map/ppermute | solution.py:159
  634.7 7.7 %collective-permute-start.30 = (f32[2,128]{1,0:T(2,128)S(1)}, f32[2,128]{1,0:T(2,128)S(1)}, u32[]{:S(2)}, u32[]{:S(2)}) collective-permute-start(f32[2,128]{1,0:T(2,128)S(1)} %get-tuple-element.184), channel_id=1, source_target_pairs={{0,24},{2,26},{4,28},{6,30},{8,0},{10,2},{12,4},{14,6},{16,8},{18,... | collective-permute-start | bytes 3080 | tf_op jit(solution)/shard_map/ppermute | solution.py:159
  647.2 16.9 %collective-permute-start.36 = (bf16[128,1024]{0,1:T(8,128)(2,1)S(1)}, bf16[128,1024]{0,1:T(8,128)(2,1)}, u32[]{:S(2)}, u32[]{:S(2)}) collective-permute-start(bf16[128,1024]{0,1:T(8,128)(2,1)S(1)} %bitcast.50), channel_id=1, source_target_pairs={{0,8},{2,10},{4,12},{6,14},{8,16},{10,18},{12,20},{14,22},{16,24},... | collective-permute-start | bytes 786440 | tf_op jit(solution)/shard_map/ppermute | solution.py:118
  648.5 30.7 %collective-permute-start.37 = (bf16[128,1024]{0,1:T(8,128)(2,1)}, bf16[128,1024]{0,1:T(8,128)(2,1)}, u32[]{:S(2)}, u32[]{:S(2)}) collective-permute-start(bf16[128,1024]{0,1:T(8,128)(2,1)} %bitcast.20), channel_id=1, source_target_pairs={{0,16},{2,18},{4,20},{6,22},{8,24},{10,26},{12,28},{14,30},{16,0},... | collective-permute-start | bytes 786440 | tf_op jit(solution)/shard_map/ppermute | solution.py:118
  650.1 29.1 %collective-permute-start.38 = (bf16[128,1024]{0,1:T(8,128)(2,1)}, bf16[128,1024]{0,1:T(8,128)(2,1)}, u32[]{:S(2)}, u32[]{:S(2)}) collective-permute-start(bf16[128,1024]{0,1:T(8,128)(2,1)} %bitcast.21), channel_id=1, source_target_pairs={{0,24},{2,26},{4,28},{6,30},{8,0},{10,2},{12,4},{14,6},{16,8},{18,... | collective-permute-start | bytes 786440 | tf_op jit(solution)/shard_map/ppermute | solution.py:118
  (31 other events, 201.8 us)
Sparse Core Ops, SparseCore 0:
  12.8 94.2 all-gather.3
  108.7 103.1 all-gather.7
  213.5 106.3 all-gather.5
  322.0 60.3 reduce-scatter.7
  384.5 36.7 reduce-scatter.9
  423.7 34.1 reduce-scatter.11
  460.3 30.1 reduce-scatter.13
  493.3 29.9 reduce-scatter.17
  550.7 46.6 reduce-scatter.15
  619.9 54.4 reduce-scatter.19

commit v4 on v3

--- a/solution.py
+++ b/solution.py
@@ -636,7 +636,10 @@
     q_part = add_middle(q_part, (two_c,))
     mixed_sum = sum_outer(jnp.concatenate([two_c, q_part], 1))
     down_two, q_sum = mixed_sum[:, :two], mixed_sum[:, two:].astype(F32)
-    kv_part = add_middle(kv_part, (q_part, two_b, own_got))
+    kv_part = add_middle(kv_part, (q_part, two_b))
+    late_done, two_a, two_b, one_a, one_b, _ = lax.optimization_barrier(
+        (late_got, two_a, two_b, one_a, one_b, kv_part)
+    )
     kv_sum = sum_outer(kv_part).astype(F32)
     out_part = add_middle(out_part, (kv_part, mixed_sum))
     out_sum = sum_outer_direct(out_part)
@@ -645,7 +648,7 @@
     grad_gain_one = grad_gain_one + to_mp(grad_gain_one)
     grad_middle = jnp.concatenate([m[0] for m in middles], 0)
     grad_input = grad_middle + norm_back(grad_normed, unit_one, inverse_one, gain_one)
-    result = middle + (late.astype(F32) + late_got.astype(F32))
+    result = middle + (late.astype(F32) + late_done.astype(F32))
     gain_parts = jnp.stack([grad_gain_one, grad_gain_two], 0)
     gain_blocks = jnp.swapaxes(gain_parts.reshape(2, count, -1), 0, 1)
     chosen = order[:, None] == jnp.arange(count, dtype=jnp.int32)[None, :]

time: 703 us -> 691 us (0.983)
  waiting for transfers between devices: 261 us -> 252 us
    ppermute x10, waiting for transfers between devices: 35.7 us -> 81.5 us  [to_middle(): return lax.ppermute(values, 'seq', flip_pairs(lax.axis_size('seq'), 2))]
    ppermute x6, waiting for transfers between devices: 77.7 us -> 35.5 us  [to_mp(): return lax.ppermute(own, 'mp', [(0, 1), (1, 0)])]
    ppermute x3, waiting for transfers between devices: 23.5 us -> 11.4 us  [sum_outer_direct(): lax.ppermute(sent, 'seq', [(s, (s + 4 * step) % count) for s in range(cou...]
    unnamed x76 -> x72, local copies, waits for them, and re-layouts: 28 us -> 28.1 us
  transfers between devices with their start and end apart: 49 -> 49, of which waited for: 14 -> 15; matrix products, arithmetic and copies ran while one was open for 11% -> 11% of each run, Pallas kernels for 38% -> 39%
where the time goes in v4:
time: 691 us; the launch traced here: 678 us
  Pallas kernels  264 us (38%)
  waiting for transfers between devices  252 us (36%)
  starting transfers between devices  54 us (8%)
  local copies, waits for them, and re-layouts  46.1 us (7%)
  other arithmetic  44.5 us (6%)
  between operations  17.8 us (3%)
    all_gather x3, waiting for transfers between devices, gather(): return lax.all_gather(jnp.concatenate(shards, 1), 'seq', axis=0, tiled=True)  100 us
    ppermute x10, waiting for transfers between devices, to_middle(): return lax.ppermute(values, 'seq', flip_pairs(lax.axis_size('seq'), 2))  81.5 us
    pallas_call x3, Pallas kernels, feed_forward(): pl.pallas_call(functools.partial(feed, block, steps, place * 128 if carri...  78.1 us
    pallas_call x9, Pallas kernels, weight_grad(): pl.pallas_call(functools.partial(grad_block, len(right[0]), outers), grid...  75.1 us
    ppermute x6, waiting for transfers between devices, to_mp(): return lax.ppermute(own, 'mp', [(0, 1), (1, 0)])  35.5 us
    pallas_call x3, Pallas kernels, rows_times(): pl.pallas_call(functools.partial(multiply, turned, len(pieces)), grid=(ou...  33.1 us
    unnamed x72, local copies, waits for them, and re-layouts  28.1 us
    pallas_call x8, Pallas kernels, add_middle(): pl.pallas_call(add_block, grid=(columns // wide,), in_specs=[spec] * 2 +...  23.1 us
  transfers between devices with their start and end apart: 49, of which 15 were waited for; matrix products, arithmetic and copies ran while one was open for 11% of the time, Pallas kernels for 39%

profile of v4, /device:TPU:0, one launch (start us, length us, event | category | flops | bytes accessed | tf_op | source)
XLA Modules:
  0.0 678.4 jit_solution(16523122365572729921)
XLA Ops:
  27.3 79.8 %all-gather.4.cloned.1.call-done.refs_1_.wo_ref.refs_2_ = bf16[2048,4224]{1,0:T(8,128)(2,1)} async-done(((bf16[128,4224]{1,0:T(8,128)(2,1)}), bf16[2048,4224]{1,0:T(8,128)(2,1)}) %all-gather.4.cloned.1.call-update) | async-done | bytes 17301520 | tf_op jit(solution)/shard_map/all_gather | solution.py:504
  111.7 13.3 %shard_map.203.q_ref.k_ref.v_ref = bf16[640,3072]{1,0:T(8,128)(2,1)} custom-call(bf16[640,2048]{1,0:T(8,128)(2,1)} %fusion.5.refs_0_, bf16[2048,4224]{1,0:T(8,128)(2,1)} %all-gather.4.cloned.1.call-done.refs_1_.wo_ref.refs_2_), custom_call_target="tpu_custom_call" | custom-call | flops 80530640 | bytes 191365 | tf_op jit(solution)/shard_map/pallas_call | solution.py:290
  131.9 8.9 %shard_map.204.refs_0_ = bf16[640,1024]{1,0:T(8,128)(2,1)} custom-call(bf16[640,3072]{1,0:T(8,128)(2,1)} %shard_map.203.q_ref.k_ref.v_ref, bf16[640,3072]{1,0:T(8,128)(2,1)} %shard_map.203.q_ref.k_ref.v_ref, bf16[640,3072]{1,0:T(8,128)(2,1)} %shard_map.203.q_ref.k_ref.v_ref, bf16[64,2048]{1,0:T(8,128)(2,1)} %copy-done.8, bf16[64,2048]{1,0:T(8,128)(2,1)} %copy-done.8, ...), custom_call_target="tpu_custom_call" | custom-call | flops 3355443 | bytes 52428 | tf_op jit(solution)/shard_map/pallas_call | solution.py:236
  140.8 6.7 shard_map.205
  149.5 4.0 shard_map.206
  153.6 6.6 collective-permute-start.3
  160.2 4.0 shard_map.207
  167.8 33.7 %collective-permute-done.1 = bf16[640,2048]{1,0:T(8,128)(2,1)} collective-permute-done((bf16[640,2048]{1,0:T(8,128)(2,1)}, bf16[640,2048]{1,0:T(8,128)(2,1)}, u32[]{:S(2)}, u32[]{:S(2)}) %collective-permute-start.1) | collective-permute-done | bytes 2621472 | tf_op jit(solution)/shard_map/ppermute | solution.py:568
  201.5 3.8 multiply_reduce_fusion
  211.9 37.5 %shard_map.208 = (bf16[640,3072]{1,0:T(8,128)(2,1)}, bf16[640,1536]{1,0:T(8,128)(2,1)}, f32[640,2048]{1,0:T(8,128)}, f32[640,2048]{1,0:T(8,128)}) custom-call(bf16[640,2048]{1,0:T(8,128)(2,1)} %multiply_convert_fusion.h_ref.refs_0_, bf16[640,2048]{1,0:T(8,128)(2,1)} %dm_ref.9, bf16[2048,4608]{1,0:T(8,128)(2,1)} %all-gather.8.cloned.1.call-done.wgu_ref.wd_ref, ...), custom_call_target="tpu_custom_call" | custom-call | flops 241591904 | bytes 503316 | tf_op jit(solution)/shard_map/pallas_call | solution.py:369
  249.3 4.7 collective-permute-start.7
  254.0 4.1 shard_map.209
  258.5 6.9 %collective-permute-done.6.left_got_ref = bf16[1024,640]{1,0:T(8,128)(2,1)S(1)} collective-permute-done((bf16[1024,640]{1,0:T(8,128)(2,1)}, bf16[1024,640]{1,0:T(8,128)(2,1)S(1)}, u32[]{:S(2)}, u32[]{:S(2)}) %collective-permute-start.6) | collective-permute-done | bytes 1310752 | tf_op jit(solution)/shard_map/ppermute | solution.py:97
  266.4 8.9 %shard_map.210 = (bf16[512,1536]{1,0:T(8,128)(2,1)}, bf16[512,1536]{1,0:T(8,128)(2,1)}) custom-call(bf16[1024,640]{1,0:T(8,128)(2,1)} %get-tuple-element.68.left_ref, bf16[1024,640]{1,0:T(8,128)(2,1)} %copy-done.3, bf16[640,3072]{1,0:T(8,128)(2,1)} %get-tuple-element.70.refs_0_, bf16[640,3072]{1,0:T(8,128)(2,1)} %collective-permute-done.7.refs_1_), custom_call_target="tpu_custom_call" | custom-call | flops 40265320 | bytes 96993 | tf_op jit(solution)/shard_map/pallas_call | solution.py:429
  275.3 8.7 %shard_map.211.refs_2_ = bf16[1024,1536]{1,0:T(8,128)(2,1)} custom-call(bf16[1024,640]{1,0:T(8,128)(2,1)} %get-tuple-element.71.left_ref, bf16[1024,640]{1,0:T(8,128)(2,1)} %copy-done.4, bf16[640,1536]{1,0:T(8,128)(2,1)} %get-tuple-element.72.refs_0_, bf16[640,1536]{1,0:T(8,128)(2,1)} %collective-permute-done.8.refs_1_, ...), custom_call_target="tpu_custom_call" | custom-call | flops 40265320 | bytes 96993 | tf_op jit(solution)/shard_map/pallas_call | solution.py:429
  284.1 8.5 %collective-permute-start.9 = (bf16[512,1536]{1,0:T(8,128)(2,1)}, bf16[512,1536]{1,0:T(8,128)(2,1)}, u32[]{:S(2)}, u32[]{:S(2)}) collective-permute-start(bf16[512,1536]{1,0:T(8,128)(2,1)} %get-tuple-element.74.refs_3_), channel_id=1, source_target_pairs={{0,4},{2,6},{4,0},{6,2},{8,12},{10,14},{12,8},{14,10},{16,20},{18,... | collective-permute-start | bytes 4718600 | tf_op jit(solution)/shard_map/ppermute | solution.py:101
  292.6 8.5 %shard_map.212 = (bf16[512,1536]{1,0:T(8,128)(2,1)}, bf16[512,1536]{1,0:T(8,128)(2,1)}) custom-call(bf16[1024,640]{1,0:T(8,128)(2,1)} %get-tuple-element.68.left_ref, bf16[1024,640]{1,0:T(8,128)(2,1)} %copy-done.3, bf16[640,3072]{1,0:T(8,128)(2,1)} %get-tuple-element.70.refs_0_, bf16[640,3072]{1,0:T(8,128)(2,1)} %collective-permute-done.7.refs_1_, ...), custom_call_target="tpu_custom_call" | custom-call | flops 40265320 | bytes 96993 | tf_op jit(solution)/shard_map/pallas_call | solution.py:429
  301.1 18.8 %all-gather.6.cloned.1.call-done.wgu_ref.wd_ref = bf16[2048,4224]{1,0:T(8,128)(2,1)} async-done(((bf16[128,4224]{1,0:T(8,128)(2,1)}), bf16[2048,4224]{1,0:T(8,128)(2,1)}) %all-gather.6.cloned.1.call-update) | async-done | bytes 17301520 | tf_op jit(solution)/shard_map/all_gather | solution.py:504
  319.8 22.7 %shard_map.213 = (bf16[384,2560]{1,0:T(8,128)(2,1)}, bf16[384,1280]{1,0:T(8,128)(2,1)}, bf16[384,2048]{1,0:T(8,128)(2,1)}, bf16[384,2048]{1,0:T(8,128)(2,1)}) custom-call(bf16[640,2048]{1,0:T(8,128)(2,1)} %multiply_convert_fusion.h_ref.refs_0_, bf16[640,2048]{1,0:T(8,128)(2,1)} %dm_ref.9, bf16[2048,4224]{1,0:T(8,128)(2,1)} %all-gather.6.cloned.1.call-done.wgu_ref.wd_ref, ...), custom_call_target="tpu_custom_call" | custom-call | flops 120795952 | bytes 346030 | tf_op jit(solution)/shard_map/pallas_call | solution.py:369
  342.5 3.0 shard_map.214.refs_2_
  347.1 18.0 %shard_map.215 = (bf16[256,2560]{1,0:T(8,128)(2,1)}, bf16[256,1280]{1,0:T(8,128)(2,1)}, bf16[256,2048]{1,0:T(8,128)(2,1)}, bf16[256,2048]{1,0:T(8,128)(2,1)}) custom-call(bf16[640,2048]{1,0:T(8,128)(2,1)} %multiply_convert_fusion.h_ref.refs_0_, bf16[640,2048]{1,0:T(8,128)(2,1)} %dm_ref.9, bf16[2048,4224]{1,0:T(8,128)(2,1)} %all-gather.6.cloned.1.call-done.wgu_ref.wd_ref, ...), custom_call_target="tpu_custom_call" | custom-call | flops 80530640 | bytes 283115 | tf_op jit(solution)/shard_map/pallas_call | solution.py:369
  366.1 16.3 %reduce-scatter.8.cloned.1.call-done = bf16[256,1536]{1,0:T(8,128)(2,1)} async-done(((bf16[1024,1536]{1,0:T(8,128)(2,1)}), bf16[256,1536]{1,0:T(8,128)(2,1)}) %reduce-scatter.8.cloned.1.call-update) | async-done | bytes 786448 | tf_op jit(solution)/shard_map/reduce_scatter | solution.py:107
  387.1 9.6 %shard_map.216 = (f32[384,2048]{1,0:T(8,128)}, bf16[384,2048]{1,0:T(8,128)(2,1)}, bf16[384,1024]{1,0:T(8,128)(2,1)}, f32[1,2048]{1,0:T(1,128)}) custom-call(bf16[384,2048]{1,0:T(8,128)(2,1)} %get-tuple-element.80.own_ref, bf16[384,2048]{1,0:T(8,128)(2,1)} %collective-permute-done.10.got_ref, f32[640,2048]{1,0:T(8,128)} %copy-done, bf16[640,2048]{1,0:T(8,128)(2,1)} %dm_ref.9, ...), custom_call_target="tpu_custom_call" | custom-call | flops 16106127 | bytes 167772 | tf_op jit(solution)/shard_map/pallas_call | solution.py:472
  398.9 8.4 %shard_map.217 = (bf16[512,1280]{1,0:T(8,128)(2,1)}, bf16[512,1280]{1,0:T(8,128)(2,1)}) custom-call(bf16[1024,640]{1,0:T(8,128)(2,1)} %get-tuple-element.68.left_ref, bf16[1024,640]{1,0:T(8,128)(2,1)} %copy-done.3, bf16[384,2560]{1,0:T(8,128)(2,1)} %get-tuple-element.78.refs_0_, bf16[256,2560]{1,0:T(8,128)(2,1)} %get-tuple-element.81.refs_0_.refs_1_, ...), custom_call_target="tpu_custom_call" | custom-call | flops 33554432 | bytes 85196 | tf_op jit(solution)/shard_map/pallas_call | solution.py:429
  407.3 3.4 collective-permute-done.15
  413.4 7.1 %shard_map.218 = (f32[256,2048]{1,0:T(8,128)}, bf16[256,2048]{1,0:T(8,128)(2,1)}, bf16[256,1024]{1,0:T(8,128)(2,1)}, f32[1,2048]{1,0:T(1,128)}) custom-call(bf16[256,2048]{1,0:T(8,128)(2,1)} %get-tuple-element.83.own_ref, bf16[256,2048]{1,0:T(8,128)(2,1)} %collective-permute-done.11.got_ref, f32[640,2048]{1,0:T(8,128)} %copy-done, bf16[640,2048]{1,0:T(8,128)(2,1)} %dm_ref.9, ...), custom_call_target="tpu_custom_call" | custom-call | flops 10737418 | bytes 125829 | tf_op jit(solution)/shard_map/pallas_call | solution.py:472
  420.6 3.0 shard_map.219.refs_4_
  425.4 8.6 %shard_map.220 = (bf16[512,1280]{1,0:T(8,128)(2,1)}, bf16[512,1280]{1,0:T(8,128)(2,1)}) custom-call(bf16[1024,640]{1,0:T(8,128)(2,1)} %get-tuple-element.68.left_ref, bf16[1024,640]{1,0:T(8,128)(2,1)} %copy-done.3, bf16[384,2560]{1,0:T(8,128)(2,1)} %get-tuple-element.78.refs_0_, bf16[256,2560]{1,0:T(8,128)(2,1)} %get-tuple-element.81.refs_0_.refs_1_, ...), custom_call_target="tpu_custom_call" | custom-call | flops 33554432 | bytes 85196 | tf_op jit(solution)/shard_map/pallas_call | solution.py:429
  433.9 3.9 shard_map.221
  437.8 13.1 %shard_map.222 = (bf16[640,1024]{1,0:T(8,128)(2,1)}, bf16[640,2048]{1,0:T(8,128)(2,1)}) custom-call(bf16[640,3072]{1,0:T(8,128)(2,1)} %shard_map.203.q_ref.k_ref.v_ref, bf16[640,3072]{1,0:T(8,128)(2,1)} %shard_map.203.q_ref.k_ref.v_ref, bf16[640,3072]{1,0:T(8,128)(2,1)} %shard_map.203.q_ref.k_ref.v_ref, bf16[64,2048]{1,0:T(8,128)(2,1)} %copy-done.8, ...), custom_call_target="tpu_custom_call" | custom-call | flops 8388608 | bytes 91750 | tf_op jit(solution)/shard_map/pallas_call | solution.py:252
  450.9 3.5 collective-permute-done.18.got_ref
  464.5 8.5 %shard_map.224 = (bf16[512,1280]{1,0:T(8,128)(2,1)}, bf16[512,1280]{1,0:T(8,128)(2,1)}) custom-call(bf16[1024,640]{1,0:T(8,128)(2,1)} %get-tuple-element.71.left_ref, bf16[1024,640]{1,0:T(8,128)(2,1)} %copy-done.4, bf16[384,1280]{1,0:T(8,128)(2,1)} %get-tuple-element.95.refs_0_, bf16[256,1280]{1,0:T(8,128)(2,1)} %get-tuple-element.96.refs_1_, ...), custom_call_target="tpu_custom_call" | custom-call | flops 33554432 | bytes 85196 | tf_op jit(solution)/shard_map/pallas_call | solution.py:429
  473.0 14.2 %collective-permute-done.19.got_ref = bf16[512,1280]{1,0:T(8,128)(2,1)S(1)} collective-permute-done((bf16[512,1280]{1,0:T(8,128)(2,1)}, bf16[512,1280]{1,0:T(8,128)(2,1)S(1)}, u32[]{:S(2)}, u32[]{:S(2)}) %collective-permute-start.19) | collective-permute-done | bytes 1310752 | tf_op jit(solution)/shard_map/ppermute | solution.py:101
  492.9 6.6 shard_map.226
  499.8 10.3 %shard_map.227 = (bf16[512,2048]{1,0:T(8,128)(2,1)}, bf16[512,2048]{1,0:T(8,128)(2,1)}) custom-call(bf16[1024,640]{1,0:T(8,128)(2,1)} %get-tuple-element.99.left_ref, bf16[1024,640]{1,0:T(8,128)(2,1)} %collective-permute-done.4.refs_2_.left_got_ref, bf16[640,2048]{1,0:T(8,128)(2,1)} %get-tuple-element.100.refs_0_.refs_1_, ...), custom_call_target="tpu_custom_call" | custom-call | flops 53687092 | bytes 120586 | tf_op jit(solution)/shard_map/pallas_call | solution.py:429
  510.1 13.0 %shard_map.228.refs_2_ = bf16[640,2048]{1,0:T(8,128)(2,1)} custom-call(bf16[640,1024]{1,0:T(8,128)(2,1)} %get-tuple-element.94.refs_0_, bf16[640,2048]{1,0:T(8,128)(2,1)} %get-tuple-element.100.refs_0_.refs_1_, bf16[2048,4224]{1,0:T(8,128)(2,1)} %all-gather.4.cloned.1.call-done.refs_1_.wo_ref.refs_2_, bf16[512,2048]{1,0:T(8,128)(2,1)} %get-tuple-element.103.refs_3_.keep_ref, ...), custom_call_target="tpu_custom_call" | custom-call | flops 80530640 | bytes 191365 | tf_op jit(solution)/shard_map/pallas_call | solution.py:290
  523.2 6.7 shard_map.229
  532.5 12.6 %collective-permute-done.25.got_ref = bf16[512,1024]{1,0:T(8,128)(2,1)} collective-permute-done((bf16[512,1024]{1,0:T(8,128)(2,1)}, bf16[512,1024]{1,0:T(8,128)(2,1)}, u32[]{:S(2)}, u32[]{:S(2)}) %collective-permute-start.25) | collective-permute-done | bytes 1048608 | tf_op jit(solution)/shard_map/ppermute | solution.py:101
  554.1 45.9 %collective-permute-done.24.got_ref = bf16[512,2048]{1,0:T(8,128)(2,1)} collective-permute-done((bf16[512,2048]{1,0:T(8,128)(2,1)}, bf16[512,2048]{1,0:T(8,128)(2,1)}, u32[]{:S(2)}, u32[]{:S(2)}) %collective-permute-start.24) | collective-permute-done | bytes 2097184 | tf_op jit(solution)/shard_map/ppermute | solution.py:101
  599.9 3.4 shard_map.232.refs_0_
  605.5 7.6 %add_convert_fusion = bf16[640,2048]{1,0:T(8,128)(2,1)} fusion(f32[640,2048]{1,0:T(8,128)} %copy-done, bf16[640,2048]{1,0:T(8,128)(2,1)} %collective-permute-done.17.refs_2_, bf16[640,2048]{1,0:T(8,128)(2,1)} %constant_dynamic-update-slice_fusion.1), kind=kLoop, calls=%fused_computation.17 | loop fusion | flops 6553600 | bytes 13107200 | tf_op jit(solution)/shard_map/convert_element_type | solution.py:670
  613.1 3.7 fusion.11
  622.0 2.9 copy.96
  624.9 2.9 copy.95
  631.5 3.5 collective-permute-start.33
  635.4 6.0 fusion.10
  650.0 2.9 collective-permute-start.38
  657.5 9.4 %collective-permute-done.37 = bf16[128,1024]{0,1:T(8,128)(2,1)} collective-permute-done((bf16[128,1024]{0,1:T(8,128)(2,1)}, bf16[128,1024]{0,1:T(8,128)(2,1)}, u32[]{:S(2)}, u32[]{:S(2)}) %collective-permute-start.37) | collective-permute-done | bytes 262176 | tf_op jit(solution)/shard_map/ppermute | solution.py:118
  (231 shorter events, 112.6 us)
Async XLA Ops:
  7.2 99.9 %all-gather.4.cloned.1.call-start = ((), (), s32[]{:S(2)}) async-start(), calls=%async_computation.7 | async-start | bytes 18382848 | tf_op jit(solution)/shard_map/all_gather | solution.py:504
  12.7 199.2 %all-gather.8.cloned.1.call-start = ((), (), s32[]{:S(2)}) async-start(), calls=%async_computation.9 | async-start | bytes 20054016 | tf_op jit(solution)/shard_map/all_gather | solution.py:504
  17.8 302.0 %all-gather.6.cloned.1.call-start = ((), (), s32[]{:S(2)}) async-start(), calls=%async_computation.8 | async-start | bytes 18382848 | tf_op jit(solution)/shard_map/all_gather | solution.py:504
  23.4 359.0 %reduce-scatter.8.cloned.1.call-start = ((), (), s32[]{:S(2)}) async-start(), calls=%async_computation.10 | async-start | bytes 3932160 | tf_op jit(solution)/shard_map/reduce_scatter | solution.py:107
  126.0 5.3 collective-permute-start
  147.5 54.0 %collective-permute-start.1 = (bf16[640,2048]{1,0:T(8,128)(2,1)}, bf16[640,2048]{1,0:T(8,128)(2,1)}, u32[]{:S(2)}, u32[]{:S(2)}) collective-permute-start(bf16[640,2048]{1,0:T(8,128)(2,1)} %shard_map.205), channel_id=1, source_target_pairs={{0,1},{1,0},{2,3},{3,2},{4,5},{5,4},{6,7},{7,6},{8,9},{9,8},{10,11... | collective-permute-start | bytes 7864328 | tf_op jit(solution)/shard_map/ppermute | solution.py:568
  153.6 54.8 %collective-permute-start.3 = (bf16[1024,640]{1,0:T(8,128)(2,1)}, bf16[1024,640]{1,0:T(8,128)(2,1)S(1)}, u32[]{:S(2)}, u32[]{:S(2)}) collective-permute-start(bf16[1024,640]{1,0:T(8,128)(2,1)} %get-tuple-element.64), channel_id=1, source_target_pairs={{0,2},{2,0},{4,6},{6,4},{8,10},{10,8},{12,14},{14,12},{16,18},{18,... | collective-permute-start | bytes 3932168 | tf_op jit(solution)/shard_map/ppermute | solution.py:97
  165.2 44.9 %collective-permute-start.4 = (bf16[1024,640]{1,0:T(8,128)(2,1)}, bf16[1024,640]{1,0:T(8,128)(2,1)}, u32[]{:S(2)}, u32[]{:S(2)}) collective-permute-start(bf16[1024,640]{1,0:T(8,128)(2,1)} %get-tuple-element.65), channel_id=1, source_target_pairs={{0,2},{2,0},{4,6},{6,4},{8,10},{10,8},{12,14},{14,12},{16,18},{18,... | collective-permute-start | bytes 3932168 | tf_op jit(solution)/shard_map/ppermute | solution.py:97
  165.3 44.1 %collective-permute-start.5 = (bf16[64,3072]{1,0:T(8,128)(2,1)S(1)}, bf16[64,3072]{1,0:T(8,128)(2,1)S(1)}, u32[]{:S(2)}, u32[]{:S(2)}) collective-permute-start(bf16[64,3072]{1,0:T(8,128)(2,1)S(1)} %slice.195), channel_id=1, source_target_pairs={{2,0},{4,2},{6,4},{8,6},{10,8},{12,10},{14,12},{16,14},{18,16},{20... | collective-permute-start | bytes 1179656 | tf_op jit(solution)/shard_map/ppermute | solution.py:576
  166.6 43.6 %collective-permute-start.2 = (bf16[640,1024]{1,0:T(8,128)(2,1)}, bf16[640,1024]{1,0:T(8,128)(2,1)}, u32[]{:S(2)}, u32[]{:S(2)}) collective-permute-start(bf16[640,1024]{1,0:T(8,128)(2,1)} %shard_map.204.refs_0_), channel_id=1, source_target_pairs={{0,2},{2,0},{4,6},{6,4},{8,10},{10,8},{12,14},{14,12},{16,18},{18,... | collective-permute-start | bytes 3932168 | tf_op jit(solution)/shard_map/ppermute | solution.py:97
  249.3 16.1 %collective-permute-start.7 = (bf16[640,3072]{1,0:T(8,128)(2,1)}, bf16[640,3072]{1,0:T(8,128)(2,1)}, u32[]{:S(2)}, u32[]{:S(2)}) collective-permute-start(bf16[640,3072]{1,0:T(8,128)(2,1)} %get-tuple-element.70.refs_0_), channel_id=1, source_target_pairs={{0,2},{2,0},{4,6},{6,4},{8,10},{10,8},{12,14},{14,12},{16,18},{18,... | collective-permute-start | bytes 11796488 | tf_op jit(solution)/shard_map/ppermute | solution.py:97
  254.0 21.3 %collective-permute-start.8 = (bf16[640,1536]{1,0:T(8,128)(2,1)}, bf16[640,1536]{1,0:T(8,128)(2,1)}, u32[]{:S(2)}, u32[]{:S(2)}) collective-permute-start(bf16[640,1536]{1,0:T(8,128)(2,1)} %get-tuple-element.72.refs_0_), channel_id=1, source_target_pairs={{0,2},{2,0},{4,6},{6,4},{8,10},{10,8},{12,14},{14,12},{16,18},{18,... | collective-permute-start | bytes 5898248 | tf_op jit(solution)/shard_map/ppermute | solution.py:97
  258.1 7.2 %collective-permute-start.6 = (bf16[1024,640]{1,0:T(8,128)(2,1)}, bf16[1024,640]{1,0:T(8,128)(2,1)S(1)}, u32[]{:S(2)}, u32[]{:S(2)}) collective-permute-start(bf16[1024,640]{1,0:T(8,128)(2,1)} %get-tuple-element.69), channel_id=1, source_target_pairs={{0,2},{2,0},{4,6},{6,4},{8,10},{10,8},{12,14},{14,12},{16,18},{18,... | collective-permute-start | bytes 3932168 | tf_op jit(solution)/shard_map/ppermute | solution.py:97
  284.0 170.5 %reduce-scatter.10.cloned.1.call-start = ((), (), s32[]{:S(2)}) async-start(), calls=%async_computation.11 | async-start | bytes 1966080 | tf_op jit(solution)/shard_map/reduce_scatter | solution.py:107
  284.1 58.4 %collective-permute-start.9 = (bf16[512,1536]{1,0:T(8,128)(2,1)}, bf16[512,1536]{1,0:T(8,128)(2,1)}, u32[]{:S(2)}, u32[]{:S(2)}) collective-permute-start(bf16[512,1536]{1,0:T(8,128)(2,1)} %get-tuple-element.74.refs_3_), channel_id=1, source_target_pairs={{0,4},{2,6},{4,0},{6,2},{8,12},{10,14},{12,8},{14,10},{16,20},{18,... | collective-permute-start | bytes 4718600 | tf_op jit(solution)/shard_map/ppermute | solution.py:101
  345.5 154.3 %reduce-scatter.16.cloned.1.call-start = ((), (), s32[]{:S(2)}) async-start(), calls=%async_computation.14 | async-start | bytes 1966080 | tf_op jit(solution)/shard_map/reduce_scatter | solution.py:107
  345.6 52.0 %collective-permute-start.12 = (bf16[384,2560]{1,0:T(8,128)(2,1)}, bf16[384,2560]{1,0:T(8,128)(2,1)}, u32[]{:S(2)}, u32[]{:S(2)}) collective-permute-start(bf16[384,2560]{1,0:T(8,128)(2,1)} %get-tuple-element.78.refs_0_), channel_id=1, source_target_pairs={{0,2},{2,0},{4,6},{6,4},{8,10},{10,8},{12,14},{14,12},{16,18},{18,... | collective-permute-start | bytes 5898248 | tf_op jit(solution)/shard_map/ppermute | solution.py:97
  345.9 37.5 %collective-permute-start.10 = (bf16[384,2048]{1,0:T(8,128)(2,1)}, bf16[384,2048]{1,0:T(8,128)(2,1)}, u32[]{:S(2)}, u32[]{:S(2)}) collective-permute-start(bf16[384,2048]{1,0:T(8,128)(2,1)} %get-tuple-element.80.own_ref), channel_id=1, source_target_pairs={{0,1},{1,0},{2,3},{3,2},{4,5},{5,4},{6,7},{7,6},{8,9},{9,8},{10,11... | collective-permute-start | bytes 4718600 | tf_op jit(solution)/shard_map/ppermute | solution.py:568
  365.1 33.8 %collective-permute-start.13 = (bf16[256,2560]{1,0:T(8,128)(2,1)}, bf16[256,2560]{1,0:T(8,128)(2,1)}, u32[]{:S(2)}, u32[]{:S(2)}) collective-permute-start(bf16[256,2560]{1,0:T(8,128)(2,1)} %get-tuple-element.81.refs_0_.refs_1_), channel_id=1, source_target_pairs={{0,2},{2,0},{4,6},{6,4},{8,10},{10,8},{12,14},{14,12},{16,18},{18,... | collective-permute-start | bytes 3932168 | tf_op jit(solution)/shard_map/ppermute | solution.py:97
  365.2 55.4 %collective-permute-start.16 = (bf16[512,1536]{1,0:T(8,128)(2,1)}, bf16[512,1536]{1,0:T(8,128)(2,1)}, u32[]{:S(2)}, u32[]{:S(2)}) collective-permute-start(bf16[512,1536]{1,0:T(8,128)(2,1)} %get-tuple-element.76.refs_3_), channel_id=1, source_target_pairs={{0,4},{2,6},{4,0},{6,2},{8,12},{10,14},{12,8},{14,10},{16,20},{18,... | collective-permute-start | bytes 4718600 | tf_op jit(solution)/shard_map/ppermute | solution.py:101
  365.3 47.5 %collective-permute-start.11 = (bf16[256,2048]{1,0:T(8,128)(2,1)}, bf16[256,2048]{1,0:T(8,128)(2,1)}, u32[]{:S(2)}, u32[]{:S(2)}) collective-permute-start(bf16[256,2048]{1,0:T(8,128)(2,1)} %get-tuple-element.83.own_ref), channel_id=1, source_target_pairs={{0,1},{1,0},{2,3},{3,2},{4,5},{5,4},{6,7},{7,6},{8,9},{9,8},{10,11... | collective-permute-start | bytes 3145736 | tf_op jit(solution)/shard_map/ppermute | solution.py:568
  383.4 27.3 %collective-permute-start.15 = (bf16[128,1536]{1,0:T(8,128)(2,1)S(1)}, bf16[128,1536]{1,0:T(8,128)(2,1)}, u32[]{:S(2)}, u32[]{:S(2)}) collective-permute-start(bf16[128,1536]{1,0:T(8,128)(2,1)S(1)} %slice.197), channel_id=1, source_target_pairs={{0,4},{2,6},{4,0},{6,2},{8,12},{10,14},{12,8},{14,10},{16,20},{18,... | collective-permute-start | bytes 1179656 | tf_op jit(solution)/shard_map/ppermute | solution.py:101
  397.6 15.1 %collective-permute-start.14 = (bf16[64,1024]{1,0:T(8,128)(2,1)S(1)}, bf16[64,1024]{1,0:T(8,128)(2,1)S(1)}, u32[]{:S(2)}, u32[]{:S(2)}) collective-permute-start(bf16[64,1024]{1,0:T(8,128)(2,1)S(1)} %slice.156), channel_id=1, source_target_pairs={{2,0},{4,2},{6,4},{8,6},{10,8},{12,10},{14,12},{16,14},{18,16},{20... | collective-permute-start | bytes 393224 | tf_op jit(solution)/shard_map/ppermute | solution.py:613
  423.6 99.5 %reduce-scatter.12.cloned.1.call-start = ((), (), s32[]{:S(2)}) async-start(), calls=%async_computation.12 | async-start | bytes 1638400 | tf_op jit(solution)/shard_map/reduce_scatter | solution.py:107
  423.7 30.8 %collective-permute-start.18 = (bf16[512,1280]{1,0:T(8,128)(2,1)}, bf16[512,1280]{1,0:T(8,128)(2,1)}, u32[]{:S(2)}, u32[]{:S(2)}) collective-permute-start(bf16[512,1280]{1,0:T(8,128)(2,1)} %get-tuple-element.85.refs_1_), channel_id=1, source_target_pairs={{0,4},{2,6},{4,0},{6,2},{8,12},{10,14},{12,8},{14,10},{16,20},{18,... | collective-permute-start | bytes 3932168 | tf_op jit(solution)/shard_map/ppermute | solution.py:101
  457.2 96.8 %reduce-scatter.14.cloned.1.call-start = ((), (), s32[]{:S(2)}) async-start(), calls=%async_computation.13 | async-start | bytes 1638400 | tf_op jit(solution)/shard_map/reduce_scatter | solution.py:107
  457.3 29.9 %collective-permute-start.19 = (bf16[512,1280]{1,0:T(8,128)(2,1)}, bf16[512,1280]{1,0:T(8,128)(2,1)S(1)}, u32[]{:S(2)}, u32[]{:S(2)}) collective-permute-start(bf16[512,1280]{1,0:T(8,128)(2,1)} %get-tuple-element.89.refs_3_), channel_id=1, source_target_pairs={{0,4},{2,6},{4,0},{6,2},{8,12},{10,14},{12,8},{14,10},{16,20},{18,... | collective-permute-start | bytes 3932168 | tf_op jit(solution)/shard_map/ppermute | solution.py:101
  459.1 5.1 collective-permute-start.20
  459.1 5.4 collective-permute-start.21
  459.6 40.2 %collective-permute-start.22 = (bf16[640,2048]{1,0:T(8,128)(2,1)}, bf16[640,2048]{1,0:T(8,128)(2,1)}, u32[]{:S(2)}, u32[]{:S(2)}) collective-permute-start(bf16[640,2048]{1,0:T(8,128)(2,1)} %get-tuple-element.100.refs_0_.refs_1_), channel_id=1, source_target_pairs={{0,2},{2,0},{4,6},{6,4},{8,10},{10,8},{12,14},{14,12},{16,18},{18,... | collective-permute-start | bytes 7864328 | tf_op jit(solution)/shard_map/ppermute | solution.py:97
  463.5 66.3 %collective-permute-start.17 = (bf16[640,2048]{1,0:T(8,128)(2,1)}, bf16[640,2048]{1,0:T(8,128)(2,1)}, u32[]{:S(2)}, u32[]{:S(2)}) collective-permute-start(bf16[640,2048]{1,0:T(8,128)(2,1)} %constant_dynamic-update-slice_fusion.1), channel_id=1, source_target_pairs={{0,1},{1,0},{2,3},{3,2},{4,5},{5,4},{6,7},{7,6},{8,9},{9,8},{10,11... | collective-permute-start | bytes 7864328 | tf_op jit(solution)/shard_map/ppermute | solution.py:568
  464.2 28.7 %collective-permute-start.23 = (bf16[640,1024]{1,0:T(8,128)(2,1)}, bf16[640,1024]{1,0:T(8,128)(2,1)}, u32[]{:S(2)}, u32[]{:S(2)}) collective-permute-start(bf16[640,1024]{1,0:T(8,128)(2,1)} %get-tuple-element.94.refs_0_), channel_id=1, source_target_pairs={{0,2},{2,0},{4,6},{6,4},{8,10},{10,8},{12,14},{14,12},{16,18},{18,... | collective-permute-start | bytes 3932168 | tf_op jit(solution)/shard_map/ppermute | solution.py:97
  491.0 151.0 %reduce-scatter.18.cloned.1.call-start = ((), (), s32[]{:S(2)}) async-start(), calls=%async_computation.15 | async-start | bytes 2949120 | tf_op jit(solution)/shard_map/reduce_scatter | solution.py:107
  491.0 32.1 %collective-permute-start.27 = (bf16[1024,640]{1,0:T(8,128)(2,1)}, bf16[1024,640]{1,0:T(8,128)(2,1)}, u32[]{:S(2)}, u32[]{:S(2)}) collective-permute-start(bf16[1024,640]{1,0:T(8,128)(2,1)} %get-tuple-element.105), channel_id=1, source_target_pairs={{0,2},{2,0},{4,6},{6,4},{8,10},{10,8},{12,14},{14,12},{16,18},{18,... | collective-permute-start | bytes 3932168 | tf_op jit(solution)/shard_map/ppermute | solution.py:97
  491.1 38.7 %collective-permute-start.26 = (bf16[512,1280]{1,0:T(8,128)(2,1)}, bf16[512,1280]{1,0:T(8,128)(2,1)}, u32[]{:S(2)}, u32[]{:S(2)}) collective-permute-start(bf16[512,1280]{1,0:T(8,128)(2,1)} %get-tuple-element.98.refs_1_), channel_id=1, source_target_pairs={{0,4},{2,6},{4,0},{6,2},{8,12},{10,14},{12,8},{14,10},{16,20},{18,... | collective-permute-start | bytes 3932168 | tf_op jit(solution)/shard_map/ppermute | solution.py:101
  499.5 45.6 %collective-permute-start.25 = (bf16[512,1024]{1,0:T(8,128)(2,1)}, bf16[512,1024]{1,0:T(8,128)(2,1)}, u32[]{:S(2)}, u32[]{:S(2)}) collective-permute-start(bf16[512,1024]{1,0:T(8,128)(2,1)} %get-tuple-element.102.refs_3_), channel_id=1, source_target_pairs={{0,4},{2,6},{4,0},{6,2},{8,12},{10,14},{12,8},{14,10},{16,20},{18,... | collective-permute-start | bytes 3145736 | tf_op jit(solution)/shard_map/ppermute | solution.py:101
  550.7 118.3 %reduce-scatter.20.cloned.1.call-start = ((), (), s32[]{:S(2)}) async-start(), calls=%async_computation.16 | async-start | bytes 2621440 | tf_op jit(solution)/shard_map/reduce_scatter | solution.py:107
  551.0 48.9 %collective-permute-start.24 = (bf16[512,2048]{1,0:T(8,128)(2,1)}, bf16[512,2048]{1,0:T(8,128)(2,1)}, u32[]{:S(2)}, u32[]{:S(2)}) collective-permute-start(bf16[512,2048]{1,0:T(8,128)(2,1)} %get-tuple-element.104.refs_4_), channel_id=1, source_target_pairs={{0,4},{2,6},{4,0},{6,2},{8,12},{10,14},{12,8},{14,10},{16,20},{18,... | collective-permute-start | bytes 6291464 | tf_op jit(solution)/shard_map/ppermute | solution.py:101
  552.8 60.3 %collective-permute-start.28 = (bf16[640,2048]{1,0:T(8,128)(2,1)}, bf16[640,2048]{1,0:T(8,128)(2,1)}, u32[]{:S(2)}, u32[]{:S(2)}) collective-permute-start(bf16[640,2048]{1,0:T(8,128)(2,1)} %shard_map.228.refs_2_), channel_id=1, source_target_pairs={{0,1},{1,0},{2,3},{3,2},{4,5},{5,4},{6,7},{7,6},{8,9},{9,8},{10,11... | collective-permute-start | bytes 7864328 | tf_op jit(solution)/shard_map/ppermute | solution.py:568
  553.7 88.2 %collective-permute-start.35 = (bf16[512,1024]{1,0:T(8,128)(2,1)}, bf16[512,1024]{1,0:T(8,128)(2,1)}, u32[]{:S(2)}, u32[]{:S(2)}) collective-permute-start(bf16[512,1024]{1,0:T(8,128)(2,1)} %get-tuple-element.107.refs_1_), channel_id=1, source_target_pairs={{0,4},{2,6},{4,0},{6,2},{8,12},{10,14},{12,8},{14,10},{16,20},{18,... | collective-permute-start | bytes 3145736 | tf_op jit(solution)/shard_map/ppermute | solution.py:101
  616.8 3.7 collective-permute-start.29
  620.7 7.1 %collective-permute-start.30 = (f32[8,2,128]{2,1,0:T(2,128)S(1)}, f32[8,2,128]{2,1,0:T(2,128)S(1)}, u32[]{:S(2)}, u32[]{:S(2)}) collective-permute-start(f32[8,2,128]{2,1,0:T(2,128)S(1)} %slice.199), channel_id=1, source_target_pairs={{0,2},{2,0},{4,6},{6,4},{8,10},{10,8},{12,14},{14,12},{16,18},{18,... | collective-permute-start | bytes 24584 | tf_op jit(solution)/shard_map/ppermute | solution.py:97
  631.5 9.9 %collective-permute-start.32 = (f32[2,128]{1,0:T(2,128)S(1)}, f32[2,128]{1,0:T(2,128)S(1)}, u32[]{:S(2)}, u32[]{:S(2)}) collective-permute-start(f32[2,128]{1,0:T(2,128)S(1)} %get-tuple-element.193), channel_id=1, source_target_pairs={{0,8},{2,10},{4,12},{6,14},{8,16},{10,18},{12,20},{14,22},{16,24},... | collective-permute-start | bytes 3080 | tf_op jit(solution)/shard_map/ppermute | solution.py:159
  631.5 9.8 %collective-permute-start.33 = (f32[2,128]{1,0:T(2,128)S(1)}, f32[2,128]{1,0:T(2,128)S(1)}, u32[]{:S(2)}, u32[]{:S(2)}) collective-permute-start(f32[2,128]{1,0:T(2,128)S(1)} %get-tuple-element.195), channel_id=1, source_target_pairs={{0,16},{2,18},{4,20},{6,22},{8,24},{10,26},{12,28},{14,30},{16,0},... | collective-permute-start | bytes 3080 | tf_op jit(solution)/shard_map/ppermute | solution.py:159
  635.0 6.4 collective-permute-start.34
  646.2 11.3 %collective-permute-start.36 = (bf16[128,1024]{0,1:T(8,128)(2,1)S(1)}, bf16[128,1024]{0,1:T(8,128)(2,1)}, u32[]{:S(2)}, u32[]{:S(2)}) collective-permute-start(bf16[128,1024]{0,1:T(8,128)(2,1)S(1)} %bitcast.50), channel_id=1, source_target_pairs={{0,8},{2,10},{4,12},{6,14},{8,16},{10,18},{12,20},{14,22},{16,24},... | collective-permute-start | bytes 786440 | tf_op jit(solution)/shard_map/ppermute | solution.py:118
  648.8 18.2 %collective-permute-start.37 = (bf16[128,1024]{0,1:T(8,128)(2,1)}, bf16[128,1024]{0,1:T(8,128)(2,1)}, u32[]{:S(2)}, u32[]{:S(2)}) collective-permute-start(bf16[128,1024]{0,1:T(8,128)(2,1)} %bitcast.20), channel_id=1, source_target_pairs={{0,16},{2,18},{4,20},{6,22},{8,24},{10,26},{12,28},{14,30},{16,0},... | collective-permute-start | bytes 786440 | tf_op jit(solution)/shard_map/ppermute | solution.py:118
  650.0 17.0 %collective-permute-start.38 = (bf16[128,1024]{0,1:T(8,128)(2,1)}, bf16[128,1024]{0,1:T(8,128)(2,1)}, u32[]{:S(2)}, u32[]{:S(2)}) collective-permute-start(bf16[128,1024]{0,1:T(8,128)(2,1)} %bitcast.21), channel_id=1, source_target_pairs={{0,24},{2,26},{4,28},{6,30},{8,0},{10,2},{12,4},{14,6},{16,8},{18,... | collective-permute-start | bytes 786440 | tf_op jit(solution)/shard_map/ppermute | solution.py:118
  (29 other events, 107.9 us)
Sparse Core Ops, SparseCore 0:
  12.8 94.2 all-gather.3
  108.7 103.1 all-gather.7
  213.5 106.3 all-gather.5
  322.0 60.3 reduce-scatter.7
  384.5 36.7 reduce-scatter.9
  423.7 34.2 reduce-scatter.15
  460.3 30.1 reduce-scatter.11
  493.4 29.9 reduce-scatter.13
  550.8 46.7 reduce-scatter.17
  603.5 42.6 reduce-scatter.19

commit v5 on v4

--- a/solution.py
+++ b/solution.py
@@ -300,7 +300,7 @@
     )(*pieces, weights, *after)
 
 
-PARTS = ((768, 2), (640, 2))
+PARTS = ((768, 2), (1280, 1))
 
 
 def feed(block, steps, first_row, h_ref, dm_ref, wgu_ref, wd_ref, *refs):

time: 691 us -> 690 us (level)
    unnamed x72 -> x67, local copies, waits for them, and re-layouts: 28.1 us -> 24.7 us
  transfers between devices with their start and end apart: 49 -> 49, of which waited for: 15 -> 15; matrix products, arithmetic and copies ran while one was open for 11% -> 10% of each run, Pallas kernels for 39% -> 39%
where the time goes in v5:
time: 690 us; the launch traced here: 677 us
  Pallas kernels  262 us (38%)
  waiting for transfers between devices  255 us (37%)
  starting transfers between devices  54.7 us (8%)
  other arithmetic  45.3 us (7%)
  local copies, waits for them, and re-layouts  42.1 us (6%)
  between operations  17.9 us (3%)
    all_gather x3, waiting for transfers between devices, gather(): return lax.all_gather(jnp.concatenate(shards, 1), 'seq', axis=0, tiled=True)  102 us
    ppermute x10, waiting for transfers between devices, to_middle(): return lax.ppermute(values, 'seq', flip_pairs(lax.axis_size('seq'), 2))  81 us
    pallas_call x3, Pallas kernels, feed_forward(): pl.pallas_call(functools.partial(feed, block, steps, place * 128 if carri...  76.7 us
    pallas_call x9, Pallas kernels, weight_grad(): pl.pallas_call(functools.partial(grad_block, len(right[0]), outers), grid...  74.9 us
    ppermute x6, waiting for transfers between devices, to_mp(): return lax.ppermute(own, 'mp', [(0, 1), (1, 0)])  35.5 us
    pallas_call x3, Pallas kernels, rows_times(): pl.pallas_call(functools.partial(multiply, turned, len(pieces)), grid=(ou...  33.1 us
    unnamed x67, local copies, waits for them, and re-layouts  24.7 us
    pallas_call x8, Pallas kernels, add_middle(): pl.pallas_call(add_block, grid=(columns // wide,), in_specs=[spec] * 2 +...  23 us
  transfers between devices with their start and end apart: 49, of which 15 were waited for; matrix products, arithmetic and copies ran while one was open for 10% of the time, Pallas kernels for 39%

profile of v5, /device:TPU:0, one launch (start us, length us, event | category | flops | bytes accessed | tf_op | source)
XLA Modules:
  0.0 677.3 jit_solution(6208630336679741233)
XLA Ops:
  25.3 81.6 %all-gather.4.cloned.1.call-done.refs_1_.wo_ref.refs_2_ = bf16[2048,4224]{1,0:T(8,128)(2,1)} async-done(((bf16[128,4224]{1,0:T(8,128)(2,1)}), bf16[2048,4224]{1,0:T(8,128)(2,1)}) %all-gather.4.cloned.1.call-update) | async-done | bytes 17301520 | tf_op jit(solution)/shard_map/all_gather | solution.py:504
  111.6 13.3 %shard_map.203.q_ref.k_ref.v_ref = bf16[640,3072]{1,0:T(8,128)(2,1)} custom-call(bf16[640,2048]{1,0:T(8,128)(2,1)} %fusion.5.refs_0_, bf16[2048,4224]{1,0:T(8,128)(2,1)} %all-gather.4.cloned.1.call-done.refs_1_.wo_ref.refs_2_), custom_call_target="tpu_custom_call" | custom-call | flops 80530640 | bytes 191365 | tf_op jit(solution)/shard_map/pallas_call | solution.py:290
  131.8 8.9 %shard_map.204.refs_0_ = bf16[640,1024]{1,0:T(8,128)(2,1)} custom-call(bf16[640,3072]{1,0:T(8,128)(2,1)} %shard_map.203.q_ref.k_ref.v_ref, bf16[640,3072]{1,0:T(8,128)(2,1)} %shard_map.203.q_ref.k_ref.v_ref, bf16[640,3072]{1,0:T(8,128)(2,1)} %shard_map.203.q_ref.k_ref.v_ref, bf16[64,2048]{1,0:T(8,128)(2,1)} %copy-done.8, bf16[64,2048]{1,0:T(8,128)(2,1)} %copy-done.8, ...), custom_call_target="tpu_custom_call" | custom-call | flops 3355443 | bytes 52428 | tf_op jit(solution)/shard_map/pallas_call | solution.py:236
  140.7 6.7 shard_map.205
  149.5 4.0 shard_map.206
  153.5 6.6 collective-permute-start.3
  160.1 4.0 shard_map.207
  167.7 33.7 %collective-permute-done.1 = bf16[640,2048]{1,0:T(8,128)(2,1)} collective-permute-done((bf16[640,2048]{1,0:T(8,128)(2,1)}, bf16[640,2048]{1,0:T(8,128)(2,1)}, u32[]{:S(2)}, u32[]{:S(2)}) %collective-permute-start.1) | collective-permute-done | bytes 2621472 | tf_op jit(solution)/shard_map/ppermute | solution.py:568
  201.4 3.8 multiply_reduce_fusion
  211.7 37.5 %shard_map.208 = (bf16[640,3072]{1,0:T(8,128)(2,1)}, bf16[640,1536]{1,0:T(8,128)(2,1)}, f32[640,2048]{1,0:T(8,128)}, f32[640,2048]{1,0:T(8,128)}) custom-call(bf16[640,2048]{1,0:T(8,128)(2,1)} %multiply_convert_fusion.h_ref.refs_0_, bf16[640,2048]{1,0:T(8,128)(2,1)} %dm_ref.9, bf16[2048,4608]{1,0:T(8,128)(2,1)} %all-gather.8.cloned.1.call-done.wgu_ref.wd_ref, ...), custom_call_target="tpu_custom_call" | custom-call | flops 241591904 | bytes 503316 | tf_op jit(solution)/shard_map/pallas_call | solution.py:369
  249.2 4.7 collective-permute-start.7
  253.9 4.1 shard_map.209
  258.4 6.9 %collective-permute-done.6.left_got_ref = bf16[1024,640]{1,0:T(8,128)(2,1)S(1)} collective-permute-done((bf16[1024,640]{1,0:T(8,128)(2,1)}, bf16[1024,640]{1,0:T(8,128)(2,1)S(1)}, u32[]{:S(2)}, u32[]{:S(2)}) %collective-permute-start.6) | collective-permute-done | bytes 1310752 | tf_op jit(solution)/shard_map/ppermute | solution.py:97
  266.3 8.9 %shard_map.210 = (bf16[512,1536]{1,0:T(8,128)(2,1)}, bf16[512,1536]{1,0:T(8,128)(2,1)}) custom-call(bf16[1024,640]{1,0:T(8,128)(2,1)} %get-tuple-element.68.left_ref, bf16[1024,640]{1,0:T(8,128)(2,1)} %copy-done.3, bf16[640,3072]{1,0:T(8,128)(2,1)} %get-tuple-element.70.refs_0_, bf16[640,3072]{1,0:T(8,128)(2,1)} %collective-permute-done.7.refs_1_), custom_call_target="tpu_custom_call" | custom-call | flops 40265320 | bytes 96993 | tf_op jit(solution)/shard_map/pallas_call | solution.py:429
  275.2 8.7 %shard_map.211.refs_2_ = bf16[1024,1536]{1,0:T(8,128)(2,1)} custom-call(bf16[1024,640]{1,0:T(8,128)(2,1)} %get-tuple-element.71.left_ref, bf16[1024,640]{1,0:T(8,128)(2,1)} %copy-done.4, bf16[640,1536]{1,0:T(8,128)(2,1)} %get-tuple-element.72.refs_0_, bf16[640,1536]{1,0:T(8,128)(2,1)} %collective-permute-done.8.refs_1_, ...), custom_call_target="tpu_custom_call" | custom-call | flops 40265320 | bytes 96993 | tf_op jit(solution)/shard_map/pallas_call | solution.py:429
  284.0 8.6 %collective-permute-start.9 = (bf16[512,1536]{1,0:T(8,128)(2,1)}, bf16[512,1536]{1,0:T(8,128)(2,1)}, u32[]{:S(2)}, u32[]{:S(2)}) collective-permute-start(bf16[512,1536]{1,0:T(8,128)(2,1)} %get-tuple-element.74.refs_3_), channel_id=1, source_target_pairs={{0,4},{2,6},{4,0},{6,2},{8,12},{10,14},{12,8},{14,10},{16,20},{18,... | collective-permute-start | bytes 4718600 | tf_op jit(solution)/shard_map/ppermute | solution.py:101
  292.5 8.5 %shard_map.212 = (bf16[512,1536]{1,0:T(8,128)(2,1)}, bf16[512,1536]{1,0:T(8,128)(2,1)}) custom-call(bf16[1024,640]{1,0:T(8,128)(2,1)} %get-tuple-element.68.left_ref, bf16[1024,640]{1,0:T(8,128)(2,1)} %copy-done.3, bf16[640,3072]{1,0:T(8,128)(2,1)} %get-tuple-element.70.refs_0_, bf16[640,3072]{1,0:T(8,128)(2,1)} %collective-permute-done.7.refs_1_, ...), custom_call_target="tpu_custom_call" | custom-call | flops 40265320 | bytes 96993 | tf_op jit(solution)/shard_map/pallas_call | solution.py:429
  301.0 18.6 %all-gather.6.cloned.1.call-done.wgu_ref.wd_ref = bf16[2048,4224]{1,0:T(8,128)(2,1)} async-done(((bf16[128,4224]{1,0:T(8,128)(2,1)}), bf16[2048,4224]{1,0:T(8,128)(2,1)}) %all-gather.6.cloned.1.call-update) | async-done | bytes 17301520 | tf_op jit(solution)/shard_map/all_gather | solution.py:504
  319.7 21.9 %shard_map.213 = (bf16[384,2560]{1,0:T(8,128)(2,1)}, bf16[384,1280]{1,0:T(8,128)(2,1)}, bf16[384,2048]{1,0:T(8,128)(2,1)}, bf16[384,2048]{1,0:T(8,128)(2,1)}) custom-call(bf16[640,2048]{1,0:T(8,128)(2,1)} %multiply_convert_fusion.h_ref.refs_0_, bf16[640,2048]{1,0:T(8,128)(2,1)} %dm_ref.9, bf16[2048,4224]{1,0:T(8,128)(2,1)} %all-gather.6.cloned.1.call-done.wgu_ref.wd_ref, ...), custom_call_target="tpu_custom_call" | custom-call | flops 120795952 | bytes 346030 | tf_op jit(solution)/shard_map/pallas_call | solution.py:369
  341.6 3.0 shard_map.214.refs_2_
  346.5 17.4 %shard_map.215 = (bf16[256,2560]{1,0:T(8,128)(2,1)}, bf16[256,1280]{1,0:T(8,128)(2,1)}, bf16[256,2048]{1,0:T(8,128)(2,1)}, bf16[256,2048]{1,0:T(8,128)(2,1)}) custom-call(bf16[640,2048]{1,0:T(8,128)(2,1)} %multiply_convert_fusion.h_ref.refs_0_, bf16[640,2048]{1,0:T(8,128)(2,1)} %dm_ref.9, bf16[2048,4224]{1,0:T(8,128)(2,1)} %all-gather.6.cloned.1.call-done.wgu_ref.wd_ref, ...), custom_call_target="tpu_custom_call" | custom-call | flops 80530640 | bytes 283115 | tf_op jit(solution)/shard_map/pallas_call | solution.py:369
  364.7 17.5 %reduce-scatter.8.cloned.1.call-done = bf16[256,1536]{1,0:T(8,128)(2,1)} async-done(((bf16[1024,1536]{1,0:T(8,128)(2,1)}), bf16[256,1536]{1,0:T(8,128)(2,1)}) %reduce-scatter.8.cloned.1.call-update) | async-done | bytes 786448 | tf_op jit(solution)/shard_map/reduce_scatter | solution.py:107
  386.9 9.6 %shard_map.216 = (f32[384,2048]{1,0:T(8,128)}, bf16[384,2048]{1,0:T(8,128)(2,1)}, bf16[384,1024]{1,0:T(8,128)(2,1)}, f32[1,2048]{1,0:T(1,128)}) custom-call(bf16[384,2048]{1,0:T(8,128)(2,1)} %get-tuple-element.80.own_ref, bf16[384,2048]{1,0:T(8,128)(2,1)} %collective-permute-done.10.got_ref, f32[640,2048]{1,0:T(8,128)} %copy-done, bf16[640,2048]{1,0:T(8,128)(2,1)} %dm_ref.9, ...), custom_call_target="tpu_custom_call" | custom-call | flops 16106127 | bytes 167772 | tf_op jit(solution)/shard_map/pallas_call | solution.py:472
  398.9 8.4 %shard_map.217 = (bf16[512,1280]{1,0:T(8,128)(2,1)}, bf16[512,1280]{1,0:T(8,128)(2,1)}) custom-call(bf16[1024,640]{1,0:T(8,128)(2,1)} %get-tuple-element.68.left_ref, bf16[1024,640]{1,0:T(8,128)(2,1)} %copy-done.3, bf16[384,2560]{1,0:T(8,128)(2,1)} %get-tuple-element.78.refs_0_, bf16[256,2560]{1,0:T(8,128)(2,1)} %get-tuple-element.81.refs_0_.refs_1_, ...), custom_call_target="tpu_custom_call" | custom-call | flops 33554432 | bytes 85196 | tf_op jit(solution)/shard_map/pallas_call | solution.py:429
  412.2 7.1 %shard_map.218 = (f32[256,2048]{1,0:T(8,128)}, bf16[256,2048]{1,0:T(8,128)(2,1)}, bf16[256,1024]{1,0:T(8,128)(2,1)}, f32[1,2048]{1,0:T(1,128)}) custom-call(bf16[256,2048]{1,0:T(8,128)(2,1)} %get-tuple-element.83.own_ref, bf16[256,2048]{1,0:T(8,128)(2,1)} %collective-permute-done.11.got_ref, f32[640,2048]{1,0:T(8,128)} %copy-done, bf16[640,2048]{1,0:T(8,128)(2,1)} %dm_ref.9, ...), custom_call_target="tpu_custom_call" | custom-call | flops 10737418 | bytes 125829 | tf_op jit(solution)/shard_map/pallas_call | solution.py:472
  419.4 3.0 shard_map.219.refs_4_
  424.2 8.3 %shard_map.220 = (bf16[512,1280]{1,0:T(8,128)(2,1)}, bf16[512,1280]{1,0:T(8,128)(2,1)}) custom-call(bf16[1024,640]{1,0:T(8,128)(2,1)} %get-tuple-element.68.left_ref, bf16[1024,640]{1,0:T(8,128)(2,1)} %copy-done.3, bf16[384,2560]{1,0:T(8,128)(2,1)} %get-tuple-element.78.refs_0_, bf16[256,2560]{1,0:T(8,128)(2,1)} %get-tuple-element.81.refs_0_.refs_1_, ...), custom_call_target="tpu_custom_call" | custom-call | flops 33554432 | bytes 85196 | tf_op jit(solution)/shard_map/pallas_call | solution.py:429
  432.5 3.9 shard_map.221
  436.3 13.1 %shard_map.222 = (bf16[640,1024]{1,0:T(8,128)(2,1)}, bf16[640,2048]{1,0:T(8,128)(2,1)}) custom-call(bf16[640,3072]{1,0:T(8,128)(2,1)} %shard_map.203.q_ref.k_ref.v_ref, bf16[640,3072]{1,0:T(8,128)(2,1)} %shard_map.203.q_ref.k_ref.v_ref, bf16[640,3072]{1,0:T(8,128)(2,1)} %shard_map.203.q_ref.k_ref.v_ref, bf16[64,2048]{1,0:T(8,128)(2,1)} %copy-done.8, ...), custom_call_target="tpu_custom_call" | custom-call | flops 8388608 | bytes 91750 | tf_op jit(solution)/shard_map/pallas_call | solution.py:252
  449.4 3.8 collective-permute-done.18.got_ref
  462.9 8.6 %shard_map.224 = (bf16[512,1280]{1,0:T(8,128)(2,1)}, bf16[512,1280]{1,0:T(8,128)(2,1)}) custom-call(bf16[1024,640]{1,0:T(8,128)(2,1)} %get-tuple-element.71.left_ref, bf16[1024,640]{1,0:T(8,128)(2,1)} %copy-done.4, bf16[384,1280]{1,0:T(8,128)(2,1)} %get-tuple-element.95.refs_0_, bf16[256,1280]{1,0:T(8,128)(2,1)} %get-tuple-element.96.refs_1_, ...), custom_call_target="tpu_custom_call" | custom-call | flops 33554432 | bytes 85196 | tf_op jit(solution)/shard_map/pallas_call | solution.py:429
  471.4 14.4 %collective-permute-done.19.got_ref = bf16[512,1280]{1,0:T(8,128)(2,1)S(1)} collective-permute-done((bf16[512,1280]{1,0:T(8,128)(2,1)}, bf16[512,1280]{1,0:T(8,128)(2,1)S(1)}, u32[]{:S(2)}, u32[]{:S(2)}) %collective-permute-start.19) | collective-permute-done | bytes 1310752 | tf_op jit(solution)/shard_map/ppermute | solution.py:101
  491.9 6.6 shard_map.226
  498.7 10.3 %shard_map.227 = (bf16[512,2048]{1,0:T(8,128)(2,1)}, bf16[512,2048]{1,0:T(8,128)(2,1)}) custom-call(bf16[1024,640]{1,0:T(8,128)(2,1)} %get-tuple-element.99.left_ref, bf16[1024,640]{1,0:T(8,128)(2,1)} %collective-permute-done.4.refs_2_.left_got_ref, bf16[640,2048]{1,0:T(8,128)(2,1)} %get-tuple-element.100.refs_0_.refs_1_, ...), custom_call_target="tpu_custom_call" | custom-call | flops 53687092 | bytes 120586 | tf_op jit(solution)/shard_map/pallas_call | solution.py:429
  509.0 13.0 %shard_map.228.refs_2_ = bf16[640,2048]{1,0:T(8,128)(2,1)} custom-call(bf16[640,1024]{1,0:T(8,128)(2,1)} %get-tuple-element.94.refs_0_, bf16[640,2048]{1,0:T(8,128)(2,1)} %get-tuple-element.100.refs_0_.refs_1_, bf16[2048,4224]{1,0:T(8,128)(2,1)} %all-gather.4.cloned.1.call-done.refs_1_.wo_ref.refs_2_, bf16[512,2048]{1,0:T(8,128)(2,1)} %get-tuple-element.103.refs_3_.keep_ref, ...), custom_call_target="tpu_custom_call" | custom-call | flops 80530640 | bytes 191365 | tf_op jit(solution)/shard_map/pallas_call | solution.py:290
  522.1 6.7 shard_map.229
  531.4 12.6 %collective-permute-done.25.got_ref = bf16[512,1024]{1,0:T(8,128)(2,1)} collective-permute-done((bf16[512,1024]{1,0:T(8,128)(2,1)}, bf16[512,1024]{1,0:T(8,128)(2,1)}, u32[]{:S(2)}, u32[]{:S(2)}) %collective-permute-start.25) | collective-permute-done | bytes 1048608 | tf_op jit(solution)/shard_map/ppermute | solution.py:101
  546.8 2.8 pad_maximum_fusion
  552.6 46.0 %collective-permute-done.24.got_ref = bf16[512,2048]{1,0:T(8,128)(2,1)} collective-permute-done((bf16[512,2048]{1,0:T(8,128)(2,1)}, bf16[512,2048]{1,0:T(8,128)(2,1)}, u32[]{:S(2)}, u32[]{:S(2)}) %collective-permute-start.24) | collective-permute-done | bytes 2097184 | tf_op jit(solution)/shard_map/ppermute | solution.py:101
  598.6 3.4 shard_map.232.refs_0_
  603.2 7.2 %add_convert_fusion = bf16[640,2048]{1,0:T(8,128)(2,1)} fusion(f32[640,2048]{1,0:T(8,128)} %copy-done, bf16[640,2048]{1,0:T(8,128)(2,1)} %collective-permute-done.17.refs_2_, bf16[640,2048]{1,0:T(8,128)(2,1)} %constant_dynamic-update-slice_fusion), kind=kLoop, calls=%fused_computation.17 | loop fusion | flops 6553600 | bytes 13107200 | tf_op jit(solution)/shard_map/convert_element_type | solution.py:670
  610.4 3.8 fusion.11
  619.4 2.9 copy.96
  622.3 2.9 copy.95
  634.6 6.0 fusion.10
  647.7 3.3 collective-permute-start.38
  653.7 3.0 collective-permute-done.36
  656.7 9.1 %collective-permute-done.37 = bf16[128,1024]{0,1:T(8,128)(2,1)} collective-permute-done((bf16[128,1024]{0,1:T(8,128)(2,1)}, bf16[128,1024]{0,1:T(8,128)(2,1)}, u32[]{:S(2)}, u32[]{:S(2)}) %collective-permute-start.37) | collective-permute-done | bytes 262176 | tf_op jit(solution)/shard_map/ppermute | solution.py:118
  (225 shorter events, 111.0 us)
Async XLA Ops:
  7.2 99.8 %all-gather.4.cloned.1.call-start = ((), (), s32[]{:S(2)}) async-start(), calls=%async_computation.7 | async-start | bytes 18382848 | tf_op jit(solution)/shard_map/all_gather | solution.py:504
  12.6 199.2 %all-gather.8.cloned.1.call-start = ((), (), s32[]{:S(2)}) async-start(), calls=%async_computation.9 | async-start | bytes 20054016 | tf_op jit(solution)/shard_map/all_gather | solution.py:504
  18.9 300.8 %all-gather.6.cloned.1.call-start = ((), (), s32[]{:S(2)}) async-start(), calls=%async_computation.8 | async-start | bytes 18382848 | tf_op jit(solution)/shard_map/all_gather | solution.py:504
  21.4 360.7 %reduce-scatter.8.cloned.1.call-start = ((), (), s32[]{:S(2)}) async-start(), calls=%async_computation.10 | async-start | bytes 3932160 | tf_op jit(solution)/shard_map/reduce_scatter | solution.py:107
  125.9 5.2 collective-permute-start
  147.4 53.9 %collective-permute-start.1 = (bf16[640,2048]{1,0:T(8,128)(2,1)}, bf16[640,2048]{1,0:T(8,128)(2,1)}, u32[]{:S(2)}, u32[]{:S(2)}) collective-permute-start(bf16[640,2048]{1,0:T(8,128)(2,1)} %shard_map.205), channel_id=1, source_target_pairs={{0,1},{1,0},{2,3},{3,2},{4,5},{5,4},{6,7},{7,6},{8,9},{9,8},{10,11... | collective-permute-start | bytes 7864328 | tf_op jit(solution)/shard_map/ppermute | solution.py:568
  153.5 54.8 %collective-permute-start.3 = (bf16[1024,640]{1,0:T(8,128)(2,1)}, bf16[1024,640]{1,0:T(8,128)(2,1)S(1)}, u32[]{:S(2)}, u32[]{:S(2)}) collective-permute-start(bf16[1024,640]{1,0:T(8,128)(2,1)} %get-tuple-element.64), channel_id=1, source_target_pairs={{0,2},{2,0},{4,6},{6,4},{8,10},{10,8},{12,14},{14,12},{16,18},{18,... | collective-permute-start | bytes 3932168 | tf_op jit(solution)/shard_map/ppermute | solution.py:97
  165.1 44.9 %collective-permute-start.4 = (bf16[1024,640]{1,0:T(8,128)(2,1)}, bf16[1024,640]{1,0:T(8,128)(2,1)}, u32[]{:S(2)}, u32[]{:S(2)}) collective-permute-start(bf16[1024,640]{1,0:T(8,128)(2,1)} %get-tuple-element.65), channel_id=1, source_target_pairs={{0,2},{2,0},{4,6},{6,4},{8,10},{10,8},{12,14},{14,12},{16,18},{18,... | collective-permute-start | bytes 3932168 | tf_op jit(solution)/shard_map/ppermute | solution.py:97
  165.2 44.1 %collective-permute-start.5 = (bf16[64,3072]{1,0:T(8,128)(2,1)S(1)}, bf16[64,3072]{1,0:T(8,128)(2,1)S(1)}, u32[]{:S(2)}, u32[]{:S(2)}) collective-permute-start(bf16[64,3072]{1,0:T(8,128)(2,1)S(1)} %slice.169), channel_id=1, source_target_pairs={{2,0},{4,2},{6,4},{8,6},{10,8},{12,10},{14,12},{16,14},{18,16},{20... | collective-permute-start | bytes 1179656 | tf_op jit(solution)/shard_map/ppermute | solution.py:576
  166.5 43.6 %collective-permute-start.2 = (bf16[640,1024]{1,0:T(8,128)(2,1)}, bf16[640,1024]{1,0:T(8,128)(2,1)}, u32[]{:S(2)}, u32[]{:S(2)}) collective-permute-start(bf16[640,1024]{1,0:T(8,128)(2,1)} %shard_map.204.refs_0_), channel_id=1, source_target_pairs={{0,2},{2,0},{4,6},{6,4},{8,10},{10,8},{12,14},{14,12},{16,18},{18,... | collective-permute-start | bytes 3932168 | tf_op jit(solution)/shard_map/ppermute | solution.py:97
  249.2 16.1 %collective-permute-start.7 = (bf16[640,3072]{1,0:T(8,128)(2,1)}, bf16[640,3072]{1,0:T(8,128)(2,1)}, u32[]{:S(2)}, u32[]{:S(2)}) collective-permute-start(bf16[640,3072]{1,0:T(8,128)(2,1)} %get-tuple-element.70.refs_0_), channel_id=1, source_target_pairs={{0,2},{2,0},{4,6},{6,4},{8,10},{10,8},{12,14},{14,12},{16,18},{18,... | collective-permute-start | bytes 11796488 | tf_op jit(solution)/shard_map/ppermute | solution.py:97
  253.9 21.3 %collective-permute-start.8 = (bf16[640,1536]{1,0:T(8,128)(2,1)}, bf16[640,1536]{1,0:T(8,128)(2,1)}, u32[]{:S(2)}, u32[]{:S(2)}) collective-permute-start(bf16[640,1536]{1,0:T(8,128)(2,1)} %get-tuple-element.72.refs_0_), channel_id=1, source_target_pairs={{0,2},{2,0},{4,6},{6,4},{8,10},{10,8},{12,14},{14,12},{16,18},{18,... | collective-permute-start | bytes 5898248 | tf_op jit(solution)/shard_map/ppermute | solution.py:97
  258.0 7.2 %collective-permute-start.6 = (bf16[1024,640]{1,0:T(8,128)(2,1)}, bf16[1024,640]{1,0:T(8,128)(2,1)S(1)}, u32[]{:S(2)}, u32[]{:S(2)}) collective-permute-start(bf16[1024,640]{1,0:T(8,128)(2,1)} %get-tuple-element.69), channel_id=1, source_target_pairs={{0,2},{2,0},{4,6},{6,4},{8,10},{10,8},{12,14},{14,12},{16,18},{18,... | collective-permute-start | bytes 3932168 | tf_op jit(solution)/shard_map/ppermute | solution.py:97
  283.9 169.3 %reduce-scatter.10.cloned.1.call-start = ((), (), s32[]{:S(2)}) async-start(), calls=%async_computation.11 | async-start | bytes 1966080 | tf_op jit(solution)/shard_map/reduce_scatter | solution.py:107
  284.0 57.6 %collective-permute-start.9 = (bf16[512,1536]{1,0:T(8,128)(2,1)}, bf16[512,1536]{1,0:T(8,128)(2,1)}, u32[]{:S(2)}, u32[]{:S(2)}) collective-permute-start(bf16[512,1536]{1,0:T(8,128)(2,1)} %get-tuple-element.74.refs_3_), channel_id=1, source_target_pairs={{0,4},{2,6},{4,0},{6,2},{8,12},{10,14},{12,8},{14,10},{16,20},{18,... | collective-permute-start | bytes 4718600 | tf_op jit(solution)/shard_map/ppermute | solution.py:101
  344.5 154.2 %reduce-scatter.16.cloned.1.call-start = ((), (), s32[]{:S(2)}) async-start(), calls=%async_computation.14 | async-start | bytes 1966080 | tf_op jit(solution)/shard_map/reduce_scatter | solution.py:107
  344.8 52.6 %collective-permute-start.12 = (bf16[384,2560]{1,0:T(8,128)(2,1)}, bf16[384,2560]{1,0:T(8,128)(2,1)}, u32[]{:S(2)}, u32[]{:S(2)}) collective-permute-start(bf16[384,2560]{1,0:T(8,128)(2,1)} %get-tuple-element.78.refs_0_), channel_id=1, source_target_pairs={{0,2},{2,0},{4,6},{6,4},{8,10},{10,8},{12,14},{14,12},{16,18},{18,... | collective-permute-start | bytes 5898248 | tf_op jit(solution)/shard_map/ppermute | solution.py:97
  345.1 38.1 %collective-permute-start.10 = (bf16[384,2048]{1,0:T(8,128)(2,1)}, bf16[384,2048]{1,0:T(8,128)(2,1)}, u32[]{:S(2)}, u32[]{:S(2)}) collective-permute-start(bf16[384,2048]{1,0:T(8,128)(2,1)} %get-tuple-element.80.own_ref), channel_id=1, source_target_pairs={{0,1},{1,0},{2,3},{3,2},{4,5},{5,4},{6,7},{7,6},{8,9},{9,8},{10,11... | collective-permute-start | bytes 4718600 | tf_op jit(solution)/shard_map/ppermute | solution.py:568
  363.9 35.0 %collective-permute-start.13 = (bf16[256,2560]{1,0:T(8,128)(2,1)}, bf16[256,2560]{1,0:T(8,128)(2,1)}, u32[]{:S(2)}, u32[]{:S(2)}) collective-permute-start(bf16[256,2560]{1,0:T(8,128)(2,1)} %get-tuple-element.81.refs_0_.refs_1_), channel_id=1, source_target_pairs={{0,2},{2,0},{4,6},{6,4},{8,10},{10,8},{12,14},{14,12},{16,18},{18,... | collective-permute-start | bytes 3932168 | tf_op jit(solution)/shard_map/ppermute | solution.py:97
  364.0 55.4 %collective-permute-start.16 = (bf16[512,1536]{1,0:T(8,128)(2,1)}, bf16[512,1536]{1,0:T(8,128)(2,1)}, u32[]{:S(2)}, u32[]{:S(2)}) collective-permute-start(bf16[512,1536]{1,0:T(8,128)(2,1)} %get-tuple-element.76.refs_3_), channel_id=1, source_target_pairs={{0,4},{2,6},{4,0},{6,2},{8,12},{10,14},{12,8},{14,10},{16,20},{18,... | collective-permute-start | bytes 4718600 | tf_op jit(solution)/shard_map/ppermute | solution.py:101
  364.1 47.5 %collective-permute-start.11 = (bf16[256,2048]{1,0:T(8,128)(2,1)}, bf16[256,2048]{1,0:T(8,128)(2,1)}, u32[]{:S(2)}, u32[]{:S(2)}) collective-permute-start(bf16[256,2048]{1,0:T(8,128)(2,1)} %get-tuple-element.83.own_ref), channel_id=1, source_target_pairs={{0,1},{1,0},{2,3},{3,2},{4,5},{5,4},{6,7},{7,6},{8,9},{9,8},{10,11... | collective-permute-start | bytes 3145736 | tf_op jit(solution)/shard_map/ppermute | solution.py:568
  383.2 26.4 %collective-permute-start.15 = (bf16[128,1536]{1,0:T(8,128)(2,1)S(1)}, bf16[128,1536]{1,0:T(8,128)(2,1)}, u32[]{:S(2)}, u32[]{:S(2)}) collective-permute-start(bf16[128,1536]{1,0:T(8,128)(2,1)S(1)} %slice.171), channel_id=1, source_target_pairs={{0,4},{2,6},{4,0},{6,2},{8,12},{10,14},{12,8},{14,10},{16,20},{18,... | collective-permute-start | bytes 1179656 | tf_op jit(solution)/shard_map/ppermute | solution.py:101
  397.4 14.2 %collective-permute-start.14 = (bf16[64,1024]{1,0:T(8,128)(2,1)S(1)}, bf16[64,1024]{1,0:T(8,128)(2,1)S(1)}, u32[]{:S(2)}, u32[]{:S(2)}) collective-permute-start(bf16[64,1024]{1,0:T(8,128)(2,1)S(1)} %slice.136), channel_id=1, source_target_pairs={{2,0},{4,2},{6,4},{8,6},{10,8},{12,10},{14,12},{16,14},{18,16},{20... | collective-permute-start | bytes 393224 | tf_op jit(solution)/shard_map/ppermute | solution.py:613
  422.4 99.7 %reduce-scatter.12.cloned.1.call-start = ((), (), s32[]{:S(2)}) async-start(), calls=%async_computation.12 | async-start | bytes 1638400 | tf_op jit(solution)/shard_map/reduce_scatter | solution.py:107
  422.4 30.8 %collective-permute-start.18 = (bf16[512,1280]{1,0:T(8,128)(2,1)}, bf16[512,1280]{1,0:T(8,128)(2,1)}, u32[]{:S(2)}, u32[]{:S(2)}) collective-permute-start(bf16[512,1280]{1,0:T(8,128)(2,1)} %get-tuple-element.85.refs_1_), channel_id=1, source_target_pairs={{0,4},{2,6},{4,0},{6,2},{8,12},{10,14},{12,8},{14,10},{16,20},{18,... | collective-permute-start | bytes 3932168 | tf_op jit(solution)/shard_map/ppermute | solution.py:101
  456.0 96.7 %reduce-scatter.14.cloned.1.call-start = ((), (), s32[]{:S(2)}) async-start(), calls=%async_computation.13 | async-start | bytes 1638400 | tf_op jit(solution)/shard_map/reduce_scatter | solution.py:107
  456.0 29.9 %collective-permute-start.19 = (bf16[512,1280]{1,0:T(8,128)(2,1)}, bf16[512,1280]{1,0:T(8,128)(2,1)S(1)}, u32[]{:S(2)}, u32[]{:S(2)}) collective-permute-start(bf16[512,1280]{1,0:T(8,128)(2,1)} %get-tuple-element.89.refs_3_), channel_id=1, source_target_pairs={{0,4},{2,6},{4,0},{6,2},{8,12},{10,14},{12,8},{14,10},{16,20},{18,... | collective-permute-start | bytes 3932168 | tf_op jit(solution)/shard_map/ppermute | solution.py:101
  457.8 4.8 collective-permute-start.20
  457.8 5.0 collective-permute-start.21
  458.4 40.4 %collective-permute-start.22 = (bf16[640,2048]{1,0:T(8,128)(2,1)}, bf16[640,2048]{1,0:T(8,128)(2,1)}, u32[]{:S(2)}, u32[]{:S(2)}) collective-permute-start(bf16[640,2048]{1,0:T(8,128)(2,1)} %get-tuple-element.100.refs_0_.refs_1_), channel_id=1, source_target_pairs={{0,2},{2,0},{4,6},{6,4},{8,10},{10,8},{12,14},{14,12},{16,18},{18,... | collective-permute-start | bytes 7864328 | tf_op jit(solution)/shard_map/ppermute | solution.py:97
  462.1 66.6 %collective-permute-start.17 = (bf16[640,2048]{1,0:T(8,128)(2,1)}, bf16[640,2048]{1,0:T(8,128)(2,1)}, u32[]{:S(2)}, u32[]{:S(2)}) collective-permute-start(bf16[640,2048]{1,0:T(8,128)(2,1)} %constant_dynamic-update-slice_fusion), channel_id=1, source_target_pairs={{0,1},{1,0},{2,3},{3,2},{4,5},{5,4},{6,7},{7,6},{8,9},{9,8},{10,11... | collective-permute-start | bytes 7864328 | tf_op jit(solution)/shard_map/ppermute | solution.py:568
  462.6 29.2 %collective-permute-start.23 = (bf16[640,1024]{1,0:T(8,128)(2,1)}, bf16[640,1024]{1,0:T(8,128)(2,1)}, u32[]{:S(2)}, u32[]{:S(2)}) collective-permute-start(bf16[640,1024]{1,0:T(8,128)(2,1)} %get-tuple-element.94.refs_0_), channel_id=1, source_target_pairs={{0,2},{2,0},{4,6},{6,4},{8,10},{10,8},{12,14},{14,12},{16,18},{18,... | collective-permute-start | bytes 3932168 | tf_op jit(solution)/shard_map/ppermute | solution.py:97
  489.7 151.5 %reduce-scatter.18.cloned.1.call-start = ((), (), s32[]{:S(2)}) async-start(), calls=%async_computation.15 | async-start | bytes 2949120 | tf_op jit(solution)/shard_map/reduce_scatter | solution.py:107
  490.0 32.1 %collective-permute-start.27 = (bf16[1024,640]{1,0:T(8,128)(2,1)}, bf16[1024,640]{1,0:T(8,128)(2,1)}, u32[]{:S(2)}, u32[]{:S(2)}) collective-permute-start(bf16[1024,640]{1,0:T(8,128)(2,1)} %get-tuple-element.105), channel_id=1, source_target_pairs={{0,2},{2,0},{4,6},{6,4},{8,10},{10,8},{12,14},{14,12},{16,18},{18,... | collective-permute-start | bytes 3932168 | tf_op jit(solution)/shard_map/ppermute | solution.py:97
  490.1 38.7 %collective-permute-start.26 = (bf16[512,1280]{1,0:T(8,128)(2,1)}, bf16[512,1280]{1,0:T(8,128)(2,1)}, u32[]{:S(2)}, u32[]{:S(2)}) collective-permute-start(bf16[512,1280]{1,0:T(8,128)(2,1)} %get-tuple-element.98.refs_1_), channel_id=1, source_target_pairs={{0,4},{2,6},{4,0},{6,2},{8,12},{10,14},{12,8},{14,10},{16,20},{18,... | collective-permute-start | bytes 3932168 | tf_op jit(solution)/shard_map/ppermute | solution.py:101
  498.4 45.6 %collective-permute-start.25 = (bf16[512,1024]{1,0:T(8,128)(2,1)}, bf16[512,1024]{1,0:T(8,128)(2,1)}, u32[]{:S(2)}, u32[]{:S(2)}) collective-permute-start(bf16[512,1024]{1,0:T(8,128)(2,1)} %get-tuple-element.102.refs_3_), channel_id=1, source_target_pairs={{0,4},{2,6},{4,0},{6,2},{8,12},{10,14},{12,8},{14,10},{16,20},{18,... | collective-permute-start | bytes 3145736 | tf_op jit(solution)/shard_map/ppermute | solution.py:101
  549.7 118.2 %reduce-scatter.20.cloned.1.call-start = ((), (), s32[]{:S(2)}) async-start(), calls=%async_computation.16 | async-start | bytes 2621440 | tf_op jit(solution)/shard_map/reduce_scatter | solution.py:107
  549.7 48.9 %collective-permute-start.24 = (bf16[512,2048]{1,0:T(8,128)(2,1)}, bf16[512,2048]{1,0:T(8,128)(2,1)}, u32[]{:S(2)}, u32[]{:S(2)}) collective-permute-start(bf16[512,2048]{1,0:T(8,128)(2,1)} %get-tuple-element.104.refs_4_), channel_id=1, source_target_pairs={{0,4},{2,6},{4,0},{6,2},{8,12},{10,14},{12,8},{14,10},{16,20},{18,... | collective-permute-start | bytes 6291464 | tf_op jit(solution)/shard_map/ppermute | solution.py:101
  551.5 58.9 %collective-permute-start.28 = (bf16[640,2048]{1,0:T(8,128)(2,1)}, bf16[640,2048]{1,0:T(8,128)(2,1)}, u32[]{:S(2)}, u32[]{:S(2)}) collective-permute-start(bf16[640,2048]{1,0:T(8,128)(2,1)} %shard_map.228.refs_2_), channel_id=1, source_target_pairs={{0,1},{1,0},{2,3},{3,2},{4,5},{5,4},{6,7},{7,6},{8,9},{9,8},{10,11... | collective-permute-start | bytes 7864328 | tf_op jit(solution)/shard_map/ppermute | solution.py:568
  552.2 89.0 %collective-permute-start.35 = (bf16[512,1024]{1,0:T(8,128)(2,1)}, bf16[512,1024]{1,0:T(8,128)(2,1)}, u32[]{:S(2)}, u32[]{:S(2)}) collective-permute-start(bf16[512,1024]{1,0:T(8,128)(2,1)} %get-tuple-element.107.refs_1_), channel_id=1, source_target_pairs={{0,4},{2,6},{4,0},{6,2},{8,12},{10,14},{12,8},{14,10},{16,20},{18,... | collective-permute-start | bytes 3145736 | tf_op jit(solution)/shard_map/ppermute | solution.py:101
  614.2 3.7 collective-permute-start.29
  618.1 7.1 %collective-permute-start.30 = (f32[8,2,128]{2,1,0:T(2,128)S(1)}, f32[8,2,128]{2,1,0:T(2,128)S(1)}, u32[]{:S(2)}, u32[]{:S(2)}) collective-permute-start(f32[8,2,128]{2,1,0:T(2,128)S(1)} %slice.173), channel_id=1, source_target_pairs={{0,2},{2,0},{4,6},{6,4},{8,10},{10,8},{12,14},{14,12},{16,18},{18,... | collective-permute-start | bytes 24584 | tf_op jit(solution)/shard_map/ppermute | solution.py:97
  628.9 11.7 %collective-permute-start.32 = (f32[2,128]{1,0:T(2,128)S(1)}, f32[2,128]{1,0:T(2,128)S(1)}, u32[]{:S(2)}, u32[]{:S(2)}) collective-permute-start(f32[2,128]{1,0:T(2,128)S(1)} %get-tuple-element.189), channel_id=1, source_target_pairs={{0,8},{2,10},{4,12},{6,14},{8,16},{10,18},{12,20},{14,22},{16,24},... | collective-permute-start | bytes 3080 | tf_op jit(solution)/shard_map/ppermute | solution.py:159
  629.9 10.7 %collective-permute-start.33 = (f32[2,128]{1,0:T(2,128)S(1)}, f32[2,128]{1,0:T(2,128)S(1)}, u32[]{:S(2)}, u32[]{:S(2)}) collective-permute-start(f32[2,128]{1,0:T(2,128)S(1)} %get-tuple-element.191), channel_id=1, source_target_pairs={{0,16},{2,18},{4,20},{6,22},{8,24},{10,26},{12,28},{14,30},{16,0},... | collective-permute-start | bytes 3080 | tf_op jit(solution)/shard_map/ppermute | solution.py:159
  632.6 8.0 %collective-permute-start.34 = (f32[2,128]{1,0:T(2,128)S(1)}, f32[2,128]{1,0:T(2,128)S(1)}, u32[]{:S(2)}, u32[]{:S(2)}) collective-permute-start(f32[2,128]{1,0:T(2,128)S(1)} %get-tuple-element.190), channel_id=1, source_target_pairs={{0,24},{2,26},{4,28},{6,30},{8,0},{10,2},{12,4},{14,6},{16,8},{18,... | collective-permute-start | bytes 3080 | tf_op jit(solution)/shard_map/ppermute | solution.py:159
  645.5 11.3 %collective-permute-start.36 = (bf16[128,1024]{0,1:T(8,128)(2,1)S(1)}, bf16[128,1024]{0,1:T(8,128)(2,1)}, u32[]{:S(2)}, u32[]{:S(2)}) collective-permute-start(bf16[128,1024]{0,1:T(8,128)(2,1)S(1)} %bitcast.50), channel_id=1, source_target_pairs={{0,8},{2,10},{4,12},{6,14},{8,16},{10,18},{12,20},{14,22},{16,24},... | collective-permute-start | bytes 786440 | tf_op jit(solution)/shard_map/ppermute | solution.py:118
  646.7 19.2 %collective-permute-start.37 = (bf16[128,1024]{0,1:T(8,128)(2,1)}, bf16[128,1024]{0,1:T(8,128)(2,1)}, u32[]{:S(2)}, u32[]{:S(2)}) collective-permute-start(bf16[128,1024]{0,1:T(8,128)(2,1)} %bitcast.20), channel_id=1, source_target_pairs={{0,16},{2,18},{4,20},{6,22},{8,24},{10,26},{12,28},{14,30},{16,0},... | collective-permute-start | bytes 786440 | tf_op jit(solution)/shard_map/ppermute | solution.py:118
  647.7 18.1 %collective-permute-start.38 = (bf16[128,1024]{0,1:T(8,128)(2,1)}, bf16[128,1024]{0,1:T(8,128)(2,1)}, u32[]{:S(2)}, u32[]{:S(2)}) collective-permute-start(bf16[128,1024]{0,1:T(8,128)(2,1)} %bitcast.21), channel_id=1, source_target_pairs={{0,24},{2,26},{4,28},{6,30},{8,0},{10,2},{12,4},{14,6},{16,8},{18,... | collective-permute-start | bytes 786440 | tf_op jit(solution)/shard_map/ppermute | solution.py:118
  (28 other events, 99.4 us)
Sparse Core Ops, SparseCore 0:
  12.7 94.2 all-gather.3
  108.5 103.1 all-gather.7
  213.3 106.2 all-gather.5
  321.8 60.2 reduce-scatter.7
  384.3 36.7 reduce-scatter.9
  423.2 33.7 reduce-scatter.15
  459.3 30.1 reduce-scatter.11
  492.4 29.9 reduce-scatter.13
  549.8 47.1 reduce-scatter.17
  602.2 43.0 reduce-scatter.19
